TPU v7x, 32 devices: a whole 2x2x4 slice. The times are simulated.
32 devices in a mesh: dp: 4 (over y, x), seq: 2 (over core), tensor: 4 (over z).
Axes of the slice: x: 2, y: 2, z: 4, core: 2. Of those that a mesh axis runs over, the one named last changes fastest.
Arguments:
- tokens: bfloat16 [4096, 8192], P(('dp', 'seq'), 'tensor'), may hold values from -6 to 6
- out_grad: bfloat16 [4096, 8192], P(('dp', 'seq'), 'tensor'), may hold values from -6 to 6
- up_perm: int32 [2, 8, 8], replicated, may hold values from 0 to 7, each once within a row
- down_perm: int32 [2, 8, 8], replicated, may hold values from 0 to 7, each once within a row
- up_weight: bfloat16 [64, 2, 256, 256], P('tensor'), may hold values from -0.25 to 0.25
- down_weight: bfloat16 [64, 2, 256, 256], P('tensor'), may hold values from -0.1875 to 0.1875
Outputs:
- output: bfloat16 [4096, 8192], P(('dp', 'seq'), 'tensor')
- input_grad: bfloat16 [4096, 8192], P(('dp', 'seq'), 'tensor')
- grad_up: float32 [64, 2, 256, 256], P('tensor', None, ('dp', 'seq'))
- grad_down: float32 [64, 2, 256, 256], P('tensor', None, ('dp', 'seq'))
Inputs may be any that keep to these rules, and one draw needn't show every extreme that they name: `up_perm`: for each section, every run of 8 consecutive entries along the last dimension is a permutation of 0 to 7. `down_perm`: for each section, every run of 8 consecutive entries along the last dimension is a permutation of 0 to 7.
All inputs are finite; a program needn't handle non-finite values.
Results may differ from a plain program's by a relative error of at most 0.0049.
Values may be sent and summed in bfloat16 or wider, within the bound.
No kernel may reach another device: no remote copies, remote signals or barrier semaphores. Data moves between devices by JAX's collectives and lax.ppermute only.
A program may use at most 128 MiB of HBM per device.

v0:
```python
import jax
import jax.numpy as jnp
from jax import lax
from jax.sharding import PartitionSpec as P


def partner(block, axis, stride):
    count = lax.axis_size(axis)
    route = []
    for low in range(count):
        high = low | 1 << stride
        if high != low and high < count:
            route += [(low, high), (high, low)]
    return lax.ppermute(block, axis, route)


def select_blocks(blocks3, index_row):
    count = blocks3.shape[1]
    onehot = (index_row[:, None] == jnp.arange(count, dtype=jnp.int32)[None, :]).astype(
        jnp.bfloat16
    )
    picked = jnp.einsum("tfb,hf->thb", blocks3, onehot, preferred_element_type=jnp.float32)
    return picked.astype(jnp.bfloat16)


def spread_blocks(terms, index_row, count):
    onehot = (index_row[:, None] == jnp.arange(count, dtype=jnp.int32)[None, :]).astype(jnp.float32)
    placed = jnp.einsum("thc,hf->tfc", terms, onehot, precision=lax.Precision.HIGHEST)
    return placed.reshape(terms.shape[0], count * terms.shape[2])


def on_device(tokens, out_grad, up_perm, down_perm, up_weight, down_weight):
    tok_rows, width_local = tokens.shape
    hid_local = up_weight.shape[0]
    block_size = up_weight.shape[2]
    blocks_local = width_local // block_size
    groups = lax.axis_size("tensor")
    my_group = lax.axis_index("tensor")
    per_group = hid_local // blocks_local
    up_local = lax.dynamic_slice_in_dim(up_perm, my_group * per_group, per_group, 1).reshape(
        2, hid_local
    )
    down_local = lax.dynamic_slice_in_dim(down_perm, my_group * per_group, per_group, 1).reshape(
        2, hid_local
    )
    partner_bit = groups.bit_length() - 2
    far_tokens, far_grad = partner((tokens, out_grad), "tensor", partner_bit)
    near_blocks = tokens.reshape(tok_rows, blocks_local, block_size)
    far_blocks = far_tokens.reshape(tok_rows, blocks_local, block_size)
    in_near = select_blocks(near_blocks, up_local[0])
    in_far = select_blocks(far_blocks, up_local[1])
    pre_act = jnp.einsum(
        "thb,hbc->thc", in_near, up_weight[:, 0], preferred_element_type=jnp.float32
    )
    pre_act = pre_act + jnp.einsum(
        "thb,hbc->thc", in_far, up_weight[:, 1], preferred_element_type=jnp.float32
    )
    hidden = jax.nn.gelu(pre_act).astype(jnp.bfloat16)
    out_near = spread_blocks(
        jnp.einsum("thb,hbc->thc", hidden, down_weight[:, 0], preferred_element_type=jnp.float32),
        down_local[0],
        blocks_local,
    )
    out_far = spread_blocks(
        jnp.einsum("thb,hbc->thc", hidden, down_weight[:, 1], preferred_element_type=jnp.float32),
        down_local[1],
        blocks_local,
    )
    output = (out_near + partner(out_far, "tensor", partner_bit)).astype(jnp.bfloat16)
    grad_near_blocks = out_grad.reshape(tok_rows, blocks_local, block_size)
    grad_far_blocks = far_grad.reshape(tok_rows, blocks_local, block_size)
    gsel_near = select_blocks(grad_near_blocks, down_local[0])
    gsel_far = select_blocks(grad_far_blocks, down_local[1])
    d_hidden = jnp.einsum(
        "thc,hbc->thb", gsel_near, down_weight[:, 0], preferred_element_type=jnp.float32
    )
    d_hidden = d_hidden + jnp.einsum(
        "thc,hbc->thb", gsel_far, down_weight[:, 1], preferred_element_type=jnp.float32
    )
    _, pull_back = jax.vjp(jax.nn.gelu, pre_act)
    d_pre = pull_back(d_hidden)[0].astype(jnp.bfloat16)
    grad_scale = float(tok_rows * lax.axis_size("dp") * lax.axis_size("seq")) ** (-0.5)
    grad_down = (
        jnp.stack(
            [
                jnp.einsum("thb,thc->hbc", hidden, gsel_near, preferred_element_type=jnp.float32),
                jnp.einsum("thb,thc->hbc", hidden, gsel_far, preferred_element_type=jnp.float32),
            ],
            axis=1,
        )
        * grad_scale
    )
    grad_up = (
        jnp.stack(
            [
                jnp.einsum("thb,thc->hbc", in_near, d_pre, preferred_element_type=jnp.float32),
                jnp.einsum("thb,thc->hbc", in_far, d_pre, preferred_element_type=jnp.float32),
            ],
            axis=1,
        )
        * grad_scale
    )
    back_near = spread_blocks(
        jnp.einsum("thc,hbc->thb", d_pre, up_weight[:, 0], preferred_element_type=jnp.float32),
        up_local[0],
        blocks_local,
    )
    back_far = spread_blocks(
        jnp.einsum("thc,hbc->thb", d_pre, up_weight[:, 1], preferred_element_type=jnp.float32),
        up_local[1],
        blocks_local,
    )
    input_grad = (back_near + partner(back_far, "tensor", partner_bit)).astype(jnp.bfloat16)
    grad_up_part, grad_down_part = (
        lax.psum_scatter(grad_up, ("dp", "seq"), scatter_dimension=2, tiled=True),
        lax.psum_scatter(grad_down, ("dp", "seq"), scatter_dimension=2, tiled=True),
    )
    return (output, input_grad, grad_up_part, grad_down_part)


def solution(mesh):
    in_specs = (
        P(("dp", "seq"), "tensor"),
        P(("dp", "seq"), "tensor"),
        P(),
        P(),
        P("tensor", None, None, None),
        P("tensor", None, None, None),
    )
    out_specs = (
        P(("dp", "seq"), "tensor"),
        P(("dp", "seq"), "tensor"),
        P("tensor", None, ("dp", "seq"), None),
        P("tensor", None, ("dp", "seq"), None),
    )
    return jax.shard_map(
        on_device, mesh=mesh, in_specs=in_specs, out_specs=out_specs, check_vma=False
    )
```

profile of v0, /device:TPU:8, one launch (start us, length us, event | category | flops | bytes accessed | tf_op | source)
XLA Modules:
  0.0 650.3 jit_solution(13192053446722903053)
XLA Ops:
  7.2 2.7 collective-permute-start
  9.9 0.3 collective-permute-start.2
  10.2 0.7 constant_dynamic-slice_fusion.2
  11.3 2.4 copy.40
  13.7 0.7 copy.36
  14.4 2.9 convert_bitcast_fusion.3
  17.3 7.5 %copy.18 = bf16[512,16,256]{0,2,1:T(8,128)(2,1)} copy(bf16[512,16,256]{2,1,0:T(8,128)(2,1)} %convert_bitcast_fusion.3) | data formatting | bytes 8388608 | tf_op jit(solution)/shard_map/convert_element_type | solution.py:23
  24.8 2.9 convert_bitcast_fusion.1
  27.7 117.2 %collective-permute-done = bf16[512,2048]{1,0:T(8,128)(2,1)} collective-permute-done((bf16[512,2048]{1,0:T(8,128)(2,1)}, bf16[512,2048]{1,0:T(8,128)(2,1)}, u32[]{:S(2)}, u32[]{:S(2)}) %collective-permute-start) | collective-permute-done | bytes 2097184 | tf_op jit(solution)/shard_map/ppermute | solution.py:14
  144.9 2.3 copy.37
  147.2 2.9 convert_bitcast_fusion.2
  150.1 7.5 %copy.19 = bf16[512,16,256]{0,2,1:T(8,128)(2,1)} copy(bf16[512,16,256]{2,1,0:T(8,128)(2,1)} %convert_bitcast_fusion.2) | data formatting | bytes 8388608 | tf_op jit(solution)/shard_map/convert_element_type | solution.py:23
  157.6 32.2 %collective-permute-done.2 = bf16[512,2048]{1,0:T(8,128)(2,1)} collective-permute-done((bf16[512,2048]{1,0:T(8,128)(2,1)}, bf16[512,2048]{1,0:T(8,128)(2,1)}, u32[]{:S(2)}, u32[]{:S(2)}) %collective-permute-start.2) | collective-permute-done | bytes 2097184 | tf_op jit(solution)/shard_map/ppermute | solution.py:14
  189.8 2.4 copy.41
  192.2 1.5 convert_bitcast_fusion
  193.8 0.7 copy-done.4
  194.5 4.9 fusion.47
  199.5 0.2 copy-done.7
  199.7 9.2 %fusion.18 = (bf16[512,16,256]{2,0,1:T(8,128)(2,1)S(1)}, f32[16,512,256]{2,1,0:T(8,128)}) fusion(f32[16,512,256]{2,1,0:T(8,128)} %fusion.47, bf16[512,16,256]{0,2,1:T(8,128)(2,1)S(1)} %copy-done.7, bf16[16,2,256,256]{3,2,1,0:T(8,128)(2,1)} %param.10), kind=kOutput, calls=%fused_computation.25 | convolution fusion | flops 1094713344 | bytes 27262976 | tf_op jit(solution)/shard_map/thb,hbc->thc/dot_general | solution.py:52
  208.8 6.8 %fusion.33 = f32[16,1,256,256]{3,2,0,1:T(8,128)S(1)} fusion(bf16[512,16,256]{2,0,1:T(8,128)(2,1)S(1)} %get-tuple-element.12, bf16[512,16,256]{2,1,0:T(8,128)(2,1)} %convert_bitcast_fusion.1), kind=kOutput, calls=%fused_computation.44 | convolution fusion | flops 1073741824 | bytes 12582912 | tf_op jit(solution)/shard_map/thb,thc->hbc/dot_general | solution.py:86
  215.7 3.2 fusion.36
  218.9 3.9 maximum_multiply_fusion.1
  222.9 7.7 %fusion.25 = f32[16,512,256]{2,1,0:T(8,128)} fusion(bf16[512,16,256]{2,1,0:T(8,128)(2,1)} %copy-done.6, bf16[16,2,256,256]{3,2,1,0:T(8,128)(2,1)} %param.11), kind=kOutput, calls=%fused_computation.38 | convolution fusion | flops 1073741824 | bytes 14680064 | tf_op jit(solution)/shard_map/thc,hbc->thb/dot_general | solution.py:77
  230.6 18.0 %fusion.6 = bf16[512,16,256]{2,0,1:T(8,128)(2,1)S(1)} fusion(f32[16,512,256]{2,1,0:T(8,128)} %fusion.25, f32[16,512,256]{2,1,0:T(8,128)} %get-tuple-element.13, f32[16,512,256]{2,1,0:T(8,128)} %fusion.47, bf16[512,16,256]{2,1,0:T(8,128)(2,1)} %convert_bitcast_fusion.1, bf16[16,2,256,256]{3,2,1,0:T(8,128)(2,1)} %param.11), kind=kOutput, calls=%fused_computation.8 | convolution fusion | flops 1119879168 | bytes 35651584 | tf_op jit(solution)/shard_map/thc,hbc->thb/dot_general | solution.py:74
  248.7 1.3 convolution_bitcast_fusion
  250.0 0.9 copy-done
  250.9 1.6 copy-done.8
  252.5 1.3 convolution_bitcast_fusion.1
  253.7 3.9 maximum_multiply_fusion
  257.7 4.4 fusion.45
  262.1 7.9 %fusion.7 = f32[8,512,256]{2,0,1:T(8,128)S(1)} fusion(f32[16,512,256]{2,1,0:T(8,128)S(1)} %fusion.45, s32[16]{0:T(128)S(1)} %eq.40), kind=kOutput, calls=%fused_computation.11 | convolution fusion | flops 201326720 | bytes 12582976 | tf_op jit(solution)/shard_map/thc,hf->tfc/dot_general | solution.py:28
  270.1 4.2 copy.43
  274.3 3.4 collective-permute-start.3
  277.6 1.3 fusion.40
  278.9 7.9 %fusion.14 = f32[8,512,256]{2,0,1:T(8,128)S(1)} fusion(f32[16,512,256]{2,1,0:T(8,128)S(1)} %fusion.40, s32[16]{0:T(128)S(1)} %eq.44), kind=kOutput, calls=%fused_computation.20 | convolution fusion | flops 201326720 | bytes 12582976 | tf_op jit(solution)/shard_map/thc,hf->tfc/dot_general | solution.py:28
  286.8 4.4 copy.39
  291.3 1.3 fusion.49
  292.6 7.9 %fusion.9 = f32[8,512,256]{2,0,1:T(8,128)S(1)} fusion(f32[16,512,256]{2,1,0:T(8,128)S(1)} %fusion.49, s32[16]{0:T(128)S(1)} %eq.36), kind=kOutput, calls=%fused_computation.13 | convolution fusion | flops 201326720 | bytes 12582976 | tf_op jit(solution)/shard_map/thc,hf->tfc/dot_general | solution.py:28
  300.5 2.1 copy.42
  302.6 1.3 fusion.43
  303.9 7.9 %fusion.16 = f32[8,512,256]{2,0,1:T(8,128)S(1)} fusion(f32[16,512,256]{2,1,0:T(8,128)S(1)} %fusion.43, s32[16]{0:T(128)S(1)} %eq.32), kind=kOutput, calls=%fused_computation.22 | convolution fusion | flops 201326720 | bytes 12582976 | tf_op jit(solution)/shard_map/thc,hf->tfc/dot_general | solution.py:28
  311.8 2.0 copy.38
  313.8 230.9 %collective-permute-done.3 = f32[512,2048]{1,0:T(8,128)} collective-permute-done((f32[512,2048]{1,0:T(8,128)}, f32[512,2048]{1,0:T(8,128)}, u32[]{:S(2)}, u32[]{:S(2)}) %collective-permute-start.3) | collective-permute-done | bytes 4194336 | tf_op jit(solution)/shard_map/ppermute | solution.py:14
  544.7 4.1 add_convert_fusion
  548.8 85.7 %collective-permute-done.1 = f32[512,2048]{1,0:T(8,128)} collective-permute-done((f32[512,2048]{1,0:T(8,128)}, f32[512,2048]{1,0:T(8,128)}, u32[]{:S(2)}, u32[]{:S(2)}) %collective-permute-start.1) | collective-permute-done | bytes 4194336 | tf_op jit(solution)/shard_map/ppermute | solution.py:14
  634.5 4.1 add_convert_fusion.1
  638.6 2.3 copy.25
  640.9 2.3 copy.24
  (33 shorter events, 0.5 us)
Async XLA Ops:
  7.2 631.4 %reduce-scatter.5.cloned.1.call-start = ((), (), s32[]{:S(2)}) async-start(), calls=%async_computation.3 | async-start | bytes 9437184 | tf_op jit(solution)/shard_map/reduce_scatter | solution.py:116
  7.2 137.7 %collective-permute-start = (bf16[512,2048]{1,0:T(8,128)(2,1)}, bf16[512,2048]{1,0:T(8,128)(2,1)}, u32[]{:S(2)}, u32[]{:S(2)}) collective-permute-start(bf16[512,2048]{1,0:T(8,128)(2,1)} %param.6), channel_id=1, source_target_pairs={{0,2},{2,0},{1,3},{3,1},{4,6},{6,4},{5,7},{7,5},{8,10},{10,8},{9,1... | collective-permute-start | bytes 6291464 | tf_op jit(solution)/shard_map/ppermute | solution.py:14
  9.9 179.9 %collective-permute-start.2 = (bf16[512,2048]{1,0:T(8,128)(2,1)}, bf16[512,2048]{1,0:T(8,128)(2,1)}, u32[]{:S(2)}, u32[]{:S(2)}) collective-permute-start(bf16[512,2048]{1,0:T(8,128)(2,1)} %param.7), channel_id=1, source_target_pairs={{0,2},{2,0},{1,3},{3,1},{4,6},{6,4},{5,7},{7,5},{8,10},{10,8},{9,1... | collective-permute-start | bytes 6291464 | tf_op jit(solution)/shard_map/ppermute | solution.py:14
  11.3 2.4 copy-start.12
  189.8 4.0 copy-start.9
  192.2 2.3 copy-start.4
  194.5 21.2 %copy-start.6 = (bf16[512,16,256]{2,1,0:T(8,128)(2,1)}, bf16[512,16,256]{2,1,0:T(8,128)(2,1)S(1)}, u32[]{:S(2)}) copy-start(bf16[512,16,256]{2,1,0:T(8,128)(2,1)S(1)} %convert_bitcast_fusion) | copy-start | bytes 12582916
  194.5 5.2 copy-start.7
  208.8 6.9 %copy-start.2 = (bf16[512,16,256]{2,0,1:T(8,128)(2,1)}, bf16[512,16,256]{2,0,1:T(8,128)(2,1)S(1)}, u32[]{:S(2)}) copy-start(bf16[512,16,256]{2,0,1:T(8,128)(2,1)S(1)} %get-tuple-element.12) | copy-start | bytes 12582916
  222.8 418.1 %reduce-scatter.3.cloned.1.call-start = ((), (), s32[]{:S(2)}) async-start(), calls=%async_computation.2 | async-start | bytes 9437184 | tf_op jit(solution)/shard_map/reduce_scatter | solution.py:115
  230.6 18.0 %copy-start.5 = (bf16[512,16,256]{0,2,1:T(8,128)(2,1)S(1)}, bf16[512,16,256]{0,2,1:T(8,128)(2,1)}, u32[]{:S(2)}) copy-start(bf16[512,16,256]{0,2,1:T(8,128)(2,1)} %copy.19) | copy-start | bytes 12582916
  248.7 2.2 copy-start
  248.7 3.8 copy-start.8
  270.0 7.6 %copy-start.3 = (bf16[512,16,256]{2,0,1:T(8,128)(2,1)S(1)}, bf16[512,16,256]{2,0,1:T(8,128)(2,1)}, u32[]{:S(2)}) copy-start(bf16[512,16,256]{2,0,1:T(8,128)(2,1)} %copy-done.2) | copy-start | bytes 12582916
  270.0 7.6 %copy-start.11 = (bf16[16,2,256,256]{3,2,1,0:T(8,128)(2,1)S(1)}, bf16[16,2,256,256]{3,2,1,0:T(8,128)(2,1)}, u32[]{:S(2)}) copy-start(bf16[16,2,256,256]{3,2,1,0:T(8,128)(2,1)} %param.11) | copy-start | bytes 12582916
  274.3 270.5 %collective-permute-start.3 = (f32[512,2048]{1,0:T(8,128)}, f32[512,2048]{1,0:T(8,128)}, u32[]{:S(2)}, u32[]{:S(2)}) collective-permute-start(f32[512,2048]{1,0:T(8,128)} %bitcast.49), channel_id=1, source_target_pairs={{0,2},{2,0},{1,3},{3,1},{4,6},{6,4},{5,7},{7,5},{8,10},{10,8},{9,1... | collective-permute-start | bytes 12582920 | tf_op jit(solution)/shard_map/ppermute | solution.py:14
  286.8 4.4 copy-start.1
  286.8 4.4 copy-start.10
  291.2 343.3 %collective-permute-start.1 = (f32[512,2048]{1,0:T(8,128)}, f32[512,2048]{1,0:T(8,128)}, u32[]{:S(2)}, u32[]{:S(2)}) collective-permute-start(f32[512,2048]{1,0:T(8,128)} %bitcast.41), channel_id=1, source_target_pairs={{0,2},{2,0},{1,3},{3,1},{4,6},{6,4},{5,7},{7,5},{8,10},{10,8},{9,1... | collective-permute-start | bytes 12582920 | tf_op jit(solution)/shard_map/ppermute | solution.py:14
Sparse Core Ops, SparseCore 0:
  223.0 73.2 reduce-scatter.4
  300.1 71.2 reduce-scatter.2
where the time goes:
time: 663 us; the launch traced here: 650 us
  waiting for transfers between devices  466 us (70%)
  matrix products  103 us (16%)
  local copies, waits for them, and re-layouts  44.7 us (7%)
  other arithmetic  16 us (2%)
  between operations  14.5 us (2%)
    ppermute x4, waiting for transfers between devices, partner(): return lax.ppermute(block, axis, route)  466 us
    dot_general x4, matrix products, spread_blocks(): jnp.einsum('thc,hf->tfc', terms, onehot, precision=lax.Precision.HIGHEST)  31.7 us
    unnamed x36, local copies, waits for them, and re-layouts  28.6 us
    dot_general x1, matrix products, on_device(): jnp.einsum('thc,hbc->thb', gsel_near, down_weight[:, 0], preferred_elemen...  18 us
    convert_element_type x2, local copies, waits for them, and re-layouts, select_blocks(): return picked.astype(jnp.bfloat16)  15 us
  transfers between devices with their start and end apart: 6, of which 4 were waited for; matrix products, arithmetic and copies ran while one was open for 19% of the time, Pallas kernels for 0%

commit v1 on v0

v1 whole, which is shorter than its diff:
```python
import functools
import math

import jax
import jax.numpy as jnp
from jax import lax
from jax.experimental import pallas as pl
from jax.experimental.pallas import tpu as pltpu
from jax.sharding import PartitionSpec as P

F32 = jnp.float32
BF16 = jnp.bfloat16
ROOT = math.sqrt(2.0 / math.pi)
CUBIC = 0.044715


def dot(a, b, over):
    return lax.dot_general(a, b, ((over[:1], over[1:]), ((), ())), preferred_element_type=F32)


def activate(pre, d_hidden):
    square = pre * pre
    tanh = jnp.tanh(ROOT * (pre + CUBIC * (square * pre)))
    cdf = 0.5 * (1.0 + tanh)
    slope = cdf + (0.5 * ROOT) * pre * (1.0 - tanh * tanh) * (1.0 + (3.0 * CUBIC) * square)
    return (pre * cdf).astype(BF16), (d_hidden * slope).astype(BF16)


def layer_kernel(first, rows, ids, *refs):
    refs = list(refs)
    take = lambda count: [refs.pop(0) for _ in range(count)]
    chunks = 1 if first else 2
    (x_near,), x_far = take(1), take(chunks)
    (g_near,), g_far = take(1), take(chunks)
    up, down = take(2)
    if not first:
        hidden_before, d_pre_before = take(2)
    result = take(4)
    if first:
        hidden_out, d_pre_out = take(2)
    else:
        sums = take(8)
    xs, gs, out_acc, back_acc = take(4)
    if not first:
        up_sum, down_sum = take(2)
    step = pl.program_id(0)
    steps = pl.num_programs(0)
    blocks, _, size = xs.shape
    half = blocks // 2
    low = 0 if first else rows[0]
    count = rows[0] if first else rows[1]

    @pl.when(step == 0)
    def _():
        for dst, near, far in ((xs, x_near, x_far), (gs, g_near, g_far)):
            for b in range(half):
                cols = slice(b * size, (b + 1) * size)
                dst[b] = near[:, cols]
                at = 0
                for part in far:
                    dst[half + b, at : at + part.shape[0]] = part[:, cols]
                    at += part.shape[0]
        out_acc[...] = jnp.zeros_like(out_acc)
        back_acc[...] = jnp.zeros_like(back_acc)

    in0, in1, out0, out1 = (ids[k, step] for k in range(4))
    now = pl.ds(low, count)
    x_cat = jnp.concatenate([xs[in0, now], xs[in1, now]], axis=1)
    g_cat = jnp.concatenate([gs[out0, now], gs[out1, now]], axis=1)
    up_cat = up[0].reshape(2 * size, size)
    down_cat = jnp.concatenate([down[0, 0], down[0, 1]], axis=1)
    pre = dot(x_cat, up_cat, (1, 0))
    d_hidden = dot(g_cat, down_cat, (1, 1))
    hidden, d_pre = activate(pre, d_hidden)
    out = dot(hidden, down_cat, (1, 0))
    back = dot(d_pre, up_cat, (1, 1))
    out_acc[out0] += out[:, :size]
    out_acc[out1] += out[:, size:]
    back_acc[in0] += back[:, :size]
    back_acc[in1] += back[:, size:]
    if first:
        hidden_out[0] = hidden
        d_pre_out[0] = d_pre
    else:
        before = pl.ds(0, low)
        x_before = jnp.concatenate([xs[in0, before], xs[in1, before]], axis=1)
        g_before = jnp.concatenate([gs[out0, before], gs[out1, before]], axis=1)
        up_sum[...] = dot(x_cat, d_pre, (0, 0)) + dot(x_before, d_pre_before[0], (0, 0))
        down_sum[...] = dot(hidden, g_cat, (0, 0)) + dot(hidden_before[0], g_before, (0, 0))
        me = ids[4, 0]
        shard = sums[0].shape[3]
        shards = size // shard

        def store(keep_up, send_up, keep_down, send_down):
            for place in range(shards):
                start = pl.multiple_of((place ^ me) * shard, shard)
                to_up, to_down = (send_up, send_down) if place & 1 else (keep_up, keep_down)
                for s in range(2):
                    to_up[place >> 1, 0, s] = up_sum[pl.ds(s * size + start, shard)].astype(BF16)
                    to_down[place >> 1, 0, s] = down_sum[
                        pl.ds(start, shard), s * size : (s + 1) * size
                    ].astype(BF16)

        pl.when(step < steps // 2)(lambda: store(*sums[:4]))
        pl.when(step >= steps // 2)(lambda: store(*sums[4:]))

    @pl.when(step == steps - 1)
    def _():
        for b in range(blocks):
            side, cols = divmod(b, half)
            cols = slice(cols * size, (cols + 1) * size)
            result[side][:, cols] = out_acc[b].astype(BF16)
            result[2 + side][:, cols] = back_acc[b].astype(BF16)


def layer(first, rows, shards, ids, x_near, x_far, g_near, g_far, up, down, before=()):
    steps, _, size, _ = up.shape
    width = x_near.shape[1]
    blocks = 2 * width // size
    hid = steps // 2
    all_rows = rows[0] if first else sum(rows)
    count = rows[0] if first else rows[1]

    def whole(shape):
        return pl.BlockSpec(shape, lambda i, ids: (0,) * len(shape))

    weight = pl.BlockSpec((1, 2, size, size), lambda i, ids: (i, 0, 0, 0))
    kept = pl.BlockSpec((1, rows[0], size), lambda i, ids: (i, 0, 0))
    far = [whole(part.shape) for part in x_far]
    near = whole((all_rows, width))
    in_specs = [near, *far, near, *far, weight, weight]
    out_shape = [jax.ShapeDtypeStruct((count, width), BF16)] * 4
    out_specs = [whole((count, width))] * 4
    scratch = [
        pltpu.VMEM((blocks, all_rows, size), BF16),
        pltpu.VMEM((blocks, all_rows, size), BF16),
        pltpu.VMEM((blocks, count, size), F32),
        pltpu.VMEM((blocks, count, size), F32),
    ]
    if first:
        out_shape += [jax.ShapeDtypeStruct((steps, count, size), BF16)] * 2
        out_specs += [kept] * 2
    else:
        in_specs += [kept] * 2
        shard = size // shards
        out_shape += [jax.ShapeDtypeStruct((shards // 2, hid, 2, shard, size), BF16)] * 8
        for part in range(2):
            out_specs += [
                pl.BlockSpec(
                    (shards // 2, 1, 2, shard, size),
                    lambda i, ids, part=part: (0, jnp.clip(i - part * hid, 0, hid - 1), 0, 0, 0),
                )
            ] * 4
        scratch += [pltpu.VMEM((2 * size, size), F32), pltpu.VMEM((size, 2 * size), F32)]
    flops = steps * size * size * 2 * (8 * count + (0 if first else 4 * all_rows))
    return pl.pallas_call(
        functools.partial(layer_kernel, first, rows),
        out_shape=out_shape,
        grid_spec=pltpu.PrefetchScalarGridSpec(
            num_scalar_prefetch=1,
            grid=(steps,),
            in_specs=in_specs,
            out_specs=out_specs,
            scratch_shapes=scratch,
        ),
        compiler_params=pltpu.CompilerParams(
            dimension_semantics=("arbitrary",), vmem_limit_bytes=60 << 20
        ),
        cost_estimate=pl.CostEstimate(flops=flops, bytes_accessed=40 << 20, transcendentals=0),
    )(ids, x_near, *x_far, g_near, *g_far, up, down, *before)


def hop(block, bit):
    seq = lax.axis_size("seq")
    axis, bit = ("seq", bit) if bit < seq else ("dp", bit // seq)
    return lax.ppermute(block, axis, [(i, i ^ bit) for i in range(lax.axis_size(axis))])


def plane_bits():
    seq, dp = lax.axis_size("seq"), lax.axis_size("dp")
    return (
        [1 << k for k in range(seq.bit_length() - 1)],
        [seq << k for k in range(dp.bit_length() - 1)],
    )


def gather(shard, order):
    parts = {0: shard}
    for bit in order:
        for place in list(parts):
            parts[place | bit] = hop(parts[place], bit)
    return parts


def total(terms):
    return sum(term.astype(F32) for term in terms)


def reduce_scatter(keep, send, order):
    count = keep.shape[0]
    got = hop(send, order[0])
    terms = {2 * p: [keep[p], got[p]] for p in range(count)}
    for bit in order[1:]:
        away = [p for p in terms if p & bit]
        got = hop(jnp.stack([total(terms[p]).astype(BF16) for p in away]), bit)
        for k, p in enumerate(away):
            terms[p ^ bit].append(got[k])
            del terms[p]
    return total(terms[0])


def on_device(tokens, out_grad, up_perm, down_perm, up_weight, down_weight):
    tok_rows, width = tokens.shape
    hid, _, size, _ = up_weight.shape
    groups, group = lax.axis_size("tensor"), lax.axis_index("tensor")
    blocks = width // size
    away = groups // 2
    seq_bits, dp_bits = plane_bits()
    shards = lax.axis_size("dp") * lax.axis_size("seq")
    me = lax.axis_index("dp") * lax.axis_size("seq") + lax.axis_index("seq")
    pairs = [(p, p + away) if p % 2 == 0 else (p + away, p) for p in range(away)]
    into = [(other, worker) for worker, other in pairs]
    back = pairs
    works = (group % away % 2 == 0) != (group >= away)
    partner = (group + away) % groups

    rows = (tok_rows // 2, tok_rows - tok_rows // 2)
    lines = hid * 2 * size // shards

    def weight_shard(weight):
        return lax.dynamic_slice_in_dim(weight.reshape(-1, size), me * lines, lines, 0)

    up_shard = lax.ppermute(weight_shard(up_weight), "tensor", into)
    down_shard = lax.ppermute(weight_shard(down_weight), "tensor", into)
    x_far, g_far = [], []
    for low, high in ((0, rows[0]), (rows[0], tok_rows)):
        x_far.append(lax.ppermute(tokens[low:high], "tensor", into))
        g_far.append(lax.ppermute(out_grad[low:high], "tensor", into))

    def both(weight, parts):
        table = jnp.concatenate(
            [jnp.zeros((shards, lines, size), BF16), weight.reshape(shards, lines, size)]
        )
        for place, part in parts.items():
            table = lax.dynamic_update_slice_in_dim(table, part[None], place ^ me, 0)
        return table.reshape(2 * hid, 2, size, size)

    up = both(up_weight, gather(up_shard, dp_bits + seq_bits))
    down = both(down_weight, gather(down_shard, dp_bits[::-1] + seq_bits))

    def block_ids(perm):
        flat = perm.reshape(2, -1)
        theirs = lax.dynamic_slice_in_dim(flat, partner * hid, hid, 1)
        mine = lax.dynamic_slice_in_dim(flat, group * hid, hid, 1)
        side = jnp.array([[0], [blocks]], jnp.int32)
        return jnp.concatenate([theirs + side[::-1], mine + side], axis=1)

    ids = jnp.concatenate(
        [
            block_ids(up_perm),
            block_ids(down_perm),
            jnp.full((1, 2 * hid), me, jnp.int32),
        ]
    )

    one = layer(True, rows, shards, ids, tokens, x_far[:1], out_grad, g_far[:1], up, down)
    two = layer(False, rows, shards, ids, tokens, x_far, out_grad, g_far, up, down, one[4:6])

    def deliver(near, far):
        got = [lax.ppermute(part, "tensor", back) for part in far]
        return jnp.concatenate([jnp.where(works, n, f) for n, f in zip(near, got)])

    output = deliver((one[0], two[0]), (one[1], two[1]))
    input_grad = deliver((one[2], two[2]), (one[3], two[3]))

    orders = (seq_bits + dp_bits, seq_bits + dp_bits[::-1])
    sums = two[4:]
    theirs = [
        lax.ppermute(
            reduce_scatter(sums[2 * k], sums[2 * k + 1], orders[k]).astype(BF16), "tensor", back
        )
        for k in range(2)
    ]
    mine = [reduce_scatter(sums[4 + 2 * k], sums[5 + 2 * k], orders[k]) for k in range(2)]
    scale = float(tok_rows * shards) ** (-0.5)
    grads = [jnp.where(works, m, t.astype(F32)) * scale for m, t in zip(mine, theirs)]
    return output, input_grad, grads[0], grads[1]


def solution(mesh):
    in_specs = (
        P(("dp", "seq"), "tensor"),
        P(("dp", "seq"), "tensor"),
        P(),
        P(),
        P("tensor", None, None, None),
        P("tensor", None, None, None),
    )
    out_specs = (
        P(("dp", "seq"), "tensor"),
        P(("dp", "seq"), "tensor"),
        P("tensor", None, ("dp", "seq"), None),
        P("tensor", None, ("dp", "seq"), None),
    )
    return jax.shard_map(
        on_device, mesh=mesh, in_specs=in_specs, out_specs=out_specs, check_vma=False
    )
```

time: 663 us -> 380 us (0.57); the launches traced: 650 us -> 377 us
  waiting for transfers between devices: 466 us -> 203 us
  matrix products: 103 us -> 0 us
  Pallas kernels: 0 us -> 80.5 us
  starting transfers between devices: 6.47 us -> 45.4 us
  between operations: 14.5 us -> 1.05 us
  local copies, waits for them, and re-layouts: 44.7 us -> 34.6 us
    ppermute x4 -> x38, waiting for transfers between devices: 466 us -> 203 us  [the longest x26 82 us: hop(): lax.ppermute(block, axis, [(i, i ^ bit) for i in range(lax.axis_size(axis...]
    dot_general x20 -> x0, matrix products: 103 us -> none  [the longest x4 31.7 us: spread_blocks(): jnp.einsum('thc,hf->tfc', terms, onehot, precision=lax.Precision.HIGHEST)]
    pallas_call x0 -> x2, Pallas kernels: none -> 80.5 us  [layer(): pl.pallas_call(functools.partial(layer_kernel, first, rows), out_shape=ou...]
    ppermute x4 -> x38, starting transfers between devices: 6.39 us -> 45.4 us  [the longest x26 17.4 us: hop(): lax.ppermute(block, axis, [(i, i ^ bit) for i in range(lax.axis_size(axis...]
    unnamed x36 -> x32, local copies, waits for them, and re-layouts: 28.6 us -> 1.04 us
    dynamic_update_slice x0 -> x16, local copies, waits for them, and re-layouts: none -> 15.6 us  [both(): table = lax.dynamic_update_slice_in_dim(table, part[None], place ^ me, 0)]
    convert_element_type x2 -> x0, local copies, waits for them, and re-layouts: 15 us -> none  [select_blocks(): return picked.astype(jnp.bfloat16)]
    concatenate x0 -> x3, local copies, waits for them, and re-layouts: none -> 10.2 us  [the longest x2 10.1 us: both(): jnp.concatenate([jnp.zeros((shards, lines, size), BF16), weight.reshape(s...]
  transfers between devices with their start and end apart: 6 -> 38, of which waited for: 4 -> 14; matrix products, arithmetic and copies ran while one was open for 19% -> 11% of each run, Pallas kernels for 0% -> 21%
where the time goes in v1:
time: 380 us; the launch traced here: 377 us
  waiting for transfers between devices  203 us (53%)
  Pallas kernels  80.5 us (21%)
  starting transfers between devices  45.4 us (12%)
  local copies, waits for them, and re-layouts  34.6 us (9%)
  other arithmetic  12.7 us (3%)
    ppermute x26, waiting for transfers between devices, hop(): lax.ppermute(block, axis, [(i, i ^ bit) for i in range(lax.axis_size(axis...  82 us
    pallas_call x2, Pallas kernels, layer(): pl.pallas_call(functools.partial(layer_kernel, first, rows), out_shape=ou...  80.5 us
    ppermute x4, waiting for transfers between devices, deliver(): got = [lax.ppermute(part, 'tensor', back) for part in far]  65.9 us
    ppermute x2, waiting for transfers between devices, on_device(): g_far.append(lax.ppermute(out_grad[low:high], 'tensor', into))  24.6 us
    ppermute x2, waiting for transfers between devices, on_device(): lax.ppermute(reduce_scatter(sums[2 * k], sums[2 * k + 1], orders[k]).asty...  19.7 us
    ppermute x26, starting transfers between devices, hop(): lax.ppermute(block, axis, [(i, i ^ bit) for i in range(lax.axis_size(axis...  17.4 us
    dynamic_update_slice x16, local copies, waits for them, and re-layouts, both(): table = lax.dynamic_update_slice_in_dim(table, part[None], place ^ me, 0)  15.6 us
    ppermute x1, waiting for transfers between devices, on_device(): down_shard = lax.ppermute(weight_shard(down_weight), 'tensor', into)  11.1 us
  transfers between devices with their start and end apart: 38, of which 14 were waited for; matrix products, arithmetic and copies ran while one was open for 11% of the time, Pallas kernels for 21%

profile of v1, /device:TPU:8, one launch (start us, length us, event | category | flops | bytes accessed | tf_op | source)
XLA Modules:
  0.0 377.4 jit_solution(3894930401087504178)
XLA Ops:
  0.6 2.0 constant_dynamic-slice_fusion.1
  2.7 5.3 %collective-permute-start.2 = (bf16[1024,256]{1,0:T(8,128)(2,1)}, bf16[1024,256]{1,0:T(8,128)(2,1)}, u32[]{:S(2)}, u32[]{:S(2)}) collective-permute-start(bf16[1024,256]{1,0:T(8,128)(2,1)} %constant_dynamic-slice_fusion.1), channel_id=1, source_target_pairs={{2,0},{1,3},{6,4},{5,7},{10,8},{9,11},{14,12},{13,15},{18,16},{17,... | collective-permute-start | bytes 1572872 | tf_op jit(solution)/shard_map/ppermute | solution.py:233
  8.0 1.1 constant_dynamic-slice_fusion
  9.1 2.3 collective-permute-start.10
  11.3 3.1 fusion.9
  14.4 2.2 collective-permute-start
  16.7 1.5 fusion.8
  18.1 1.3 collective-permute-start.1
  19.8 11.1 %collective-permute-done.10 = bf16[1024,256]{1,0:T(8,128)(2,1)} collective-permute-done((bf16[1024,256]{1,0:T(8,128)(2,1)S(1)}, bf16[1024,256]{1,0:T(8,128)(2,1)}, u32[]{:S(2)}, u32[]{:S(2)}) %collective-permute-start.10) | collective-permute-done | bytes 524320 | tf_op jit(solution)/shard_map/ppermute | solution.py:234
  30.9 1.5 collective-permute-start.11
  33.1 6.2 %concatenate.25 = bf16[16,1024,256]{2,1,0:T(8,128)(2,1)} pad(bf16[8,1024,256]{2,1,0:T(8,128)(2,1)} %bitcast.56, bf16[]{:T(256)} %constant.55.clone.1), padding=8_0x0_0x0_0 | pad | bytes 12582914 | tf_op jit(solution)/shard_map/concatenate | solution.py:241
  39.3 3.9 %concatenate.24 = bf16[16,1024,256]{2,1,0:T(8,128)(2,1)} pad(bf16[8,1024,256]{2,1,0:T(8,128)(2,1)S(1)} %bitcast.58, bf16[]{:T(256)} %constant.55.clone.1), padding=8_0x0_0x0_0 | pad | bytes 12582914 | tf_op jit(solution)/shard_map/concatenate | solution.py:241
  43.2 1.5 collective-permute-start.12
  45.2 1.9 bitcast_dynamic-update-slice_fusion.7
  47.1 1.9 bitcast_dynamic-update-slice_fusion.15
  50.3 16.4 %collective-permute-done.3 = bf16[1024,256]{1,0:T(8,128)(2,1)S(1)} collective-permute-done((bf16[1024,256]{1,0:T(8,128)(2,1)}, bf16[1024,256]{1,0:T(8,128)(2,1)S(1)}, u32[]{:S(2)}, u32[]{:S(2)}) %collective-permute-start.3) | collective-permute-done | bytes 524320 | tf_op jit(solution)/shard_map/ppermute | solution.py:176
  66.8 1.5 collective-permute-start.13
  71.3 6.0 %collective-permute-done.13 = bf16[1024,256]{1,0:T(8,128)(2,1)S(1)} collective-permute-done((bf16[1024,256]{1,0:T(8,128)(2,1)S(1)}, bf16[1024,256]{1,0:T(8,128)(2,1)S(1)}, u32[]{:S(2)}, u32[]{:S(2)}) %collective-permute-start.13) | collective-permute-done | bytes 524320 | tf_op jit(solution)/shard_map/ppermute | solution.py:176
  85.2 6.4 %collective-permute-start.19 = (bf16[256,2048]{1,0:T(8,128)(2,1)S(1)}, bf16[256,2048]{1,0:T(8,128)(2,1)}, u32[]{:S(2)}, u32[]{:S(2)}) collective-permute-start(bf16[256,2048]{1,0:T(8,128)(2,1)S(1)} %copy-done.9), channel_id=1, source_target_pairs={{2,0},{1,3},{6,4},{5,7},{10,8},{9,11},{14,12},{13,15},{18,16},{17,... | collective-permute-start | bytes 3145736 | tf_op jit(solution)/shard_map/ppermute | solution.py:237
  92.4 2.3 collective-permute-start.20
  96.5 1.0 copy-done.15
  97.5 34.8 %shard_map.111 = (bf16[256,2048]{1,0:T(8,128)(2,1)}, bf16[256,2048]{1,0:T(8,128)(2,1)}, bf16[256,2048]{1,0:T(8,128)(2,1)}, bf16[256,2048]{1,0:T(8,128)(2,1)}, bf...) custom-call(s32[5,32]{1,0:T(8,128)} %add_add_fusion.ids, bf16[512,2048]{1,0:T(8,128)(2,1)} %refs_0_.3, ...), custom_call_target="tpu_custom_call" | custom-call | flops 8589934592 | bytes 41943040 | tf_op jit(solution)/shard_map/pallas_call | solution.py:156
  132.3 1.3 collective-permute-start.18
  133.6 24.6 %collective-permute-done.20.refs_5_ = bf16[256,2048]{1,0:T(8,128)(2,1)} collective-permute-done((bf16[256,2048]{1,0:T(8,128)(2,1)S(1)}, bf16[256,2048]{1,0:T(8,128)(2,1)}, u32[]{:S(2)}, u32[]{:S(2)}) %collective-permute-start.20) | collective-permute-done | bytes 1048608 | tf_op jit(solution)/shard_map/ppermute | solution.py:238
  158.2 45.6 %shard_map.112 = (bf16[256,2048]{1,0:T(8,128)(2,1)}, bf16[256,2048]{1,0:T(8,128)(2,1)}, bf16[256,2048]{1,0:T(8,128)(2,1)}, bf16[256,2048]{1,0:T(8,128)(2,1)}, bf...) custom-call(s32[5,32]{1,0:T(8,128)} %add_add_fusion.ids, ...), custom_call_target="tpu_custom_call" | custom-call | flops 17179869184 | bytes 41943040 | tf_op jit(solution)/shard_map/pallas_call | solution.py:156
  203.8 1.4 collective-permute-start.21
  205.3 1.4 collective-permute-start.23
  206.7 1.5 collective-permute-start.22
  208.9 24.3 %collective-permute-done.21 = bf16[256,2048]{1,0:T(8,128)(2,1)} collective-permute-done((bf16[256,2048]{1,0:T(8,128)(2,1)}, bf16[256,2048]{1,0:T(8,128)(2,1)}, u32[]{:S(2)}, u32[]{:S(2)}) %collective-permute-start.21) | collective-permute-done | bytes 1048608 | tf_op jit(solution)/shard_map/ppermute | solution.py:270
  233.1 1.5 broadcast_select_fusion.2
  234.6 20.9 %collective-permute-done.23 = bf16[256,2048]{1,0:T(8,128)(2,1)S(1)} collective-permute-done((bf16[256,2048]{1,0:T(8,128)(2,1)}, bf16[256,2048]{1,0:T(8,128)(2,1)S(1)}, u32[]{:S(2)}, u32[]{:S(2)}) %collective-permute-start.23) | collective-permute-done | bytes 1048608 | tf_op jit(solution)/shard_map/ppermute | solution.py:270
  255.7 20.8 %collective-permute-done.22 = bf16[256,2048]{1,0:T(8,128)(2,1)S(1)} collective-permute-done((bf16[256,2048]{1,0:T(8,128)(2,1)}, bf16[256,2048]{1,0:T(8,128)(2,1)S(1)}, u32[]{:S(2)}, u32[]{:S(2)}) %collective-permute-start.22) | collective-permute-done | bytes 1048608 | tf_op jit(solution)/shard_map/ppermute | solution.py:270
  277.2 1.9 collective-permute-start.25
  282.2 1.6 collective-permute-start.32
  283.8 1.6 pad_maximum_fusion
  285.4 18.0 %collective-permute-done.25 = bf16[2,16,2,32,256]{4,3,2,1,0:T(8,128)(2,1)S(1)} collective-permute-done((bf16[2,16,2,32,256]{4,3,2,1,0:T(8,128)(2,1)S(1)}, bf16[2,16,2,32,256]{4,3,2,1,0:T(8,128)(2,1)S(1)}, u32[]{:S(2)}, u32[]{:S(2)}) %collective-permute-start.25) | collective-permute-done | bytes 1048608 | tf_op jit(solution)/shard_map/ppermute | solution.py:176
  304.2 19.8 %collective-permute-done.28 = bf16[2,16,2,32,256]{4,3,2,1,0:T(8,128)(2,1)S(1)} collective-permute-done((bf16[2,16,2,32,256]{4,3,2,1,0:T(8,128)(2,1)S(1)}, bf16[2,16,2,32,256]{4,3,2,1,0:T(8,128)(2,1)S(1)}, u32[]{:S(2)}, u32[]{:S(2)}) %collective-permute-start.28) | collective-permute-done | bytes 1048608 | tf_op jit(solution)/shard_map/ppermute | solution.py:176
  325.2 1.8 collective-permute-start.36
  327.0 2.7 collective-permute-done.32
  330.0 1.3 collective-permute-start.33
  331.3 18.6 %collective-permute-done.29 = bf16[1,16,2,32,256]{4,3,2,1,0:T(8,128)(2,1)S(1)} collective-permute-done((bf16[1,16,2,32,256]{4,3,2,1,0:T(8,128)(2,1)S(1)}, bf16[1,16,2,32,256]{4,3,2,1,0:T(8,128)(2,1)S(1)}, u32[]{:S(2)}, u32[]{:S(2)}) %collective-permute-start.29) | collective-permute-done | bytes 524320 | tf_op jit(solution)/shard_map/ppermute | solution.py:176
  350.3 1.3 collective-permute-start.30
  352.0 1.3 collective-permute-start.37
  353.3 1.6 pad_maximum_fusion.1
  354.9 13.1 %collective-permute-done.30 = bf16[16,2,32,256]{3,2,1,0:T(8,128)(2,1)S(1)} collective-permute-done((bf16[16,2,32,256]{3,2,1,0:T(8,128)(2,1)S(1)}, bf16[16,2,32,256]{3,2,1,0:T(8,128)(2,1)S(1)}, u32[]{:S(2)}, u32[]{:S(2)}) %collective-permute-start.30) | collective-permute-done | bytes 524320 | tf_op jit(solution)/shard_map/ppermute | solution.py:279
  368.0 1.4 fusion.1
  369.4 6.6 %collective-permute-done.37 = bf16[16,2,32,256]{3,2,1,0:T(8,128)(2,1)S(1)} collective-permute-done((bf16[16,2,32,256]{3,2,1,0:T(8,128)(2,1)S(1)}, bf16[16,2,32,256]{3,2,1,0:T(8,128)(2,1)S(1)}, u32[]{:S(2)}, u32[]{:S(2)}) %collective-permute-start.37) | collective-permute-done | bytes 524320 | tf_op jit(solution)/shard_map/ppermute | solution.py:279
  376.0 1.4 fusion
  (112 shorter events, 24.1 us)
Async XLA Ops:
  0.6 16.1 %copy-start.3 = (bf16[512,2048]{1,0:T(8,128)(2,1)S(1)}, bf16[512,2048]{1,0:T(8,128)(2,1)}, u32[]{:S(2)}) copy-start(bf16[512,2048]{1,0:T(8,128)(2,1)} %refs_3_.1) | copy-start | bytes 6291460
  2.7 42.0 %collective-permute-start.2 = (bf16[1024,256]{1,0:T(8,128)(2,1)}, bf16[1024,256]{1,0:T(8,128)(2,1)}, u32[]{:S(2)}, u32[]{:S(2)}) collective-permute-start(bf16[1024,256]{1,0:T(8,128)(2,1)} %constant_dynamic-slice_fusion.1), channel_id=1, source_target_pairs={{2,0},{1,3},{6,4},{5,7},{10,8},{9,11},{14,12},{13,15},{18,16},{17,... | collective-permute-start | bytes 1572872 | tf_op jit(solution)/shard_map/ppermute | solution.py:233
  9.1 10.6 %copy-start.12 = (s32[2,8,8]{2,1,0:T(8,128)S(1)}, s32[2,8,8]{2,1,0:T(8,128)}, u32[]{:S(2)}) copy-start(s32[2,8,8]{2,1,0:T(8,128)} %param.11) | copy-start | bytes 1540
  9.1 10.7 %copy-start.13 = (s32[2]{0:T(128)S(1)}, s32[2]{0:T(128)}, u32[]{:S(2)}) copy-start(s32[2]{0:T(128)} %constant.68) | copy-start | bytes 28
  9.1 21.8 %collective-permute-start.10 = (bf16[1024,256]{1,0:T(8,128)(2,1)S(1)}, bf16[1024,256]{1,0:T(8,128)(2,1)}, u32[]{:S(2)}, u32[]{:S(2)}) collective-permute-start(bf16[1024,256]{1,0:T(8,128)(2,1)S(1)} %constant_dynamic-slice_fusion), channel_id=1, source_target_pairs={{2,0},{1,3},{6,4},{5,7},{10,8},{9,11},{14,12},{13,15},{18,16},{17,... | collective-permute-start | bytes 1572872 | tf_op jit(solution)/shard_map/ppermute | solution.py:234
  14.4 82.0 %collective-permute-start = (bf16[256,2048]{1,0:T(8,128)(2,1)}, bf16[256,2048]{1,0:T(8,128)(2,1)}, u32[]{:S(2)}, u32[]{:S(2)}) collective-permute-start(bf16[256,2048]{1,0:T(8,128)(2,1)} %get-tuple-element.51), channel_id=1, source_target_pairs={{2,0},{1,3},{6,4},{5,7},{10,8},{9,11},{14,12},{13,15},{18,16},{17,... | collective-permute-start | bytes 3145736 | tf_op jit(solution)/shard_map/ppermute | solution.py:237
  18.1 78.3 %collective-permute-start.1 = (bf16[256,2048]{1,0:T(8,128)(2,1)}, bf16[256,2048]{1,0:T(8,128)(2,1)S(1)}, u32[]{:S(2)}, u32[]{:S(2)}) collective-permute-start(bf16[256,2048]{1,0:T(8,128)(2,1)} %get-tuple-element.49), channel_id=1, source_target_pairs={{2,0},{1,3},{6,4},{5,7},{10,8},{9,11},{14,12},{13,15},{18,16},{17,... | collective-permute-start | bytes 3145736 | tf_op jit(solution)/shard_map/ppermute | solution.py:238
  30.9 18.1 %collective-permute-start.11 = (bf16[1024,256]{1,0:T(8,128)(2,1)}, bf16[1024,256]{1,0:T(8,128)(2,1)S(1)}, u32[]{:S(2)}, u32[]{:S(2)}) collective-permute-start(bf16[1024,256]{1,0:T(8,128)(2,1)} %collective-permute-done.10), channel_id=1, source_target_pairs={{0,16},{8,24},{16,0},{24,8},{1,17},{9,25},{17,1},{25,9},{2,18},{10... | collective-permute-start | bytes 1572872 | tf_op jit(solution)/shard_map/ppermute | solution.py:176
  43.2 25.9 %collective-permute-start.12 = (bf16[1024,256]{1,0:T(8,128)(2,1)}, bf16[1024,256]{1,0:T(8,128)(2,1)S(1)}, u32[]{:S(2)}, u32[]{:S(2)}) collective-permute-start(bf16[1024,256]{1,0:T(8,128)(2,1)} %collective-permute-done.10), channel_id=1, source_target_pairs={{0,8},{8,0},{16,24},{24,16},{1,9},{9,1},{17,25},{25,17},{2,10},{10... | collective-permute-start | bytes 1572872 | tf_op jit(solution)/shard_map/ppermute | solution.py:176
  44.7 22.0 %collective-permute-start.3 = (bf16[1024,256]{1,0:T(8,128)(2,1)}, bf16[1024,256]{1,0:T(8,128)(2,1)S(1)}, u32[]{:S(2)}, u32[]{:S(2)}) collective-permute-start(bf16[1024,256]{1,0:T(8,128)(2,1)} %collective-permute-done.2), channel_id=1, source_target_pairs={{0,8},{8,0},{16,24},{24,16},{1,9},{9,1},{17,25},{25,17},{2,10},{10... | collective-permute-start | bytes 1572872 | tf_op jit(solution)/shard_map/ppermute | solution.py:176
  49.0 21.5 %collective-permute-start.4 = (bf16[1024,256]{1,0:T(8,128)(2,1)}, bf16[1024,256]{1,0:T(8,128)(2,1)S(1)}, u32[]{:S(2)}, u32[]{:S(2)}) collective-permute-start(bf16[1024,256]{1,0:T(8,128)(2,1)} %collective-permute-done.2), channel_id=1, source_target_pairs={{0,16},{8,24},{16,0},{24,8},{1,17},{9,25},{17,1},{25,9},{2,18},{10... | collective-permute-start | bytes 1572872 | tf_op jit(solution)/shard_map/ppermute | solution.py:176
  66.8 10.5 %collective-permute-start.13 = (bf16[1024,256]{1,0:T(8,128)(2,1)S(1)}, bf16[1024,256]{1,0:T(8,128)(2,1)S(1)}, u32[]{:S(2)}, u32[]{:S(2)}) collective-permute-start(bf16[1024,256]{1,0:T(8,128)(2,1)S(1)} %collective-permute-done.11), channel_id=1, source_target_pairs={{0,8},{8,0},{16,24},{24,16},{1,9},{9,1},{17,25},{25,17},{2,10},{10... | collective-permute-start | bytes 1572872 | tf_op jit(solution)/shard_map/ppermute | solution.py:176
  69.1 9.5 %collective-permute-start.5 = (bf16[1024,256]{1,0:T(8,128)(2,1)S(1)}, bf16[1024,256]{1,0:T(8,128)(2,1)S(1)}, u32[]{:S(2)}, u32[]{:S(2)}) collective-permute-start(bf16[1024,256]{1,0:T(8,128)(2,1)S(1)} %collective-permute-done.3), channel_id=1, source_target_pairs={{0,16},{8,24},{16,0},{24,8},{1,17},{9,25},{17,1},{25,9},{2,18},{10... | collective-permute-start | bytes 1572872 | tf_op jit(solution)/shard_map/ppermute | solution.py:176
  70.5 14.7 %copy-start.9 = (bf16[256,2048]{1,0:T(8,128)(2,1)S(1)}, bf16[256,2048]{1,0:T(8,128)(2,1)}, u32[]{:S(2)}) copy-start(bf16[256,2048]{1,0:T(8,128)(2,1)} %get-tuple-element.50) | copy-start | bytes 3145732
  70.5 9.1 %collective-permute-start.14 = (bf16[1024,256]{1,0:T(8,128)(2,1)}, bf16[1024,256]{1,0:T(8,128)(2,1)S(1)}, u32[]{:S(2)}, u32[]{:S(2)}) collective-permute-start(bf16[1024,256]{1,0:T(8,128)(2,1)} %collective-permute-done.10), channel_id=1, source_target_pairs={{0,4},{4,0},{1,5},{5,1},{2,6},{6,2},{3,7},{7,3},{8,12},{12,8},{9,1... | collective-permute-start | bytes 1572872 | tf_op jit(solution)/shard_map/ppermute | solution.py:176
  71.3 21.1 %copy-start.10 = (bf16[256,2048]{1,0:T(8,128)(2,1)S(1)}, bf16[256,2048]{1,0:T(8,128)(2,1)}, u32[]{:S(2)}) copy-start(bf16[256,2048]{1,0:T(8,128)(2,1)} %get-tuple-element.48) | copy-start | bytes 3145732
  77.3 3.5 collective-permute-start.6
  78.5 3.2 collective-permute-start.15
  79.5 3.4 collective-permute-start.16
  80.7 3.2 collective-permute-start.7
  81.7 3.5 collective-permute-start.8
  82.9 9.4 %collective-permute-start.17 = (bf16[1024,256]{1,0:T(8,128)(2,1)S(1)}, bf16[1024,256]{1,0:T(8,128)(2,1)S(1)}, u32[]{:S(2)}, u32[]{:S(2)}) collective-permute-start(bf16[1024,256]{1,0:T(8,128)(2,1)S(1)} %collective-permute-done.13), channel_id=1, source_target_pairs={{0,4},{4,0},{1,5},{5,1},{2,6},{6,2},{3,7},{7,3},{8,12},{12,8},{9,1... | collective-permute-start | bytes 1572872 | tf_op jit(solution)/shard_map/ppermute | solution.py:176
  83.9 11.7 %collective-permute-start.9 = (bf16[1024,256]{1,0:T(8,128)(2,1)S(1)}, bf16[1024,256]{1,0:T(8,128)(2,1)S(1)}, u32[]{:S(2)}, u32[]{:S(2)}) collective-permute-start(bf16[1024,256]{1,0:T(8,128)(2,1)S(1)} %collective-permute-done.5), channel_id=1, source_target_pairs={{0,4},{4,0},{1,5},{5,1},{2,6},{6,2},{3,7},{7,3},{8,12},{12,8},{9,1... | collective-permute-start | bytes 1572872 | tf_op jit(solution)/shard_map/ppermute | solution.py:176
  85.2 48.4 %collective-permute-start.19 = (bf16[256,2048]{1,0:T(8,128)(2,1)S(1)}, bf16[256,2048]{1,0:T(8,128)(2,1)}, u32[]{:S(2)}, u32[]{:S(2)}) collective-permute-start(bf16[256,2048]{1,0:T(8,128)(2,1)S(1)} %copy-done.9), channel_id=1, source_target_pairs={{2,0},{1,3},{6,4},{5,7},{10,8},{9,11},{14,12},{13,15},{18,16},{17,... | collective-permute-start | bytes 3145736 | tf_op jit(solution)/shard_map/ppermute | solution.py:237
  92.4 65.8 %collective-permute-start.20 = (bf16[256,2048]{1,0:T(8,128)(2,1)S(1)}, bf16[256,2048]{1,0:T(8,128)(2,1)}, u32[]{:S(2)}, u32[]{:S(2)}) collective-permute-start(bf16[256,2048]{1,0:T(8,128)(2,1)S(1)} %copy-done.10), channel_id=1, source_target_pairs={{2,0},{1,3},{6,4},{5,7},{10,8},{9,11},{14,12},{13,15},{18,16},{17,... | collective-permute-start | bytes 3145736 | tf_op jit(solution)/shard_map/ppermute | solution.py:238
  132.3 76.0 %collective-permute-start.18 = (bf16[256,2048]{1,0:T(8,128)(2,1)}, bf16[256,2048]{1,0:T(8,128)(2,1)S(1)}, u32[]{:S(2)}, u32[]{:S(2)}) collective-permute-start(bf16[256,2048]{1,0:T(8,128)(2,1)} %get-tuple-element.23), channel_id=1, source_target_pairs={{0,2},{3,1},{4,6},{7,5},{8,10},{11,9},{12,14},{15,13},{16,18},{19,... | collective-permute-start | bytes 3145736 | tf_op jit(solution)/shard_map/ppermute | solution.py:270
  158.2 50.6 %copy-start.8 = (bf16[256,2048]{1,0:T(8,128)(2,1)S(1)}, bf16[256,2048]{1,0:T(8,128)(2,1)}, u32[]{:S(2)}) copy-start(bf16[256,2048]{1,0:T(8,128)(2,1)} %get-tuple-element.22) | copy-start | bytes 3145732
  203.8 51.7 %copy-start.7 = (bf16[256,2048]{1,0:T(8,128)(2,1)S(1)}, bf16[256,2048]{1,0:T(8,128)(2,1)}, u32[]{:S(2)}) copy-start(bf16[256,2048]{1,0:T(8,128)(2,1)} %get-tuple-element.30) | copy-start | bytes 3145732
  203.8 29.3 %collective-permute-start.21 = (bf16[256,2048]{1,0:T(8,128)(2,1)}, bf16[256,2048]{1,0:T(8,128)(2,1)}, u32[]{:S(2)}, u32[]{:S(2)}) collective-permute-start(bf16[256,2048]{1,0:T(8,128)(2,1)} %get-tuple-element.27), channel_id=1, source_target_pairs={{0,2},{3,1},{4,6},{7,5},{8,10},{11,9},{12,14},{15,13},{16,18},{19,... | collective-permute-start | bytes 3145736 | tf_op jit(solution)/shard_map/ppermute | solution.py:270
  205.3 50.2 %copy-start.14 = (bf16[4,16,2,32,256]{4,3,2,1,0:T(8,128)(2,1)S(1)}, bf16[4,16,2,32,256]{4,3,2,1,0:T(8,128)(2,1)}, u32[]{:S(2)}) copy-start(bf16[4,16,2,32,256]{4,3,2,1,0:T(8,128)(2,1)} %get-tuple-element.37) | copy-start | bytes 6291460
  205.3 50.2 %collective-permute-start.23 = (bf16[256,2048]{1,0:T(8,128)(2,1)}, bf16[256,2048]{1,0:T(8,128)(2,1)S(1)}, u32[]{:S(2)}, u32[]{:S(2)}) collective-permute-start(bf16[256,2048]{1,0:T(8,128)(2,1)} %get-tuple-element.31), channel_id=1, source_target_pairs={{0,2},{3,1},{4,6},{7,5},{8,10},{11,9},{12,14},{15,13},{16,18},{19,... | collective-permute-start | bytes 3145736 | tf_op jit(solution)/shard_map/ppermute | solution.py:270
  206.7 69.7 %collective-permute-start.22 = (bf16[256,2048]{1,0:T(8,128)(2,1)}, bf16[256,2048]{1,0:T(8,128)(2,1)S(1)}, u32[]{:S(2)}, u32[]{:S(2)}) collective-permute-start(bf16[256,2048]{1,0:T(8,128)(2,1)} %get-tuple-element.29), channel_id=1, source_target_pairs={{0,2},{3,1},{4,6},{7,5},{8,10},{11,9},{12,14},{15,13},{16,18},{19,... | collective-permute-start | bytes 3145736 | tf_op jit(solution)/shard_map/ppermute | solution.py:270
  208.2 68.4 %collective-permute-start.24 = (bf16[4,16,2,32,256]{4,3,2,1,0:T(8,128)(2,1)}, bf16[4,16,2,32,256]{4,3,2,1,0:T(8,128)(2,1)S(1)}, u32[]{:S(2)}, u32[]{:S(2)}) collective-permute-start(bf16[4,16,2,32,256]{4,3,2,1,0:T(8,128)(2,1)} %get-tuple-element.33), channel_id=1, source_target_pairs={{0,4},{4,0},{1,5},{5,1},{2,6},{6,2},{3,7},{7,3},{8,12},{12,8},{9,1... | collective-permute-start | bytes 6291464 | tf_op jit(solution)/shard_map/ppermute | solution.py:176
  208.3 70.8 %collective-permute-start.27 = (bf16[4,16,2,32,256]{4,3,2,1,0:T(8,128)(2,1)}, bf16[4,16,2,32,256]{4,3,2,1,0:T(8,128)(2,1)S(1)}, u32[]{:S(2)}, u32[]{:S(2)}) collective-permute-start(bf16[4,16,2,32,256]{4,3,2,1,0:T(8,128)(2,1)} %get-tuple-element.35), channel_id=1, source_target_pairs={{0,4},{4,0},{1,5},{5,1},{2,6},{6,2},{3,7},{7,3},{8,12},{12,8},{9,1... | collective-permute-start | bytes 6291464 | tf_op jit(solution)/shard_map/ppermute | solution.py:176
  208.8 67.7 %copy-start.6 = (bf16[256,2048]{1,0:T(8,128)(2,1)S(1)}, bf16[256,2048]{1,0:T(8,128)(2,1)}, u32[]{:S(2)}) copy-start(bf16[256,2048]{1,0:T(8,128)(2,1)} %get-tuple-element.28) | copy-start | bytes 3145732
  233.1 47.4 %collective-permute-start.34 = (bf16[4,16,2,32,256]{4,3,2,1,0:T(8,128)(2,1)}, bf16[4,16,2,32,256]{4,3,2,1,0:T(8,128)(2,1)S(1)}, u32[]{:S(2)}, u32[]{:S(2)}) collective-permute-start(bf16[4,16,2,32,256]{4,3,2,1,0:T(8,128)(2,1)} %get-tuple-element.39), channel_id=1, source_target_pairs={{0,4},{4,0},{1,5},{5,1},{2,6},{6,2},{3,7},{7,3},{8,12},{12,8},{9,1... | collective-permute-start | bytes 6291464 | tf_op jit(solution)/shard_map/ppermute | solution.py:176
  233.1 43.4 %copy-start.5 = (bf16[4,16,2,32,256]{4,3,2,1,0:T(8,128)(2,1)S(1)}, bf16[4,16,2,32,256]{4,3,2,1,0:T(8,128)(2,1)}, u32[]{:S(2)}) copy-start(bf16[4,16,2,32,256]{4,3,2,1,0:T(8,128)(2,1)} %get-tuple-element.32) | copy-start | bytes 6291460
  255.5 26.2 %collective-permute-start.31 = (bf16[4,16,2,32,256]{4,3,2,1,0:T(8,128)(2,1)S(1)}, bf16[4,16,2,32,256]{4,3,2,1,0:T(8,128)(2,1)S(1)}, u32[]{:S(2)}, u32[]{:S(2)}) collective-permute-start(bf16[4,16,2,32,256]{4,3,2,1,0:T(8,128)(2,1)S(1)} %copy-done.14), channel_id=1, source_target_pairs={{0,4},{4,0},{1,5},{5,1},{2,6},{6,2},{3,7},{7,3},{8,12},{12,8},{9,1... | collective-permute-start | bytes 6291464 | tf_op jit(solution)/shard_map/ppermute | solution.py:176
  277.2 26.2 %collective-permute-start.25 = (bf16[2,16,2,32,256]{4,3,2,1,0:T(8,128)(2,1)S(1)}, bf16[2,16,2,32,256]{4,3,2,1,0:T(8,128)(2,1)S(1)}, u32[]{:S(2)}, u32[]{:S(2)}) collective-permute-start(bf16[2,16,2,32,256]{4,3,2,1,0:T(8,128)(2,1)S(1)} %pad_maximum_fusion.2), channel_id=1, source_target_pairs={{0,8},{8,0},{16,24},{24,16},{1,9},{9,1},{17,25},{25,17},{2,10},{10... | collective-permute-start | bytes 3145736 | tf_op jit(solution)/shard_map/ppermute | solution.py:176
  279.7 44.3 %collective-permute-start.28 = (bf16[2,16,2,32,256]{4,3,2,1,0:T(8,128)(2,1)S(1)}, bf16[2,16,2,32,256]{4,3,2,1,0:T(8,128)(2,1)S(1)}, u32[]{:S(2)}, u32[]{:S(2)}) collective-permute-start(bf16[2,16,2,32,256]{4,3,2,1,0:T(8,128)(2,1)S(1)} %pad_maximum_fusion.3), channel_id=1, source_target_pairs={{0,8},{8,0},{16,24},{24,16},{1,9},{9,1},{17,25},{25,17},{2,10},{10... | collective-permute-start | bytes 3145736 | tf_op jit(solution)/shard_map/ppermute | solution.py:176
  281.1 43.8 %collective-permute-start.35 = (bf16[2,16,2,32,256]{4,3,2,1,0:T(8,128)(2,1)S(1)}, bf16[2,16,2,32,256]{4,3,2,1,0:T(8,128)(2,1)S(1)}, u32[]{:S(2)}, u32[]{:S(2)}) collective-permute-start(bf16[2,16,2,32,256]{4,3,2,1,0:T(8,128)(2,1)S(1)} %pad_maximum_fusion.5), channel_id=1, source_target_pairs={{0,16},{8,24},{16,0},{24,8},{1,17},{9,25},{17,1},{25,9},{2,18},{10... | collective-permute-start | bytes 3145736 | tf_op jit(solution)/shard_map/ppermute | solution.py:176
  282.2 47.5 %collective-permute-start.32 = (bf16[2,16,2,32,256]{4,3,2,1,0:T(8,128)(2,1)S(1)}, bf16[2,16,2,32,256]{4,3,2,1,0:T(8,128)(2,1)S(1)}, u32[]{:S(2)}, u32[]{:S(2)}) collective-permute-start(bf16[2,16,2,32,256]{4,3,2,1,0:T(8,128)(2,1)S(1)} %pad_maximum_fusion.4), channel_id=1, source_target_pairs={{0,16},{8,24},{16,0},{24,8},{1,17},{9,25},{17,1},{25,9},{2,18},{10... | collective-permute-start | bytes 3145736 | tf_op jit(solution)/shard_map/ppermute | solution.py:176
  303.6 51.2 %collective-permute-start.26 = (bf16[1,16,2,32,256]{4,3,2,1,0:T(8,128)(2,1)S(1)}, bf16[1,16,2,32,256]{4,3,2,1,0:T(8,128)(2,1)S(1)}, u32[]{:S(2)}, u32[]{:S(2)}) collective-permute-start(bf16[1,16,2,32,256]{4,3,2,1,0:T(8,128)(2,1)S(1)} %add_convert_fusion.11), channel_id=1, source_target_pairs={{0,16},{8,24},{16,0},{24,8},{1,17},{9,25},{17,1},{25,9},{2,18},{10... | collective-permute-start | bytes 1572872 | tf_op jit(solution)/shard_map/ppermute | solution.py:176
  324.2 25.7 %collective-permute-start.29 = (bf16[1,16,2,32,256]{4,3,2,1,0:T(8,128)(2,1)S(1)}, bf16[1,16,2,32,256]{4,3,2,1,0:T(8,128)(2,1)S(1)}, u32[]{:S(2)}, u32[]{:S(2)}) collective-permute-start(bf16[1,16,2,32,256]{4,3,2,1,0:T(8,128)(2,1)S(1)} %add_convert_fusion.8), channel_id=1, source_target_pairs={{0,16},{8,24},{16,0},{24,8},{1,17},{9,25},{17,1},{25,9},{2,18},{10... | collective-permute-start | bytes 1572872 | tf_op jit(solution)/shard_map/ppermute | solution.py:176
  325.2 26.4 %collective-permute-start.36 = (bf16[1,16,2,32,256]{4,3,2,1,0:T(8,128)(2,1)S(1)}, bf16[1,16,2,32,256]{4,3,2,1,0:T(8,128)(2,1)S(1)}, u32[]{:S(2)}, u32[]{:S(2)}) collective-permute-start(bf16[1,16,2,32,256]{4,3,2,1,0:T(8,128)(2,1)S(1)} %add_convert_fusion.1), channel_id=1, source_target_pairs={{0,8},{8,0},{16,24},{24,16},{1,9},{9,1},{17,25},{25,17},{2,10},{10... | collective-permute-start | bytes 1572872 | tf_op jit(solution)/shard_map/ppermute | solution.py:176
  330.0 39.4 %collective-permute-start.33 = (bf16[1,16,2,32,256]{4,3,2,1,0:T(8,128)(2,1)S(1)}, bf16[1,16,2,32,256]{4,3,2,1,0:T(8,128)(2,1)S(1)}, u32[]{:S(2)}, u32[]{:S(2)}) collective-permute-start(bf16[1,16,2,32,256]{4,3,2,1,0:T(8,128)(2,1)S(1)} %add_convert_fusion.4), channel_id=1, source_target_pairs={{0,8},{8,0},{16,24},{24,16},{1,9},{9,1},{17,25},{25,17},{2,10},{10... | collective-permute-start | bytes 1572872 | tf_op jit(solution)/shard_map/ppermute | solution.py:176
  350.3 17.7 %collective-permute-start.30 = (bf16[16,2,32,256]{3,2,1,0:T(8,128)(2,1)S(1)}, bf16[16,2,32,256]{3,2,1,0:T(8,128)(2,1)S(1)}, u32[]{:S(2)}, u32[]{:S(2)}) collective-permute-start(bf16[16,2,32,256]{3,2,1,0:T(8,128)(2,1)S(1)} %fusion.2), channel_id=1, source_target_pairs={{0,2},{3,1},{4,6},{7,5},{8,10},{11,9},{12,14},{15,13},{16,18},{19,... | collective-permute-start | bytes 1572872 | tf_op jit(solution)/shard_map/ppermute | solution.py:279
  352.0 24.0 %collective-permute-start.37 = (bf16[16,2,32,256]{3,2,1,0:T(8,128)(2,1)S(1)}, bf16[16,2,32,256]{3,2,1,0:T(8,128)(2,1)S(1)}, u32[]{:S(2)}, u32[]{:S(2)}) collective-permute-start(bf16[16,2,32,256]{3,2,1,0:T(8,128)(2,1)S(1)} %fusion.3), channel_id=1, source_target_pairs={{0,2},{3,1},{4,6},{7,5},{8,10},{11,9},{12,14},{15,13},{16,18},{19,... | collective-permute-start | bytes 1572872 | tf_op jit(solution)/shard_map/ppermute | solution.py:279
  (6 other events, 26.0 us)

commit v2 on v1

v2 whole, which is shorter than its diff:
```python
import functools
import math

import jax
import jax.numpy as jnp
from jax import lax
from jax.experimental import pallas as pl
from jax.experimental.pallas import tpu as pltpu
from jax.sharding import PartitionSpec as P

F32 = jnp.float32
BF16 = jnp.bfloat16
ROOT = math.sqrt(2.0 / math.pi)
CUBIC = 0.044715


def dot(a, b, over):
    return lax.dot_general(a, b, ((over[:1], over[1:]), ((), ())), preferred_element_type=F32)


def activate(pre, d_hidden):
    square = pre * pre
    tanh = jnp.tanh(pre * (ROOT + (ROOT * CUBIC) * square))
    cdf = 0.5 + 0.5 * tanh
    slope = cdf + pre * (0.5 - 0.5 * tanh * tanh) * (ROOT + (3.0 * ROOT * CUBIC) * square)
    return (pre * cdf).astype(BF16), (d_hidden * slope).astype(BF16)


def layer_kernel(first, rows, slots, ids, *refs):
    refs = list(refs)
    take = lambda count: [refs.pop(0) for _ in range(count)]
    near = take(2)
    far = take(1 if first else 2)
    up_far, down_far, up_near, down_near = take(4)
    if not first:
        hidden_before, d_pre_before = take(2)
    near_out = take(2)
    (far_out,) = take(1)
    if first:
        hidden_out, d_pre_out = take(2)
    else:
        sums = take(4)
    out_acc, back_acc = take(2)
    if not first:
        up_sum, down_sum = take(2)
    step = pl.program_id(0)
    steps = pl.num_programs(0)
    each, _, size, _ = up_far.shape
    low = 0 if first else rows[0]
    count = rows[0] if first else rows[1]

    @pl.when(step == 0)
    def _():
        out_acc[...] = jnp.zeros_like(out_acc)
        back_acc[...] = jnp.zeros_like(back_acc)

    theirs = step < steps // 2

    def columns(block):
        return pl.ds(pl.multiple_of(block * size, size), size)

    def both(k, at, part):
        chunk = pl.ds(0, rows[0]) if part == 0 else pl.ds(rows[0], rows[1])
        return jnp.concatenate([near[k][chunk, at[0]], far[part][k, :, at[1]]], axis=1)

    def pick(theirs_ref, ours_ref, e):
        return [jnp.where(theirs, theirs_ref[e, 1 - s], ours_ref[e, s]) for s in range(2)]

    work = []
    for e in range(each):
        ins = [columns(ids[k, step * each + e]) for k in (0, 1)]
        outs = [columns(ids[k, step * each + e]) for k in (2, 3)]
        up_cat = jnp.concatenate(pick(up_far, up_near, e), axis=0)
        down_cat = jnp.concatenate(pick(down_far, down_near, e), axis=1)
        part = 0 if first else 1
        x_cat = both(0, ins, part)
        g_cat = both(1, outs, part)
        pre = dot(x_cat, up_cat, (1, 0))
        d_hidden = dot(g_cat, down_cat, (1, 1))
        work.append((ins, outs, x_cat, g_cat, up_cat, down_cat, pre, d_hidden))
    done = []
    for e, (ins, outs, x_cat, g_cat, up_cat, down_cat, pre, d_hidden) in enumerate(work):
        hidden, d_pre = activate(pre, d_hidden)
        done.append((dot(hidden, down_cat, (1, 0)), dot(d_pre, up_cat, (1, 1))))
        if first:
            hidden_out[e] = hidden
            d_pre_out[e] = d_pre
        else:
            up_sum[e] = dot(x_cat, d_pre, (0, 0)) + dot(both(0, ins, 0), d_pre_before[e], (0, 0))
            down_sum[e] = dot(hidden, g_cat, (0, 0)) + dot(hidden_before[e], both(1, outs, 0), (0, 0))
    for (ins, outs, *_), (out, back) in zip(work, done):
        for s in range(2):
            out_acc[s, :, outs[s]] += out[:, s * size : (s + 1) * size]
            back_acc[s, :, ins[s]] += back[:, s * size : (s + 1) * size]
    if not first:
        me = ids[4, 0]
        shard = sums[0].shape[4]
        shards = size // shard

        def store(keep, send, flip):
            for e in range(each):
                for place in range(shards):
                    start = pl.multiple_of((place ^ me) * shard, shard)
                    to = send if place & 1 else keep
                    for s in range(2):
                        at = (1 - s if flip else s) * size
                        to[0, slots[0][place], e, s] = up_sum[
                            e, pl.ds(at + start, shard)
                        ].astype(BF16)
                        to[1, slots[1][place], e, s] = down_sum[
                            e, pl.ds(start, shard), at : at + size
                        ].astype(BF16)

        pl.when(theirs)(lambda: store(*sums[:2], True))
        pl.when(jnp.logical_not(theirs))(lambda: store(*sums[2:], False))

    @pl.when(step == steps - 1)
    def _():
        for k, acc in enumerate((out_acc, back_acc)):
            near_out[k][...] = acc[0].astype(BF16)
            far_out[k] = acc[1].astype(BF16)


def layer(first, rows, slots, each, ids, near, far, up_far, down_far, up, down, before=()):
    hid, _, size, _ = up.shape
    width = near[0].shape[1]
    shards = len(slots[0])
    all_rows = rows[0] if first else sum(rows)
    count = rows[0] if first else rows[1]
    turns = hid // each
    steps = 2 * turns

    def whole(shape):
        return pl.BlockSpec(shape, lambda i, ids: (0,) * len(shape))

    def weight(part):
        return pl.BlockSpec(
            (each, 2, size, size),
            lambda i, ids: (jnp.clip(i - part * turns, 0, turns - 1), 0, 0, 0),
        )

    kept = pl.BlockSpec((each, rows[0], size), lambda i, ids: (i, 0, 0))
    in_specs = [whole((all_rows, width))] * 2 + [whole(part.shape) for part in far]
    in_specs += [weight(0)] * 2 + [weight(1)] * 2
    out_shape = [jax.ShapeDtypeStruct((count, width), BF16)] * 2
    out_shape += [jax.ShapeDtypeStruct((2, count, width), BF16)]
    out_specs = [whole(out.shape) for out in out_shape]
    scratch = [pltpu.VMEM((2, count, width), F32)] * 2
    if first:
        out_shape += [jax.ShapeDtypeStruct((2 * hid, count, size), BF16)] * 2
        out_specs += [kept] * 2
    else:
        in_specs += [kept] * 2
        shard = size // shards
        out_shape += [jax.ShapeDtypeStruct((2, shards // 2, hid, 2, shard, size), BF16)] * 4
        for part in range(2):
            out_specs += [
                pl.BlockSpec(
                    (2, shards // 2, each, 2, shard, size),
                    lambda i, ids, part=part: (
                        *(0, 0, jnp.clip(i - part * turns, 0, turns - 1)),
                        *(0, 0, 0),
                    ),
                )
            ] * 2
        scratch += [
            pltpu.VMEM((each, 2 * size, size), F32),
            pltpu.VMEM((each, size, 2 * size), F32),
        ]
    return pl.pallas_call(
        functools.partial(layer_kernel, first, rows, slots),
        out_shape=out_shape,
        grid_spec=pltpu.PrefetchScalarGridSpec(
            num_scalar_prefetch=1,
            grid=(steps,),
            in_specs=in_specs,
            out_specs=out_specs,
            scratch_shapes=scratch,
        ),
        compiler_params=pltpu.CompilerParams(
            dimension_semantics=("arbitrary",), vmem_limit_bytes=60 << 20
        ),
        cost_estimate=pl.CostEstimate(flops=0, bytes_accessed=0, transcendentals=0),
    )(ids, *near, *far, up_far, down_far, up, down, *before)


def hop(block, bit):
    seq = lax.axis_size("seq")
    axis, bit = ("seq", bit) if bit < seq else ("dp", bit // seq)
    return lax.ppermute(block, axis, [(i, i ^ bit) for i in range(lax.axis_size(axis))])


def bits_of(count, unit=1):
    return [unit << k for k in range(count.bit_length() - 1)]


def gather(shard, order, me, shards):
    parts = {0: shard}
    for bit in order:
        for place in list(parts):
            parts[place | bit] = hop(parts[place], bit)
    table = jnp.zeros((shards, *shard.shape), shard.dtype)
    for place, part in parts.items():
        table = lax.dynamic_update_slice_in_dim(table, part[None], place ^ me, 0)
    return table


def total(terms):
    return sum(term.astype(F32) for term in terms)


def reduce_scatter(terms, order):
    for bit in order:
        half = terms[0].shape[0] // 2
        got = hop(total([term[half:] for term in terms]).astype(BF16), bit)
        terms = [term[:half] for term in terms] + [got]
    return total(terms)[0]


def slots_of(order, shards):
    return [
        sum(1 << (len(order) - 1 - k) for k, bit in enumerate(order) if place & bit)
        for place in range(shards)
    ]


def after(value, *earlier):
    return lax.optimization_barrier((value, *earlier))[0]


def on_device(tokens, out_grad, up_perm, down_perm, up_weight, down_weight):
    tok_rows, width = tokens.shape
    hid, _, size, _ = up_weight.shape
    groups, group = lax.axis_size("tensor"), lax.axis_index("tensor")
    away = groups // 2
    dp, seq = lax.axis_size("dp"), lax.axis_size("seq")
    shards = dp * seq
    me = lax.axis_index("dp") * seq + lax.axis_index("seq")
    seq_bits, dp_bits = bits_of(seq), bits_of(dp, seq)
    back = [(p, p + away) if p % 2 == 0 else (p + away, p) for p in range(away)]
    into = [(other, worker) for worker, other in back]
    works = (group % away % 2 == 0) != (group >= away)
    partner = (group + away) % groups

    rows = (tok_rows // 2, tok_rows - tok_rows // 2)
    lines = hid * 2 * size // shards

    def fetch(weight):
        shard = lax.dynamic_slice_in_dim(weight.reshape(-1, size), me * lines, lines, 0)
        return lax.ppermute(shard, "tensor", into)

    up_shard, down_shard = fetch(up_weight), fetch(down_weight)
    far = []
    for low, high in ((0, rows[0]), (rows[0], tok_rows)):
        pair = jnp.stack([tokens[low:high], out_grad[low:high]])
        far.append(lax.ppermute(pair, "tensor", into))
    up_far = gather(up_shard, dp_bits + seq_bits, me, shards).reshape(up_weight.shape)
    down_far = gather(down_shard, dp_bits[::-1] + seq_bits, me, shards).reshape(up_weight.shape)

    def block_ids(perm):
        flat = perm.reshape(2, -1)
        theirs = lax.dynamic_slice_in_dim(flat, partner * hid, hid, 1)
        mine = lax.dynamic_slice_in_dim(flat, group * hid, hid, 1)
        return jnp.concatenate([theirs[::-1], mine], axis=1)

    ids = jnp.concatenate(
        [block_ids(up_perm), block_ids(down_perm), jnp.full((1, 2 * hid), me, jnp.int32)]
    )

    orders = [dp_bits + seq_bits[1:], dp_bits[::-1] + seq_bits[1:]]
    slots = [slots_of(order, shards) for order in orders]
    each = min(4, hid)
    near = (tokens, out_grad)
    weights = (up_far, down_far, up_weight, down_weight)
    one = layer(True, rows, slots, each, ids, near, far[:1], *weights)
    first_out, far[1] = lax.optimization_barrier((one[2], far[1]))
    two = layer(False, rows, slots, each, ids, near, far, *weights, one[3:])

    got = [lax.ppermute(first_out, "tensor", back)]
    got[0], *two = lax.optimization_barrier((got[0], *two))
    got.append(lax.ppermute(two[2], "tensor", back))

    def plane_sum(keep, send):
        come = hop(send, seq_bits[0])
        return [reduce_scatter([keep[k], come[k]], orders[k]) for k in range(2)]

    theirs = [
        lax.ppermute(part.astype(BF16), "tensor", back) for part in plane_sum(two[3], two[4])
    ]
    mine = plane_sum(two[5], two[6])
    *got, mine[0] = lax.optimization_barrier((*got, mine[0]))

    def deliver(k):
        return jnp.concatenate(
            [jnp.where(works, part[k], come[k]) for part, come in zip((one, two), got)]
        )

    scale = float(tok_rows * shards) ** (-0.5)
    grads = [jnp.where(works, m, t.astype(F32)) * scale for m, t in zip(mine, theirs)]
    return deliver(0), deliver(1), grads[0], grads[1]


def solution(mesh):
    in_specs = (
        P(("dp", "seq"), "tensor"),
        P(("dp", "seq"), "tensor"),
        P(),
        P(),
        P("tensor", None, None, None),
        P("tensor", None, None, None),
    )
    out_specs = (
        P(("dp", "seq"), "tensor"),
        P(("dp", "seq"), "tensor"),
        P("tensor", None, ("dp", "seq"), None),
        P("tensor", None, ("dp", "seq"), None),
    )
    return jax.shard_map(
        on_device, mesh=mesh, in_specs=in_specs, out_specs=out_specs, check_vma=False
    )
```

time: 380 us -> 275 us (0.72)
  waiting for transfers between devices: 203 us -> 122 us
  Pallas kernels: 80.5 us -> 59.9 us
  other arithmetic: 12.7 us -> 29.8 us
  starting transfers between devices: 45.4 us -> 33.8 us
  local copies, waits for them, and re-layouts: 34.6 us -> 27.3 us
    ppermute x12 -> x8, waiting for transfers between devices: 121 us -> 49.4 us  [the longest x2 25.1 us: on_device(): far.append(lax.ppermute(pair, 'tensor', into))]
    pallas_call x2, Pallas kernels: 80.5 us -> 59.9 us  [layer(): pl.pallas_call(functools.partial(layer_kernel, first, rows, slots), out_s...]
    ppermute x12 -> x8, starting transfers between devices: 28 us -> 15.3 us  [the longest x2 5.82 us: fetch(): return lax.ppermute(shard, 'tensor', into)]
    convert_element_type x8 -> x6, other arithmetic: 2.91 us -> 15.1 us  [the longest x4 10.7 us: reduce_scatter(): got = hop(total([term[half:] for term in terms]).astype(BF16), bit)]
    concatenate x2 -> x0, local copies, waits for them, and re-layouts: 10.1 us -> none  [both(): jnp.concatenate([jnp.zeros((shards, lines, size), BF16), weight.reshape(s...]
    ppermute x26 -> x24, waiting for transfers between devices: 82 us -> 72.8 us  [hop(): lax.ppermute(block, axis, [(i, i ^ bit) for i in range(lax.axis_size(axis...]
    another operation x0 -> x3, local copies, waits for them, and re-layouts: none -> 7.33 us
    slice x2 -> x0, local copies, waits for them, and re-layouts: 4.56 us -> none  [the longest x1 3.1 us: on_device(): x_far.append(lax.ppermute(tokens[low:high], 'tensor', into))]
  transfers between devices with their start and end apart: 38 -> 32, of which waited for: 14 -> 15; matrix products, arithmetic and copies ran while one was open for 11% -> 19% of each run, Pallas kernels for 21% -> 22%
where the time goes in v2:
time: 275 us; the launch traced here: 274 us
  waiting for transfers between devices  122 us (44%)
  Pallas kernels  59.9 us (22%)
  starting transfers between devices  33.8 us (12%)
  other arithmetic  29.8 us (11%)
  local copies, waits for them, and re-layouts  27.3 us (10%)
    ppermute x24, waiting for transfers between devices, hop(): lax.ppermute(block, axis, [(i, i ^ bit) for i in range(lax.axis_size(axis...  72.8 us
    pallas_call x2, Pallas kernels, layer(): pl.pallas_call(functools.partial(layer_kernel, first, rows, slots), out_s...  59.9 us
    ppermute x2, waiting for transfers between devices, on_device(): far.append(lax.ppermute(pair, 'tensor', into))  25.1 us
    ppermute x24, starting transfers between devices, hop(): lax.ppermute(block, axis, [(i, i ^ bit) for i in range(lax.axis_size(axis...  18.5 us
    dynamic_update_slice x16, local copies, waits for them, and re-layouts, gather(): table = lax.dynamic_update_slice_in_dim(table, part[None], place ^ me, 0)  14.4 us
    ppermute x1, waiting for transfers between devices, on_device(): got = [lax.ppermute(first_out, 'tensor', back)]  11 us
    convert_element_type x4, other arithmetic, reduce_scatter(): got = hop(total([term[half:] for term in terms]).astype(BF16), bit)  10.7 us
    ppermute x2, waiting for transfers between devices, fetch(): return lax.ppermute(shard, 'tensor', into)  6.69 us
  transfers between devices with their start and end apart: 32, of which 15 were waited for; matrix products, arithmetic and copies ran while one was open for 19% of the time, Pallas kernels for 22%

profile of v2, /device:TPU:8, one launch (start us, length us, event | category | flops | bytes accessed | tf_op | source)
XLA Modules:
  0.0 273.9 jit_solution(3827611502496002481)
XLA Ops:
  0.6 1.9 constant_dynamic-slice_fusion.1
  2.5 4.5 %collective-permute-start.1 = (bf16[1024,256]{1,0:T(8,128)(2,1)}, bf16[1024,256]{1,0:T(8,128)(2,1)S(1)}, u32[]{:S(2)}, u32[]{:S(2)}) collective-permute-start(bf16[1024,256]{1,0:T(8,128)(2,1)} %constant_dynamic-slice_fusion.1), channel_id=1, source_target_pairs={{2,0},{1,3},{6,4},{5,7},{10,8},{9,11},{14,12},{13,15},{18,16},{17,... | collective-permute-start | bytes 1572872 | tf_op jit(solution)/shard_map/ppermute | solution.py:250
  7.0 1.9 constant_dynamic-slice_fusion
  10.2 2.8 %slice_bitcast_fusion = (bf16[1,256,2048]{2,1,0:T(8,128)(2,1)S(1)}, bf16[1,256,2048]{2,1,0:T(8,128)(2,1)S(1)}, bf16[1,256,2048]{2,1,0:T(8,128)(2,1)S(1)}, bf16[1,256,2048]{2,1,0:T(8,128)(2,1)S(1)}) fusion(bf16[512,2048]{1,0:T(8,128)(2,1)} %refs_1_.3, bf16[512,2048]{1,0:T(8,128)(2,1)} %refs_0_.3), kind=kLoop, calls=%fused_computation.38 | loop fusion | bytes 8388608 | tf_op jit(solution)/shard_map/stack | solution.py:255
  13.0 1.5 pad_maximum_fusion
  14.5 1.4 collective-permute-start
  15.9 1.5 pad_maximum_fusion.1
  17.4 2.6 collective-permute-start.17
  20.4 1.6 collective-permute-start.2
  22.6 1.5 collective-permute-start.3
  24.2 6.7 %collective-permute-done.9 = bf16[1024,256]{1,0:T(8,128)(2,1)S(1)} collective-permute-done((bf16[1024,256]{1,0:T(8,128)(2,1)}, bf16[1024,256]{1,0:T(8,128)(2,1)S(1)}, u32[]{:S(2)}, u32[]{:S(2)}) %collective-permute-start.9) | collective-permute-done | bytes 524320 | tf_op jit(solution)/shard_map/ppermute | solution.py:250
  30.9 1.5 collective-permute-start.10
  32.4 2.3 broadcast.9.clone
  35.6 2.2 broadcast.9.clone.1
  38.6 1.6 collective-permute-start.11
  40.2 1.9 bitcast_dynamic-update-slice_fusion.14
  42.1 4.9 %collective-permute-done.10 = bf16[1024,256]{1,0:T(8,128)(2,1)S(1)} collective-permute-done((bf16[1024,256]{1,0:T(8,128)(2,1)S(1)}, bf16[1024,256]{1,0:T(8,128)(2,1)S(1)}, u32[]{:S(2)}, u32[]{:S(2)}) %collective-permute-start.10) | collective-permute-done | bytes 524320 | tf_op jit(solution)/shard_map/ppermute | solution.py:190
  47.0 1.5 collective-permute-start.4
  51.6 7.8 %collective-permute-done.4 = bf16[1024,256]{1,0:T(8,128)(2,1)S(1)} collective-permute-done((bf16[1024,256]{1,0:T(8,128)(2,1)}, bf16[1024,256]{1,0:T(8,128)(2,1)S(1)}, u32[]{:S(2)}, u32[]{:S(2)}) %collective-permute-start.4) | collective-permute-done | bytes 524320 | tf_op jit(solution)/shard_map/ppermute | solution.py:190
  70.3 5.5 %collective-permute-done.refs_2_ = bf16[2,256,2048]{2,1,0:T(8,128)(2,1)S(1)} collective-permute-done((bf16[2,256,2048]{2,1,0:T(8,128)(2,1)}, bf16[2,256,2048]{2,1,0:T(8,128)(2,1)S(1)}, u32[]{:S(2)}, u32[]{:S(2)}) %collective-permute-start) | collective-permute-done | bytes 2097184 | tf_op jit(solution)/shard_map/ppermute | solution.py:256
  77.1 22.8 %shard_map.93 = (bf16[256,2048]{1,0:T(8,128)(2,1)}, bf16[256,2048]{1,0:T(8,128)(2,1)}, bf16[2,256,2048]{2,1,0:T(8,128)(2,1)}, bf16[32,256,256]{2,1,0:T(8,128)(2,1)}, bf16[32,256,256]{2,1,0:T(8,128)(2,1)}) custom-call(s32[5,32]{1,0:T(8,128)} %add_add_fusion.ids, bf16[512,2048]{1,0:T(8,128)(2,1)} %refs_0_.3, bf16[512,2048]{1,0:T(8,128)(2,1)} %refs_1_.3, ...), custom_call_target="tpu_custom_call" | custom-call | tf_op jit(solution)/shard_map/pallas_call | solution.py:170
  100.0 19.6 %collective-permute-done.17.refs_3_ = bf16[2,256,2048]{2,1,0:T(8,128)(2,1)} collective-permute-done((bf16[2,256,2048]{2,1,0:T(8,128)(2,1)}, bf16[2,256,2048]{2,1,0:T(8,128)(2,1)}, u32[]{:S(2)}, u32[]{:S(2)}) %collective-permute-start.17) | collective-permute-done | bytes 2097184 | tf_op jit(solution)/shard_map/ppermute | solution.py:256
  119.6 1.5 collective-permute-start.18
  121.1 37.1 %shard_map.94 = (bf16[256,2048]{1,0:T(8,128)(2,1)}, bf16[256,2048]{1,0:T(8,128)(2,1)}, bf16[2,256,2048]{2,1,0:T(8,128)(2,1)}, bf16[2,4,16,2,32,256]{5,4,3,2,1,0:...) custom-call(s32[5,32]{1,0:T(8,128)} %add_add_fusion.ids, ...), custom_call_target="tpu_custom_call" | custom-call | tf_op jit(solution)/shard_map/pallas_call | solution.py:170
  158.2 11.0 %collective-permute-done.18 = bf16[2,256,2048]{2,1,0:T(8,128)(2,1)S(1)} collective-permute-done((bf16[2,256,2048]{2,1,0:T(8,128)(2,1)}, bf16[2,256,2048]{2,1,0:T(8,128)(2,1)S(1)}, u32[]{:S(2)}, u32[]{:S(2)}) %collective-permute-start.18) | collective-permute-done | bytes 2097184 | tf_op jit(solution)/shard_map/ppermute | solution.py:279
  169.7 6.9 %collective-permute-done.20 = bf16[2,4,16,2,32,256]{5,4,3,2,1,0:T(8,128)(2,1)S(1)} collective-permute-done((bf16[2,4,16,2,32,256]{5,4,3,2,1,0:T(8,128)(2,1)}, bf16[2,4,16,2,32,256]{5,4,3,2,1,0:T(8,128)(2,1)S(1)}, u32[]{:S(2)}, u32[]{:S(2)}) %collective-permute-start.20) | collective-permute-done | bytes 4194336 | tf_op jit(solution)/shard_map/ppermute | solution.py:190
  176.6 4.0 %fusion.2 = (bf16[2,16,2,32,256]{4,3,2,1,0:T(8,128)(2,1)S(1)}, bf16[2,16,2,32,256]{4,3,2,1,0:T(8,128)(2,1)S(1)}) fusion(bf16[2,4,16,2,32,256]{5,4,3,2,1,0:T(8,128)(2,1)S(1)} %collective-permute-done.20, bf16[2,4,16,2,32,256]{5,4,3,2,1,0:T(8,128)(2,1)} %get-tuple-element.44), kind=kLoop, calls=%fused_computation.10 | loop fusion | flops 4194304 | bytes 6291456 | tf_op jit(solution)/shard_map/convert_element_type | solution.py:215
  180.6 1.6 collective-permute-start.27
  182.2 1.5 collective-permute-start.21
  185.0 2.3 fusion.3
  188.3 18.3 %collective-permute-done.27 = bf16[2,16,2,32,256]{4,3,2,1,0:T(8,128)(2,1)S(1)} collective-permute-done((bf16[2,16,2,32,256]{4,3,2,1,0:T(8,128)(2,1)S(1)}, bf16[2,16,2,32,256]{4,3,2,1,0:T(8,128)(2,1)S(1)}, u32[]{:S(2)}, u32[]{:S(2)}) %collective-permute-start.27) | collective-permute-done | bytes 1048608 | tf_op jit(solution)/shard_map/ppermute | solution.py:190
  206.7 1.6 collective-permute-done.21
  208.2 3.2 %fusion.8 = (bf16[1,16,2,32,256]{4,3,2,1,0:T(8,128)(2,1)}, bf16[1,16,2,32,256]{4,3,2,1,0:T(8,128)(2,1)}) fusion(bf16[2,16,2,32,256]{4,3,2,1,0:T(8,128)(2,1)S(1)} %collective-permute-done.27, bf16[2,4,16,2,32,256]{5,4,3,2,1,0:T(8,128)(2,1)S(1)} %collective-permute-done.20, bf16[2,4,16,2,32,256]{5,4,3,2,1,0:T(8,128)(2,1)} %get-tuple-element.44, ...), kind=kLoop, calls=%fused_computation.20 | loop fusion | flops 3145728 | bytes 4194304 | tf_op jit(solution)/shard_map/convert_element_type | solution.py:215
  211.9 17.2 %collective-permute-done.29 = bf16[2,16,2,32,256]{4,3,2,1,0:T(8,128)(2,1)S(1)} collective-permute-done((bf16[2,16,2,32,256]{4,3,2,1,0:T(8,128)(2,1)S(1)}, bf16[2,16,2,32,256]{4,3,2,1,0:T(8,128)(2,1)S(1)}, u32[]{:S(2)}, u32[]{:S(2)}) %collective-permute-start.29) | collective-permute-done | bytes 1048608 | tf_op jit(solution)/shard_map/ppermute | solution.py:190
  230.3 1.6 collective-permute-start.30
  232.4 7.2 %collective-permute-done.22 = bf16[1,16,2,32,256]{4,3,2,1,0:T(8,128)(2,1)} collective-permute-done((bf16[1,16,2,32,256]{4,3,2,1,0:T(8,128)(2,1)}, bf16[1,16,2,32,256]{4,3,2,1,0:T(8,128)(2,1)}, u32[]{:S(2)}, u32[]{:S(2)}) %collective-permute-start.22) | collective-permute-done | bytes 524320 | tf_op jit(solution)/shard_map/ppermute | solution.py:190
  239.7 1.9 fusion.15
  241.6 4.0 %collective-permute-done.30 = bf16[1,16,2,32,256]{4,3,2,1,0:T(8,128)(2,1)} collective-permute-done((bf16[1,16,2,32,256]{4,3,2,1,0:T(8,128)(2,1)}, bf16[1,16,2,32,256]{4,3,2,1,0:T(8,128)(2,1)}, u32[]{:S(2)}, u32[]{:S(2)}) %collective-permute-start.30) | collective-permute-done | bytes 524320 | tf_op jit(solution)/shard_map/ppermute | solution.py:190
  245.6 2.7 %fusion.17 = (bf16[16,2,32,256]{3,2,1,0:T(8,128)(2,1)S(1)}, bf16[1,16,2,32,256]{4,3,2,1,0:T(8,128)(2,1)S(1)}) fusion(bf16[1,16,2,32,256]{4,3,2,1,0:T(8,128)(2,1)} %collective-permute-done.30, bf16[2,16,2,32,256]{4,3,2,1,0:T(8,128)(2,1)} %copy-done.8, bf16[2,4,16,2,32,256]{5,4,3,2,1,0:T(8,128)(2,1)} %copy-done.2, ...), kind=kLoop, calls=%fused_computation.43 | loop fusion | flops 3670016 | bytes 4718592 | tf_op jit(solution)/shard_map/convert_element_type | solution.py:288
  248.3 1.4 collective-permute-start.31
  249.8 1.6 collective-permute-start.25
  251.7 1.9 bitcast_select_fusion.1
  253.7 1.6 pad_maximum_fusion.3
  255.2 3.8 %collective-permute-done.25 = bf16[1,16,2,32,256]{4,3,2,1,0:T(8,128)(2,1)S(1)} collective-permute-done((bf16[1,16,2,32,256]{4,3,2,1,0:T(8,128)(2,1)S(1)}, bf16[1,16,2,32,256]{4,3,2,1,0:T(8,128)(2,1)S(1)}, u32[]{:S(2)}, u32[]{:S(2)}) %collective-permute-start.25) | collective-permute-done | bytes 524320 | tf_op jit(solution)/shard_map/ppermute | solution.py:190
  259.0 1.7 fusion.16
  262.0 1.6 pad_maximum_fusion.2
  263.6 2.6 fusion.7
  266.2 6.5 %collective-permute-done.26 = bf16[16,2,32,256]{3,2,1,0:T(8,128)(2,1)S(1)} collective-permute-done((bf16[16,2,32,256]{3,2,1,0:T(8,128)(2,1)S(1)}, bf16[16,2,32,256]{3,2,1,0:T(8,128)(2,1)S(1)}, u32[]{:S(2)}, u32[]{:S(2)}) %collective-permute-start.26) | collective-permute-done | bytes 524320 | tf_op jit(solution)/shard_map/ppermute | solution.py:288
  (89 shorter events, 27.1 us)
Async XLA Ops:
  2.5 17.9 %collective-permute-start.1 = (bf16[1024,256]{1,0:T(8,128)(2,1)}, bf16[1024,256]{1,0:T(8,128)(2,1)S(1)}, u32[]{:S(2)}, u32[]{:S(2)}) collective-permute-start(bf16[1024,256]{1,0:T(8,128)(2,1)} %constant_dynamic-slice_fusion.1), channel_id=1, source_target_pairs={{2,0},{1,3},{6,4},{5,7},{10,8},{9,11},{14,12},{13,15},{18,16},{17,... | collective-permute-start | bytes 1572872 | tf_op jit(solution)/shard_map/ppermute | solution.py:250
  8.9 22.0 %collective-permute-start.9 = (bf16[1024,256]{1,0:T(8,128)(2,1)}, bf16[1024,256]{1,0:T(8,128)(2,1)S(1)}, u32[]{:S(2)}, u32[]{:S(2)}) collective-permute-start(bf16[1024,256]{1,0:T(8,128)(2,1)} %constant_dynamic-slice_fusion), channel_id=1, source_target_pairs={{2,0},{1,3},{6,4},{5,7},{10,8},{9,11},{14,12},{13,15},{18,16},{17,... | collective-permute-start | bytes 1572872 | tf_op jit(solution)/shard_map/ppermute | solution.py:250
  13.0 7.1 %copy-start.12 = (s32[2,8,8]{2,1,0:T(8,128)S(1)}, s32[2,8,8]{2,1,0:T(8,128)}, u32[]{:S(2)}) copy-start(s32[2,8,8]{2,1,0:T(8,128)} %param.8) | copy-start | bytes 1540
  13.0 7.2 %copy-start.13 = (s32[2,8,8]{2,1,0:T(8,128)S(1)}, s32[2,8,8]{2,1,0:T(8,128)}, u32[]{:S(2)}) copy-start(s32[2,8,8]{2,1,0:T(8,128)} %param.9) | copy-start | bytes 1540
  14.5 61.3 %collective-permute-start = (bf16[2,256,2048]{2,1,0:T(8,128)(2,1)}, bf16[2,256,2048]{2,1,0:T(8,128)(2,1)S(1)}, u32[]{:S(2)}, u32[]{:S(2)}) collective-permute-start(bf16[2,256,2048]{2,1,0:T(8,128)(2,1)} %pad_maximum_fusion), channel_id=1, source_target_pairs={{2,0},{1,3},{6,4},{5,7},{10,8},{9,11},{14,12},{13,15},{18,16},{17,... | collective-permute-start | bytes 6291464 | tf_op jit(solution)/shard_map/ppermute | solution.py:256
  17.4 102.2 %collective-permute-start.17 = (bf16[2,256,2048]{2,1,0:T(8,128)(2,1)}, bf16[2,256,2048]{2,1,0:T(8,128)(2,1)}, u32[]{:S(2)}, u32[]{:S(2)}) collective-permute-start(bf16[2,256,2048]{2,1,0:T(8,128)(2,1)} %pad_maximum_fusion.1), channel_id=1, source_target_pairs={{2,0},{1,3},{6,4},{5,7},{10,8},{9,11},{14,12},{13,15},{18,16},{17,... | collective-permute-start | bytes 6291464 | tf_op jit(solution)/shard_map/ppermute | solution.py:256
  20.4 18.2 %collective-permute-start.2 = (bf16[1024,256]{1,0:T(8,128)(2,1)S(1)}, bf16[1024,256]{1,0:T(8,128)(2,1)}, u32[]{:S(2)}, u32[]{:S(2)}) collective-permute-start(bf16[1024,256]{1,0:T(8,128)(2,1)S(1)} %collective-permute-done.1), channel_id=1, source_target_pairs={{0,8},{8,0},{16,24},{24,16},{1,9},{9,1},{17,25},{25,17},{2,10},{10... | collective-permute-start | bytes 1572872 | tf_op jit(solution)/shard_map/ppermute | solution.py:190
  22.6 26.7 %collective-permute-start.3 = (bf16[1024,256]{1,0:T(8,128)(2,1)S(1)}, bf16[1024,256]{1,0:T(8,128)(2,1)S(1)}, u32[]{:S(2)}, u32[]{:S(2)}) collective-permute-start(bf16[1024,256]{1,0:T(8,128)(2,1)S(1)} %collective-permute-done.1), channel_id=1, source_target_pairs={{0,16},{8,24},{16,0},{24,8},{1,17},{9,25},{17,1},{25,9},{2,18},{10... | collective-permute-start | bytes 1572872 | tf_op jit(solution)/shard_map/ppermute | solution.py:190
  30.9 16.1 %collective-permute-start.10 = (bf16[1024,256]{1,0:T(8,128)(2,1)S(1)}, bf16[1024,256]{1,0:T(8,128)(2,1)S(1)}, u32[]{:S(2)}, u32[]{:S(2)}) collective-permute-start(bf16[1024,256]{1,0:T(8,128)(2,1)S(1)} %collective-permute-done.9), channel_id=1, source_target_pairs={{0,16},{8,24},{16,0},{24,8},{1,17},{9,25},{17,1},{25,9},{2,18},{10... | collective-permute-start | bytes 1572872 | tf_op jit(solution)/shard_map/ppermute | solution.py:190
  38.6 12.1 %collective-permute-start.11 = (bf16[1024,256]{1,0:T(8,128)(2,1)S(1)}, bf16[1024,256]{1,0:T(8,128)(2,1)S(1)}, u32[]{:S(2)}, u32[]{:S(2)}) collective-permute-start(bf16[1024,256]{1,0:T(8,128)(2,1)S(1)} %collective-permute-done.9), channel_id=1, source_target_pairs={{0,8},{8,0},{16,24},{24,16},{1,9},{9,1},{17,25},{25,17},{2,10},{10... | collective-permute-start | bytes 1572872 | tf_op jit(solution)/shard_map/ppermute | solution.py:190
  47.0 12.4 %collective-permute-start.4 = (bf16[1024,256]{1,0:T(8,128)(2,1)}, bf16[1024,256]{1,0:T(8,128)(2,1)S(1)}, u32[]{:S(2)}, u32[]{:S(2)}) collective-permute-start(bf16[1024,256]{1,0:T(8,128)(2,1)} %collective-permute-done.2), channel_id=1, source_target_pairs={{0,16},{8,24},{16,0},{24,8},{1,17},{9,25},{17,1},{25,9},{2,18},{10... | collective-permute-start | bytes 1572872 | tf_op jit(solution)/shard_map/ppermute | solution.py:190
  49.4 11.9 %collective-permute-start.12 = (bf16[1024,256]{1,0:T(8,128)(2,1)S(1)}, bf16[1024,256]{1,0:T(8,128)(2,1)S(1)}, u32[]{:S(2)}, u32[]{:S(2)}) collective-permute-start(bf16[1024,256]{1,0:T(8,128)(2,1)S(1)} %collective-permute-done.10), channel_id=1, source_target_pairs={{0,8},{8,0},{16,24},{24,16},{1,9},{9,1},{17,25},{25,17},{2,10},{10... | collective-permute-start | bytes 1572872 | tf_op jit(solution)/shard_map/ppermute | solution.py:190
  50.7 11.4 %collective-permute-start.5 = (bf16[1024,256]{1,0:T(8,128)(2,1)S(1)}, bf16[1024,256]{1,0:T(8,128)(2,1)S(1)}, u32[]{:S(2)}, u32[]{:S(2)}) collective-permute-start(bf16[1024,256]{1,0:T(8,128)(2,1)S(1)} %collective-permute-done.1), channel_id=1, source_target_pairs={{0,4},{4,0},{1,5},{5,1},{2,6},{6,2},{3,7},{7,3},{8,12},{12,8},{9,1... | collective-permute-start | bytes 1572872 | tf_op jit(solution)/shard_map/ppermute | solution.py:190
  59.4 4.0 %collective-permute-start.13 = (bf16[1024,256]{1,0:T(8,128)(2,1)S(1)}, bf16[1024,256]{1,0:T(8,128)(2,1)S(1)}, u32[]{:S(2)}, u32[]{:S(2)}) collective-permute-start(bf16[1024,256]{1,0:T(8,128)(2,1)S(1)} %collective-permute-done.9), channel_id=1, source_target_pairs={{0,4},{4,0},{1,5},{5,1},{2,6},{6,2},{3,7},{7,3},{8,12},{12,8},{9,1... | collective-permute-start | bytes 1572872 | tf_op jit(solution)/shard_map/ppermute | solution.py:190
  61.2 3.0 %collective-permute-start.6 = (bf16[1024,256]{1,0:T(8,128)(2,1)}, bf16[1024,256]{1,0:T(8,128)(2,1)S(1)}, u32[]{:S(2)}, u32[]{:S(2)}) collective-permute-start(bf16[1024,256]{1,0:T(8,128)(2,1)} %collective-permute-done.2), channel_id=1, source_target_pairs={{0,4},{4,0},{1,5},{5,1},{2,6},{6,2},{3,7},{7,3},{8,12},{12,8},{9,1... | collective-permute-start | bytes 1572872 | tf_op jit(solution)/shard_map/ppermute | solution.py:190
  62.1 3.5 %collective-permute-start.7 = (bf16[1024,256]{1,0:T(8,128)(2,1)S(1)}, bf16[1024,256]{1,0:T(8,128)(2,1)S(1)}, u32[]{:S(2)}, u32[]{:S(2)}) collective-permute-start(bf16[1024,256]{1,0:T(8,128)(2,1)S(1)} %collective-permute-done.3), channel_id=1, source_target_pairs={{0,4},{4,0},{1,5},{5,1},{2,6},{6,2},{3,7},{7,3},{8,12},{12,8},{9,1... | collective-permute-start | bytes 1572872 | tf_op jit(solution)/shard_map/ppermute | solution.py:190
  63.4 3.1 %collective-permute-start.14 = (bf16[1024,256]{1,0:T(8,128)(2,1)S(1)}, bf16[1024,256]{1,0:T(8,128)(2,1)S(1)}, u32[]{:S(2)}, u32[]{:S(2)}) collective-permute-start(bf16[1024,256]{1,0:T(8,128)(2,1)S(1)} %collective-permute-done.10), channel_id=1, source_target_pairs={{0,4},{4,0},{1,5},{5,1},{2,6},{6,2},{3,7},{7,3},{8,12},{12,8},{9,1... | collective-permute-start | bytes 1572872 | tf_op jit(solution)/shard_map/ppermute | solution.py:190
  64.3 3.5 %collective-permute-start.15 = (bf16[1024,256]{1,0:T(8,128)(2,1)S(1)}, bf16[1024,256]{1,0:T(8,128)(2,1)S(1)}, u32[]{:S(2)}, u32[]{:S(2)}) collective-permute-start(bf16[1024,256]{1,0:T(8,128)(2,1)S(1)} %collective-permute-done.11), channel_id=1, source_target_pairs={{0,4},{4,0},{1,5},{5,1},{2,6},{6,2},{3,7},{7,3},{8,12},{12,8},{9,1... | collective-permute-start | bytes 1572872 | tf_op jit(solution)/shard_map/ppermute | solution.py:190
  65.6 3.0 %collective-permute-start.8 = (bf16[1024,256]{1,0:T(8,128)(2,1)S(1)}, bf16[1024,256]{1,0:T(8,128)(2,1)S(1)}, u32[]{:S(2)}, u32[]{:S(2)}) collective-permute-start(bf16[1024,256]{1,0:T(8,128)(2,1)S(1)} %collective-permute-done.4), channel_id=1, source_target_pairs={{0,4},{4,0},{1,5},{5,1},{2,6},{6,2},{3,7},{7,3},{8,12},{12,8},{9,1... | collective-permute-start | bytes 1572872 | tf_op jit(solution)/shard_map/ppermute | solution.py:190
  66.5 3.0 %collective-permute-start.16 = (bf16[1024,256]{1,0:T(8,128)(2,1)S(1)}, bf16[1024,256]{1,0:T(8,128)(2,1)S(1)}, u32[]{:S(2)}, u32[]{:S(2)}) collective-permute-start(bf16[1024,256]{1,0:T(8,128)(2,1)S(1)} %collective-permute-done.12), channel_id=1, source_target_pairs={{0,4},{4,0},{1,5},{5,1},{2,6},{6,2},{3,7},{7,3},{8,12},{12,8},{9,1... | collective-permute-start | bytes 1572872 | tf_op jit(solution)/shard_map/ppermute | solution.py:190
  75.8 1.3 copy-start
  119.6 49.6 %collective-permute-start.18 = (bf16[2,256,2048]{2,1,0:T(8,128)(2,1)}, bf16[2,256,2048]{2,1,0:T(8,128)(2,1)S(1)}, u32[]{:S(2)}, u32[]{:S(2)}) collective-permute-start(bf16[2,256,2048]{2,1,0:T(8,128)(2,1)} %get-tuple-element.31), channel_id=1, source_target_pairs={{0,2},{3,1},{4,6},{7,5},{8,10},{11,9},{12,14},{15,13},{16,18},{19,... | collective-permute-start | bytes 6291464 | tf_op jit(solution)/shard_map/ppermute | solution.py:279
  158.2 26.8 %copy-start.1 = (bf16[2,4,16,2,32,256]{5,4,3,2,1,0:T(8,128)(2,1)S(1)}, bf16[2,4,16,2,32,256]{5,4,3,2,1,0:T(8,128)(2,1)}, u32[]{:S(2)}) copy-start(bf16[2,4,16,2,32,256]{5,4,3,2,1,0:T(8,128)(2,1)} %get-tuple-element.52) | copy-start | bytes 12582916
  169.2 7.4 %collective-permute-start.20 = (bf16[2,4,16,2,32,256]{5,4,3,2,1,0:T(8,128)(2,1)}, bf16[2,4,16,2,32,256]{5,4,3,2,1,0:T(8,128)(2,1)S(1)}, u32[]{:S(2)}, u32[]{:S(2)}) collective-permute-start(bf16[2,4,16,2,32,256]{5,4,3,2,1,0:T(8,128)(2,1)} %get-tuple-element.45), channel_id=1, source_target_pairs={{0,4},{4,0},{1,5},{5,1},{2,6},{6,2},{3,7},{7,3},{8,12},{12,8},{9,1... | collective-permute-start | bytes 12582920 | tf_op jit(solution)/shard_map/ppermute | solution.py:190
  169.2 15.7 %collective-permute-start.23 = (bf16[2,4,16,2,32,256]{5,4,3,2,1,0:T(8,128)(2,1)}, bf16[2,4,16,2,32,256]{5,4,3,2,1,0:T(8,128)(2,1)S(1)}, u32[]{:S(2)}, u32[]{:S(2)}) collective-permute-start(bf16[2,4,16,2,32,256]{5,4,3,2,1,0:T(8,128)(2,1)} %get-tuple-element.53), channel_id=1, source_target_pairs={{0,4},{4,0},{1,5},{5,1},{2,6},{6,2},{3,7},{7,3},{8,12},{12,8},{9,1... | collective-permute-start | bytes 12582920 | tf_op jit(solution)/shard_map/ppermute | solution.py:190
  176.6 31.6 %copy-start.3 = (bf16[2,4,16,2,32,256]{5,4,3,2,1,0:T(8,128)(2,1)}, bf16[2,4,16,2,32,256]{5,4,3,2,1,0:T(8,128)(2,1)S(1)}, u32[]{:S(2)}) copy-start(bf16[2,4,16,2,32,256]{5,4,3,2,1,0:T(8,128)(2,1)S(1)} %collective-permute-done.20) | copy-start | bytes 12582916
  180.6 26.1 %collective-permute-start.27 = (bf16[2,16,2,32,256]{4,3,2,1,0:T(8,128)(2,1)S(1)}, bf16[2,16,2,32,256]{4,3,2,1,0:T(8,128)(2,1)S(1)}, u32[]{:S(2)}, u32[]{:S(2)}) collective-permute-start(bf16[2,16,2,32,256]{4,3,2,1,0:T(8,128)(2,1)S(1)} %get-tuple-element.56), channel_id=1, source_target_pairs={{0,16},{8,24},{16,0},{24,8},{1,17},{9,25},{17,1},{25,9},{2,18},{10... | collective-permute-start | bytes 3145736 | tf_op jit(solution)/shard_map/ppermute | solution.py:190
  182.2 26.0 %collective-permute-start.21 = (bf16[2,16,2,32,256]{4,3,2,1,0:T(8,128)(2,1)S(1)}, bf16[2,16,2,32,256]{4,3,2,1,0:T(8,128)(2,1)S(1)}, u32[]{:S(2)}, u32[]{:S(2)}) collective-permute-start(bf16[2,16,2,32,256]{4,3,2,1,0:T(8,128)(2,1)S(1)} %get-tuple-element.57), channel_id=1, source_target_pairs={{0,8},{8,0},{16,24},{24,16},{1,9},{9,1},{17,25},{25,17},{2,10},{10... | collective-permute-start | bytes 3145736 | tf_op jit(solution)/shard_map/ppermute | solution.py:190
  183.7 57.9 %collective-permute-start.19 = (bf16[2,256,2048]{2,1,0:T(8,128)(2,1)}, bf16[2,256,2048]{2,1,0:T(8,128)(2,1)}, u32[]{:S(2)}, u32[]{:S(2)}) collective-permute-start(bf16[2,256,2048]{2,1,0:T(8,128)(2,1)} %get-tuple-element.43), channel_id=1, source_target_pairs={{0,2},{3,1},{4,6},{7,5},{8,10},{11,9},{12,14},{15,13},{16,18},{19,... | collective-permute-start | bytes 6291464 | tf_op jit(solution)/shard_map/ppermute | solution.py:281
  185.0 44.2 %copy-start.2 = (bf16[2,4,16,2,32,256]{5,4,3,2,1,0:T(8,128)(2,1)}, bf16[2,4,16,2,32,256]{5,4,3,2,1,0:T(8,128)(2,1)S(1)}, u32[]{:S(2)}) copy-start(bf16[2,4,16,2,32,256]{5,4,3,2,1,0:T(8,128)(2,1)S(1)} %collective-permute-done.23) | copy-start | bytes 12582916
  187.3 41.8 %collective-permute-start.29 = (bf16[2,16,2,32,256]{4,3,2,1,0:T(8,128)(2,1)S(1)}, bf16[2,16,2,32,256]{4,3,2,1,0:T(8,128)(2,1)S(1)}, u32[]{:S(2)}, u32[]{:S(2)}) collective-permute-start(bf16[2,16,2,32,256]{4,3,2,1,0:T(8,128)(2,1)S(1)} %get-tuple-element.60), channel_id=1, source_target_pairs={{0,16},{8,24},{16,0},{24,8},{1,17},{9,25},{17,1},{25,9},{2,18},{10... | collective-permute-start | bytes 3145736 | tf_op jit(solution)/shard_map/ppermute | solution.py:190
  187.8 53.7 %collective-permute-start.24 = (bf16[2,16,2,32,256]{4,3,2,1,0:T(8,128)(2,1)}, bf16[2,16,2,32,256]{4,3,2,1,0:T(8,128)(2,1)}, u32[]{:S(2)}, u32[]{:S(2)}) collective-permute-start(bf16[2,16,2,32,256]{4,3,2,1,0:T(8,128)(2,1)} %get-tuple-element.61), channel_id=1, source_target_pairs={{0,8},{8,0},{16,24},{24,16},{1,9},{9,1},{17,25},{25,17},{2,10},{10... | collective-permute-start | bytes 3145736 | tf_op jit(solution)/shard_map/ppermute | solution.py:190
  206.7 23.7 %copy-start.9 = (bf16[2,16,2,32,256]{4,3,2,1,0:T(8,128)(2,1)}, bf16[2,16,2,32,256]{4,3,2,1,0:T(8,128)(2,1)S(1)}, u32[]{:S(2)}) copy-start(bf16[2,16,2,32,256]{4,3,2,1,0:T(8,128)(2,1)S(1)} %collective-permute-done.27) | copy-start | bytes 3145732
  208.2 22.1 %copy-start.11 = (bf16[2,16,2,32,256]{4,3,2,1,0:T(8,128)(2,1)}, bf16[2,16,2,32,256]{4,3,2,1,0:T(8,128)(2,1)S(1)}, u32[]{:S(2)}) copy-start(bf16[2,16,2,32,256]{4,3,2,1,0:T(8,128)(2,1)S(1)} %collective-permute-done.21) | copy-start | bytes 3145732
  211.4 28.3 %collective-permute-start.22 = (bf16[1,16,2,32,256]{4,3,2,1,0:T(8,128)(2,1)}, bf16[1,16,2,32,256]{4,3,2,1,0:T(8,128)(2,1)}, u32[]{:S(2)}, u32[]{:S(2)}) collective-permute-start(bf16[1,16,2,32,256]{4,3,2,1,0:T(8,128)(2,1)} %get-tuple-element.55), channel_id=1, source_target_pairs={{0,16},{8,24},{16,0},{24,8},{1,17},{9,25},{17,1},{25,9},{2,18},{10... | collective-permute-start | bytes 1572872 | tf_op jit(solution)/shard_map/ppermute | solution.py:190
  229.1 1.2 copy-start.8
  230.3 21.0 %copy-start.4 = (bf16[256,2048]{1,0:T(8,128)(2,1)S(1)}, bf16[256,2048]{1,0:T(8,128)(2,1)}, u32[]{:S(2)}) copy-start(bf16[256,2048]{1,0:T(8,128)(2,1)} %get-tuple-element.29) | copy-start | bytes 3145732
  230.3 15.2 %collective-permute-start.30 = (bf16[1,16,2,32,256]{4,3,2,1,0:T(8,128)(2,1)}, bf16[1,16,2,32,256]{4,3,2,1,0:T(8,128)(2,1)}, u32[]{:S(2)}, u32[]{:S(2)}) collective-permute-start(bf16[1,16,2,32,256]{4,3,2,1,0:T(8,128)(2,1)} %fusion.4), channel_id=1, source_target_pairs={{0,8},{8,0},{16,24},{24,16},{1,9},{9,1},{17,25},{25,17},{2,10},{10... | collective-permute-start | bytes 1572872 | tf_op jit(solution)/shard_map/ppermute | solution.py:190
  231.9 19.5 %copy-start.5 = (bf16[256,2048]{1,0:T(8,128)(2,1)S(1)}, bf16[256,2048]{1,0:T(8,128)(2,1)}, u32[]{:S(2)}) copy-start(bf16[256,2048]{1,0:T(8,128)(2,1)} %get-tuple-element.49) | copy-start | bytes 3145732
  231.9 31.7 %collective-permute-start.28 = (bf16[1,16,2,32,256]{4,3,2,1,0:T(8,128)(2,1)}, bf16[1,16,2,32,256]{4,3,2,1,0:T(8,128)(2,1)S(1)}, u32[]{:S(2)}, u32[]{:S(2)}) collective-permute-start(bf16[1,16,2,32,256]{4,3,2,1,0:T(8,128)(2,1)} %get-tuple-element.54), channel_id=1, source_target_pairs={{0,8},{8,0},{16,24},{24,16},{1,9},{9,1},{17,25},{25,17},{2,10},{10... | collective-permute-start | bytes 1572872 | tf_op jit(solution)/shard_map/ppermute | solution.py:190
  248.3 3.4 %copy-start.6 = (bf16[256,2048]{1,0:T(8,128)(2,1)S(1)}, bf16[256,2048]{1,0:T(8,128)(2,1)}, u32[]{:S(2)}) copy-start(bf16[256,2048]{1,0:T(8,128)(2,1)} %get-tuple-element.47) | copy-start | bytes 3145732
  248.3 3.4 %copy-start.7 = (bf16[256,2048]{1,0:T(8,128)(2,1)S(1)}, bf16[256,2048]{1,0:T(8,128)(2,1)}, u32[]{:S(2)}) copy-start(bf16[256,2048]{1,0:T(8,128)(2,1)} %get-tuple-element.50) | copy-start | bytes 3145732
  248.3 15.3 %collective-permute-start.31 = (bf16[16,2,32,256]{3,2,1,0:T(8,128)(2,1)S(1)}, bf16[16,2,32,256]{3,2,1,0:T(8,128)(2,1)S(1)}, u32[]{:S(2)}, u32[]{:S(2)}) collective-permute-start(bf16[16,2,32,256]{3,2,1,0:T(8,128)(2,1)S(1)} %get-tuple-element.58), channel_id=1, source_target_pairs={{0,2},{3,1},{4,6},{7,5},{8,10},{11,9},{12,14},{15,13},{16,18},{19,... | collective-permute-start | bytes 1572872 | tf_op jit(solution)/shard_map/ppermute | solution.py:288
  249.8 9.2 %collective-permute-start.25 = (bf16[1,16,2,32,256]{4,3,2,1,0:T(8,128)(2,1)S(1)}, bf16[1,16,2,32,256]{4,3,2,1,0:T(8,128)(2,1)S(1)}, u32[]{:S(2)}, u32[]{:S(2)}) collective-permute-start(bf16[1,16,2,32,256]{4,3,2,1,0:T(8,128)(2,1)S(1)} %get-tuple-element.59), channel_id=1, source_target_pairs={{0,16},{8,24},{16,0},{24,8},{1,17},{9,25},{17,1},{25,9},{2,18},{10... | collective-permute-start | bytes 1572872 | tf_op jit(solution)/shard_map/ppermute | solution.py:190
  255.2 8.4 %copy-start.10 = (bf16[2,16,2,32,256]{4,3,2,1,0:T(8,128)(2,1)S(1)}, bf16[2,16,2,32,256]{4,3,2,1,0:T(8,128)(2,1)}, u32[]{:S(2)}) copy-start(bf16[2,16,2,32,256]{4,3,2,1,0:T(8,128)(2,1)} %copy-done.9) | copy-start | bytes 3145732
  260.7 12.0 %collective-permute-start.26 = (bf16[16,2,32,256]{3,2,1,0:T(8,128)(2,1)S(1)}, bf16[16,2,32,256]{3,2,1,0:T(8,128)(2,1)S(1)}, u32[]{:S(2)}, u32[]{:S(2)}) collective-permute-start(bf16[16,2,32,256]{3,2,1,0:T(8,128)(2,1)S(1)} %fusion.16), channel_id=1, source_target_pairs={{0,2},{3,1},{4,6},{7,5},{8,10},{11,9},{12,14},{15,13},{16,18},{19,... | collective-permute-start | bytes 1572872 | tf_op jit(solution)/shard_map/ppermute | solution.py:288

commit v3 on v2

v3 whole, which is shorter than its diff:
```python
import functools
import math

import jax
import jax.numpy as jnp
from jax import lax
from jax.experimental import pallas as pl
from jax.experimental.pallas import tpu as pltpu
from jax.sharding import PartitionSpec as P

F32 = jnp.float32
BF16 = jnp.bfloat16
ROOT = math.sqrt(2.0 / math.pi)
CUBIC = 0.044715


def dot(a, b, over):
    return lax.dot_general(a, b, ((over[:1], over[1:]), ((), ())), preferred_element_type=F32)


def activate(pre, d_hidden):
    square = pre * pre
    tanh = jnp.tanh(pre * (ROOT + (ROOT * CUBIC) * square))
    cdf = 0.5 + 0.5 * tanh
    slope = cdf + pre * (0.5 - 0.5 * tanh * tanh) * (ROOT + (3.0 * ROOT * CUBIC) * square)
    return (pre * cdf).astype(BF16), (d_hidden * slope).astype(BF16)


def layer_kernel(last, slots, ids, *refs):
    refs = list(refs)
    take = lambda count: [refs.pop(0) for _ in range(count)]
    chunks = 2 if last else 1
    nears, fars = take(chunks), take(chunks)
    near, far = nears[-1], fars[-1]
    up, down = take(2)
    if last:
        hidden_kept, d_pre_kept, _ = take(3)
    (near_out,) = take(1)
    far_out = take(1 if last else 2)
    if last:
        sums = take(4)
    else:
        hidden_kept, d_pre_kept = take(2)
    out_acc, back_acc = take(2)
    if last:
        up_sum, down_sum = take(2)
    step = pl.program_id(0)
    steps = pl.num_programs(0)
    each, _, size, _ = up.shape

    @pl.when(step == 0)
    def _():
        out_acc[...] = jnp.zeros_like(out_acc)
        back_acc[...] = jnp.zeros_like(back_acc)

    theirs = step < steps // 2
    meets = theirs.astype(jnp.int32)

    def columns(block):
        return pl.ds(pl.multiple_of(block * size, size), size)

    def both(k, at, chunk=-1):
        return jnp.concatenate([nears[chunk][k, :, at[0]], fars[chunk][k, :, at[1]]], axis=1)

    def tall(first, second):
        return jnp.concatenate([first, second], axis=0)

    work = []
    for e in range(each):
        ins = [columns(ids[k, step * each + e]) for k in (0, 1)]
        outs = [columns(ids[k, step * each + e]) for k in (2, 3)]
        x_cat, g_cat = both(0, ins), both(1, outs)
        up_cat = jnp.concatenate([up[e, meets], up[e, 1 - meets]], axis=0)
        down_cat = jnp.concatenate([down[e, meets], down[e, 1 - meets]], axis=1)
        pre = dot(x_cat, up_cat, (1, 0))
        d_hidden = dot(g_cat, down_cat, (1, 1))
        work.append((ins, outs, x_cat, g_cat, up_cat, down_cat, pre, d_hidden))
    done = []
    for e, (ins, outs, x_cat, g_cat, up_cat, down_cat, pre, d_hidden) in enumerate(work):
        hidden, d_pre = activate(pre, d_hidden)
        done.append((dot(hidden, down_cat, (1, 0)), dot(d_pre, up_cat, (1, 1))))
        if last:
            up_sum[e] = dot(tall(both(0, ins, 0), x_cat), tall(d_pre_kept[e], d_pre), (0, 0))
            down_sum[e] = dot(tall(hidden_kept[e], hidden), tall(both(1, outs, 0), g_cat), (0, 0))
        else:
            hidden_kept[e] = hidden
            d_pre_kept[e] = d_pre
    for (ins, outs, *_), (out, back) in zip(work, done):
        for s in range(2):
            out_acc[s, :, outs[s]] += out[:, s * size : (s + 1) * size]
            back_acc[s, :, ins[s]] += back[:, s * size : (s + 1) * size]
    if last:
        me = ids[4, 0]
        shard = sums[0].shape[4]
        shards = size // shard

        def store(keep, send, flip):
            for e in range(each):
                for place in range(shards):
                    start = pl.multiple_of((place ^ me) * shard, shard)
                    to = send if place & 1 else keep
                    for s in range(2):
                        at = (1 - s if flip else s) * size
                        to[0, slots[0][place], e, s] = up_sum[
                            e, pl.ds(at + start, shard)
                        ].astype(BF16)
                        to[1, slots[1][place], e, s] = down_sum[
                            e, pl.ds(start, shard), at : at + size
                        ].astype(BF16)

        pl.when(theirs)(lambda: store(*sums[:2], True))
        pl.when(jnp.logical_not(theirs))(lambda: store(*sums[2:], False))

    @pl.when(step == steps - 1)
    def _():
        for k, acc in enumerate((out_acc, back_acc)):
            near_out[k] = acc[0].astype(BF16)
            row = 0
            for part in far_out:
                part[k] = acc[1, row : row + part.shape[1]].astype(BF16)
                row += part.shape[1]


def layer(slots, ids, nears, fars, weights, split=None, earlier=()):
    steps, _, size, _ = weights[0].shape
    hid = steps // 2
    _, count, width = nears[-1].shape
    shards = len(slots[0])
    last = split is None
    each = min(4, hid)
    turns = hid // each

    def whole(shape):
        return pl.BlockSpec(shape, lambda i, ids: (0,) * len(shape))

    def blocks(shape):
        return pl.BlockSpec((each, *shape[1:]), lambda i, ids: (i,) + (0,) * (len(shape) - 1))

    in_specs = [whole(part.shape) for part in (*nears, *fars)]
    in_specs += [blocks(weight.shape) for weight in weights]
    result = jax.ShapeDtypeStruct((2, count, width), BF16)
    out_shape = [result]
    out_specs = [whole(result.shape)]
    scratch = [pltpu.VMEM((2, count, width), F32)] * 2
    aliases = {}
    if last:
        in_specs += [blocks(part.shape) for part in earlier[:2]]
        in_specs += [pl.BlockSpec(memory_space=pl.ANY)]
        aliases = {len(in_specs): 1}
        out_shape.append(jax.ShapeDtypeStruct(earlier[2].shape, BF16))
        out_specs.append(whole(result.shape))
        shard = size // shards
        out_shape += [jax.ShapeDtypeStruct((2, shards // 2, hid, 2, shard, size), BF16)] * 4
        for part in range(2):
            out_specs += [
                pl.BlockSpec(
                    (2, shards // 2, each, 2, shard, size),
                    lambda i, ids, part=part: (
                        *(0, 0, jnp.clip(i - part * turns, 0, turns - 1)),
                        *(0, 0, 0),
                    ),
                )
            ] * 2
        scratch += [
            pltpu.VMEM((each, 2 * size, size), F32),
            pltpu.VMEM((each, size, 2 * size), F32),
        ]
    else:
        rest, behind = count - split[0], split[1]
        out_shape.append(jax.ShapeDtypeStruct((2, split[0], width), BF16))
        out_shape.append(jax.ShapeDtypeStruct((2, behind + rest, width), BF16))
        out_specs.append(whole((2, split[0], width)))
        out_specs.append(pl.BlockSpec((2, rest, width), lambda i, ids: (0, behind // rest, 0)))
        out_shape += [jax.ShapeDtypeStruct((steps, count, size), BF16)] * 2
        out_specs += [blocks(out_shape[-1].shape)] * 2
    return pl.pallas_call(
        functools.partial(layer_kernel, last, slots),
        out_shape=out_shape,
        grid_spec=pltpu.PrefetchScalarGridSpec(
            num_scalar_prefetch=1,
            grid=(2 * turns,),
            in_specs=in_specs,
            out_specs=out_specs,
            scratch_shapes=scratch,
        ),
        input_output_aliases=aliases,
        compiler_params=pltpu.CompilerParams(
            dimension_semantics=("arbitrary",), vmem_limit_bytes=60 << 20
        ),
        cost_estimate=pl.CostEstimate(flops=0, bytes_accessed=0, transcendentals=0),
    )(ids, *nears, *fars, *weights, *earlier)


def hop(block, bit):
    seq = lax.axis_size("seq")
    axis, bit = ("seq", bit) if bit < seq else ("dp", bit // seq)
    return lax.ppermute(block, axis, [(i, i ^ bit) for i in range(lax.axis_size(axis))])


def bits_of(count, unit=1):
    return [unit << k for k in range(count.bit_length() - 1)]


def gather(shard, order, me, weight):
    parts = {0: shard}
    for bit in order:
        for place in list(parts):
            parts[place | bit] = hop(parts[place], bit)
    ours = weight.reshape(-1, *shard.shape)
    table = jnp.concatenate([jnp.zeros_like(ours), ours])
    for place, part in parts.items():
        table = lax.dynamic_update_slice_in_dim(table, part[None], place ^ me, 0)
    return table.reshape(-1, *weight.shape[1:])


def total(terms):
    return sum(term.astype(F32) for term in terms)


def halve(terms, bit):
    half = terms[0].shape[0] // 2
    upper = total([term[half:] for term in terms]).astype(BF16)
    return [term[:half] for term in terms], upper, bit


def halved(terms, upper, bit):
    return [*terms, hop(upper, bit)]


def reduce_scatter(terms, order):
    for bit in order:
        terms = halved(*halve(terms, bit))
    return total(terms)[0]


def slots_of(order, shards):
    return [
        sum(1 << (len(order) - 1 - k) for k, bit in enumerate(order) if place & bit)
        for place in range(shards)
    ]


def after(value, *earlier):
    return lax.optimization_barrier((value, *earlier))[0]


def on_device(tokens, out_grad, up_perm, down_perm, up_weight, down_weight):
    tok_rows, width = tokens.shape
    hid, _, size, _ = up_weight.shape
    groups, group = lax.axis_size("tensor"), lax.axis_index("tensor")
    away = groups // 2
    dp, seq = lax.axis_size("dp"), lax.axis_size("seq")
    shards = dp * seq
    me = lax.axis_index("dp") * seq + lax.axis_index("seq")
    seq_bits, dp_bits = bits_of(seq), bits_of(dp, seq)
    back = [(p, p + away) if p % 2 == 0 else (p + away, p) for p in range(away)]
    into = [(other, worker) for worker, other in back]
    works = (group % away % 2 == 0) != (group >= away)
    partner = (group + away) % groups

    first, split = tok_rows // 2, 3 * tok_rows // 8
    lines = hid * 2 * size // shards

    def fetch(weight):
        shard = lax.dynamic_slice_in_dim(weight.reshape(-1, size), me * lines, lines, 0)
        return lax.ppermute(shard, "tensor", into)

    up_shard, down_shard = fetch(up_weight), fetch(down_weight)
    near = [
        jnp.stack([tokens[low:high], out_grad[low:high]])
        for low, high in ((0, first), (first, tok_rows))
    ]
    far = [lax.ppermute(near[0], "tensor", into)]
    far.append(lax.ppermute(near[1], "tensor", into))
    up = gather(up_shard, dp_bits + seq_bits, me, up_weight)
    down = gather(down_shard, dp_bits[::-1] + seq_bits, me, down_weight)
    weights = (up, down)

    def block_ids(perm):
        flat = perm.reshape(2, -1)
        theirs = lax.dynamic_slice_in_dim(flat, partner * hid, hid, 1)
        mine = lax.dynamic_slice_in_dim(flat, group * hid, hid, 1)
        return jnp.concatenate([theirs[::-1], mine], axis=1)

    ids = jnp.concatenate(
        [block_ids(up_perm), block_ids(down_perm), jnp.full((1, 2 * hid), me, jnp.int32)]
    )

    orders = [dp_bits + seq_bits[1:], dp_bits[::-1] + seq_bits[1:]]
    slots = [slots_of(order, shards) for order in orders]
    near_one, early, rest, *kept = layer(
        slots, ids, near[:1], far[:1], weights, (split, tok_rows - first)
    )
    early, far[1] = lax.optimization_barrier((early, far[1]))
    near_two, rest, *sums = layer(slots, ids, near, far, weights, earlier=(*kept, rest))
    early = lax.ppermute(early, "tensor", back)
    early, rest, near_two, sums = lax.optimization_barrier((early, rest, near_two, sums))
    rest = lax.ppermute(rest, "tensor", back)

    def terms_of(keep, send):
        come = hop(send, seq_bits[0])
        return [[keep[k], come[k]] for k in range(2)]

    theirs, mine = terms_of(*sums[:2]), terms_of(*sums[2:])
    theirs = [halved(*halve(theirs[k], orders[k][0])) for k in range(2)]
    mine = [halve(mine[k], orders[k][0]) for k in range(2)]
    uppers, theirs = lax.optimization_barrier(([upper for _, upper, _ in mine], theirs))
    mine = [halved(terms, upper, bit) for (terms, _, bit), upper in zip(mine, uppers)]
    theirs = [reduce_scatter(theirs[k], orders[k][1:]).astype(BF16) for k in range(2)]
    theirs, mine, rest = lax.optimization_barrier((theirs, mine, rest))
    theirs = [lax.ppermute(part, "tensor", back) for part in theirs]
    mine = [reduce_scatter(mine[k], orders[k][1:]) for k in range(2)]
    early, rest, mine[0] = lax.optimization_barrier((early, rest, mine[0]))

    def deliver(k):
        after = tok_rows - first
        ours = jnp.concatenate([near_one[k], near_two[k]])
        return jnp.where(works, ours, jnp.concatenate([early[k], rest[k, after:], rest[k, :after]]))

    scale = float(tok_rows * shards) ** (-0.5)
    grads = [jnp.where(works, m, t.astype(F32)) * scale for m, t in zip(mine, theirs)]
    return deliver(0), deliver(1), grads[0], grads[1]


def solution(mesh):
    in_specs = (
        P(("dp", "seq"), "tensor"),
        P(("dp", "seq"), "tensor"),
        P(),
        P(),
        P("tensor", None, None, None),
        P("tensor", None, None, None),
    )
    out_specs = (
        P(("dp", "seq"), "tensor"),
        P(("dp", "seq"), "tensor"),
        P("tensor", None, ("dp", "seq"), None),
        P("tensor", None, ("dp", "seq"), None),
    )
    return jax.shard_map(
        on_device, mesh=mesh, in_specs=in_specs, out_specs=out_specs, check_vma=False
    )
```

time: 275 us -> 263 us (0.956)
  other arithmetic: 29.8 us -> 16.1 us
  local copies, waits for them, and re-layouts: 27.3 us -> 39.5 us
  waiting for transfers between devices: 122 us -> 114 us
    ppermute x6, waiting for transfers between devices: 42.7 us -> 19.6 us  [the longest x2 9.56 us: on_device(): theirs = [lax.ppermute(part, 'tensor', back) for part in theirs]]
    concatenate x0 -> x2, local copies, waits for them, and re-layouts: none -> 12 us  [gather(): table = jnp.concatenate([jnp.zeros_like(ours), ours])]
    ppermute x24, waiting for transfers between devices: 72.8 us -> 83.6 us  [hop(): lax.ppermute(block, axis, [(i, i ^ bit) for i in range(lax.axis_size(axis...]
    convert_element_type x6 -> x8, other arithmetic: 15.1 us -> 6.96 us  [the longest x6 6.2 us: halve(): upper = total([term[half:] for term in terms]).astype(BF16)]
    another operation x3 -> x1, local copies, waits for them, and re-layouts: 7.33 us -> 2.75 us  [on_device(): jnp.stack([tokens[low:high], out_grad[low:high]])]
    slice x0 -> x4, local copies, waits for them, and re-layouts: none -> 4.05 us  [halve(): return ([term[:half] for term in terms], upper, bit)]
    ppermute x2, waiting for transfers between devices: 6.69 us -> 10.6 us  [fetch(): return lax.ppermute(shard, 'tensor', into)]
    concatenate x2 -> x0, other arithmetic: 3.14 us -> none  [deliver(): jnp.concatenate([jnp.where(works, part[k], come[k]) for part, come in zip...]
  transfers between devices with their start and end apart: 32 -> 32, of which waited for: 15 -> 14; matrix products, arithmetic and copies ran while one was open for 19% -> 20% of each run, Pallas kernels for 22% -> 22%
where the time goes in v3:
time: 263 us; the launch traced here: 262 us
  waiting for transfers between devices  114 us (43%)
  Pallas kernels  57.5 us (22%)
  local copies, waits for them, and re-layouts  39.5 us (15%)
  starting transfers between devices  34.1 us (13%)
  other arithmetic  16.1 us (6%)
    ppermute x24, waiting for transfers between devices, hop(): lax.ppermute(block, axis, [(i, i ^ bit) for i in range(lax.axis_size(axis...  83.6 us
    pallas_call x2, Pallas kernels, layer(): pl.pallas_call(functools.partial(layer_kernel, last, slots), out_shape=ou...  57.5 us
    ppermute x24, starting transfers between devices, hop(): lax.ppermute(block, axis, [(i, i ^ bit) for i in range(lax.axis_size(axis...  17.5 us
    dynamic_update_slice x16, local copies, waits for them, and re-layouts, gather(): table = lax.dynamic_update_slice_in_dim(table, part[None], place ^ me, 0)  14.4 us
    concatenate x2, local copies, waits for them, and re-layouts, gather(): table = jnp.concatenate([jnp.zeros_like(ours), ours])  12 us
    ppermute x2, waiting for transfers between devices, fetch(): return lax.ppermute(shard, 'tensor', into)  10.6 us
    ppermute x2, waiting for transfers between devices, on_device(): theirs = [lax.ppermute(part, 'tensor', back) for part in theirs]  9.56 us
    ppermute x1, waiting for transfers between devices, on_device(): far.append(lax.ppermute(near[1], 'tensor', into))  8.88 us
  transfers between devices with their start and end apart: 32, of which 14 were waited for; matrix products, arithmetic and copies ran while one was open for 20% of the time, Pallas kernels for 22%

profile of v3, /device:TPU:8, one launch (start us, length us, event | category | flops | bytes accessed | tf_op | source)
XLA Modules:
  0.0 261.9 jit_solution(7306051772250986746)
XLA Ops:
  0.6 1.9 constant_dynamic-slice_fusion.1
  2.5 4.5 %collective-permute-start.1 = (bf16[1024,256]{1,0:T(8,128)(2,1)}, bf16[1024,256]{1,0:T(8,128)(2,1)S(1)}, u32[]{:S(2)}, u32[]{:S(2)}) collective-permute-start(bf16[1024,256]{1,0:T(8,128)(2,1)} %constant_dynamic-slice_fusion.1), channel_id=1, source_target_pairs={{2,0},{1,3},{6,4},{5,7},{10,8},{9,11},{14,12},{13,15},{18,16},{17,... | collective-permute-start | bytes 1572872 | tf_op jit(solution)/shard_map/ppermute | solution.py:266
  7.0 1.9 constant_dynamic-slice_fusion
  8.9 1.3 collective-permute-start.9
  10.2 2.8 %slice_bitcast_fusion.13 = (bf16[1,256,2048]{2,1,0:T(8,128)(2,1)S(1)}, bf16[1,256,2048]{2,1,0:T(8,128)(2,1)S(1)}, bf16[1,256,2048]{2,1,0:T(8,128)(2,1)S(1)}, bf16[1,256,2048]{2,1,0:T(8,128)(2,1)S(1)}) fusion(bf16[512,2048]{1,0:T(8,128)(2,1)} %param.7, bf16[512,2048]{1,0:T(8,128)(2,1)} %param.6), kind=kLoop, calls=%fused_computation.35 | loop fusion | bytes 8388608 | tf_op jit(solution)/shard_map/stack | solution.py:270
  13.2 2.6 collective-permute-start
  15.8 1.5 pad_maximum_fusion.1.refs_1_
  17.3 2.6 collective-permute-start.17
  20.3 10.6 %collective-permute-done.9 = bf16[1024,256]{1,0:T(8,128)(2,1)S(1)} collective-permute-done((bf16[1024,256]{1,0:T(8,128)(2,1)}, bf16[1024,256]{1,0:T(8,128)(2,1)S(1)}, u32[]{:S(2)}, u32[]{:S(2)}) %collective-permute-start.9) | collective-permute-done | bytes 524320 | tf_op jit(solution)/shard_map/ppermute | solution.py:266
  30.9 1.5 collective-permute-start.10
  33.1 6.0 %concatenate.31 = bf16[16,1024,256]{2,1,0:T(8,128)(2,1)} pad(bf16[8,1024,256]{2,1,0:T(8,128)(2,1)} %bitcast.106, bf16[]{:T(256)} %constant.53.clone.1), padding=8_0x0_0x0_0 | pad | bytes 12582914 | tf_op jit(solution)/shard_map/concatenate | solution.py:210
  39.1 6.0 %concatenate.30 = bf16[16,1024,256]{2,1,0:T(8,128)(2,1)} pad(bf16[8,1024,256]{2,1,0:T(8,128)(2,1)} %bitcast.108, bf16[]{:T(256)} %constant.53.clone.1), padding=8_0x0_0x0_0 | pad | bytes 12582914 | tf_op jit(solution)/shard_map/concatenate | solution.py:210
  45.1 1.5 collective-permute-start.11
  49.3 1.9 bitcast_dynamic-update-slice_fusion.6
  51.1 17.1 %collective-permute-done.2 = bf16[1024,256]{1,0:T(8,128)(2,1)S(1)} collective-permute-done((bf16[1024,256]{1,0:T(8,128)(2,1)S(1)}, bf16[1024,256]{1,0:T(8,128)(2,1)S(1)}, u32[]{:S(2)}, u32[]{:S(2)}) %collective-permute-start.2) | collective-permute-done | bytes 524320 | tf_op jit(solution)/shard_map/ppermute | solution.py:197
  68.2 1.5 collective-permute-start.12
  72.7 6.2 %collective-permute-done.12 = bf16[1024,256]{1,0:T(8,128)(2,1)S(1)} collective-permute-done((bf16[1024,256]{1,0:T(8,128)(2,1)}, bf16[1024,256]{1,0:T(8,128)(2,1)S(1)}, u32[]{:S(2)}, u32[]{:S(2)}) %collective-permute-start.12) | collective-permute-done | bytes 524320 | tf_op jit(solution)/shard_map/ppermute | solution.py:197
  87.5 0.9 bitcast_dynamic-update-slice_fusion
  89.2 21.5 %shard_map.93 = (bf16[2,256,2048]{2,1,0:T(8,128)(2,1)}, bf16[2,192,2048]{2,1,0:T(8,128)(2,1)}, bf16[2,320,2048]{2,1,0:T(8,128)(2,1)}, bf16[32,256,256]{2,1,0:T(8,128)(2,1)}, bf16[32,256,256]{2,1,0:T(8,128)(2,1)}) custom-call(s32[5,32]{1,0:T(8,128)} %add_add_fusion.ids, bf16[2,256,2048]{2,1,0:T(8,128)(2,1)} %copy-done, ...), custom_call_target="tpu_custom_call" | custom-call | tf_op jit(solution)/shard_map/pallas_call | solution.py:176
  110.7 8.9 %collective-permute-done.17.refs_3_ = bf16[2,256,2048]{2,1,0:T(8,128)(2,1)} collective-permute-done((bf16[2,256,2048]{2,1,0:T(8,128)(2,1)}, bf16[2,256,2048]{2,1,0:T(8,128)(2,1)}, u32[]{:S(2)}, u32[]{:S(2)}) %collective-permute-start.17) | collective-permute-done | bytes 2097184 | tf_op jit(solution)/shard_map/ppermute | solution.py:274
  119.6 1.3 collective-permute-start.18
  120.9 36.0 %shard_map.94 = (bf16[2,256,2048]{2,1,0:T(8,128)(2,1)}, bf16[2,320,2048]{2,1,0:T(8,128)(2,1)}, bf16[2,4,16,2,32,256]{5,4,3,2,1,0:T(8,128)(2,1)}, bf16[2,4,16,2,3...) custom-call(s32[5,32]{1,0:T(8,128)} %add_add_fusion.ids, ...), custom_call_target="tpu_custom_call", output_to_operand_aliasing={{1}: (9, {})} | custom-call | tf_op jit(solution)/shard_map/pallas_call | solution.py:176
  156.9 1.2 collective-permute-done.18
  158.7 1.7 collective-permute-start.27
  160.5 5.1 %collective-permute-done.20 = bf16[2,4,16,2,32,256]{5,4,3,2,1,0:T(8,128)(2,1)} collective-permute-done((bf16[2,4,16,2,32,256]{5,4,3,2,1,0:T(8,128)(2,1)}, bf16[2,4,16,2,32,256]{5,4,3,2,1,0:T(8,128)(2,1)}, u32[]{:S(2)}, u32[]{:S(2)}) %collective-permute-start.20) | collective-permute-done | bytes 4194336 | tf_op jit(solution)/shard_map/ppermute | solution.py:197
  165.6 2.5 fusion.3
  168.1 1.6 collective-permute-start.22
  169.7 1.5 collective-permute-start.21
  171.8 1.7 slice_bitcast_fusion.2
  173.5 2.5 fusion.1
  176.1 17.3 %collective-permute-done.22 = bf16[2,16,2,32,256]{4,3,2,1,0:T(8,128)(2,1)S(1)} collective-permute-done((bf16[2,16,2,32,256]{4,3,2,1,0:T(8,128)(2,1)S(1)}, bf16[2,16,2,32,256]{4,3,2,1,0:T(8,128)(2,1)S(1)}, u32[]{:S(2)}, u32[]{:S(2)}) %collective-permute-start.22) | collective-permute-done | bytes 1048608 | tf_op jit(solution)/shard_map/ppermute | solution.py:197
  193.4 1.2 collective-permute-done.21
  194.9 1.6 collective-permute-start.24
  197.8 1.6 collective-permute-start.23
  199.4 1.7 slice_bitcast_fusion
  201.1 8.7 %collective-permute-done.24 = bf16[1,16,2,32,256]{4,3,2,1,0:T(8,128)(2,1)S(1)} collective-permute-done((bf16[1,16,2,32,256]{4,3,2,1,0:T(8,128)(2,1)S(1)}, bf16[1,16,2,32,256]{4,3,2,1,0:T(8,128)(2,1)S(1)}, u32[]{:S(2)}, u32[]{:S(2)}) %collective-permute-start.24) | collective-permute-done | bytes 524320 | tf_op jit(solution)/shard_map/ppermute | solution.py:197
  210.2 21.5 %collective-permute-done.23 = bf16[1,16,2,32,256]{4,3,2,1,0:T(8,128)(2,1)S(1)} collective-permute-done((bf16[1,16,2,32,256]{4,3,2,1,0:T(8,128)(2,1)S(1)}, bf16[1,16,2,32,256]{4,3,2,1,0:T(8,128)(2,1)S(1)}, u32[]{:S(2)}, u32[]{:S(2)}) %collective-permute-start.23) | collective-permute-done | bytes 524320 | tf_op jit(solution)/shard_map/ppermute | solution.py:197
  233.7 1.6 collective-permute-start.30
  235.2 1.3 collective-permute-start.29
  236.5 1.3 collective-permute-start.31
  237.8 6.0 %collective-permute-done.28 = bf16[1,16,2,32,256]{4,3,2,1,0:T(8,128)(2,1)S(1)} collective-permute-done((bf16[1,16,2,32,256]{4,3,2,1,0:T(8,128)(2,1)S(1)}, bf16[1,16,2,32,256]{4,3,2,1,0:T(8,128)(2,1)S(1)}, u32[]{:S(2)}, u32[]{:S(2)}) %collective-permute-start.28) | collective-permute-done | bytes 524320 | tf_op jit(solution)/shard_map/ppermute | solution.py:197
  244.5 1.5 slice_bitcast_fusion.18
  246.0 1.9 maximum_select_fusion
  247.9 1.9 maximum_select_fusion.1
  249.8 3.2 %collective-permute-done.29 = bf16[16,2,32,256]{3,2,1,0:T(8,128)(2,1)S(1)} collective-permute-done((bf16[16,2,32,256]{3,2,1,0:T(8,128)(2,1)S(1)}, bf16[16,2,32,256]{3,2,1,0:T(8,128)(2,1)S(1)}, u32[]{:S(2)}, u32[]{:S(2)}) %collective-permute-start.29) | collective-permute-done | bytes 524320 | tf_op jit(solution)/shard_map/ppermute | solution.py:311
  253.0 1.1 select_multiply_fusion
  254.1 6.4 %collective-permute-done.31 = bf16[16,2,32,256]{3,2,1,0:T(8,128)(2,1)S(1)} collective-permute-done((bf16[16,2,32,256]{3,2,1,0:T(8,128)(2,1)S(1)}, bf16[16,2,32,256]{3,2,1,0:T(8,128)(2,1)S(1)}, u32[]{:S(2)}, u32[]{:S(2)}) %collective-permute-start.31) | collective-permute-done | bytes 524320 | tf_op jit(solution)/shard_map/ppermute | solution.py:311
  260.5 1.4 fusion.4
  (84 shorter events, 22.2 us)
Async XLA Ops:
  2.5 44.1 %collective-permute-start.1 = (bf16[1024,256]{1,0:T(8,128)(2,1)}, bf16[1024,256]{1,0:T(8,128)(2,1)S(1)}, u32[]{:S(2)}, u32[]{:S(2)}) collective-permute-start(bf16[1024,256]{1,0:T(8,128)(2,1)} %constant_dynamic-slice_fusion.1), channel_id=1, source_target_pairs={{2,0},{1,3},{6,4},{5,7},{10,8},{9,11},{14,12},{13,15},{18,16},{17,... | collective-permute-start | bytes 1572872 | tf_op jit(solution)/shard_map/ppermute | solution.py:266
  8.9 22.0 %collective-permute-start.9 = (bf16[1024,256]{1,0:T(8,128)(2,1)}, bf16[1024,256]{1,0:T(8,128)(2,1)S(1)}, u32[]{:S(2)}, u32[]{:S(2)}) collective-permute-start(bf16[1024,256]{1,0:T(8,128)(2,1)} %constant_dynamic-slice_fusion), channel_id=1, source_target_pairs={{2,0},{1,3},{6,4},{5,7},{10,8},{9,11},{14,12},{13,15},{18,16},{17,... | collective-permute-start | bytes 1572872 | tf_op jit(solution)/shard_map/ppermute | solution.py:266
  13.0 7.0 %copy-start.5 = (s32[2,8,8]{2,1,0:T(8,128)S(1)}, s32[2,8,8]{2,1,0:T(8,128)}, u32[]{:S(2)}) copy-start(s32[2,8,8]{2,1,0:T(8,128)} %param.8) | copy-start | bytes 1540
  13.0 7.1 %copy-start.6 = (s32[2,8,8]{2,1,0:T(8,128)S(1)}, s32[2,8,8]{2,1,0:T(8,128)}, u32[]{:S(2)}) copy-start(s32[2,8,8]{2,1,0:T(8,128)} %param.9) | copy-start | bytes 1540
  13.2 25.8 %copy-start = (bf16[2,256,2048]{2,1,0:T(8,128)(2,1)}, bf16[2,256,2048]{2,1,0:T(8,128)(2,1)S(1)}, u32[]{:S(2)}) copy-start(bf16[2,256,2048]{2,1,0:T(8,128)(2,1)S(1)} %pad_maximum_fusion.refs_0_) | copy-start | bytes 6291460
  13.2 76.0 %collective-permute-start = (bf16[2,256,2048]{2,1,0:T(8,128)(2,1)S(1)}, bf16[2,256,2048]{2,1,0:T(8,128)(2,1)}, u32[]{:S(2)}, u32[]{:S(2)}) collective-permute-start(bf16[2,256,2048]{2,1,0:T(8,128)(2,1)S(1)} %pad_maximum_fusion.refs_0_), channel_id=1, source_target_pairs={{2,0},{1,3},{6,4},{5,7},{10,8},{9,11},{14,12},{13,15},{18,16},{17,... | collective-permute-start | bytes 6291464 | tf_op jit(solution)/shard_map/ppermute | solution.py:273
  17.3 102.3 %collective-permute-start.17 = (bf16[2,256,2048]{2,1,0:T(8,128)(2,1)}, bf16[2,256,2048]{2,1,0:T(8,128)(2,1)}, u32[]{:S(2)}, u32[]{:S(2)}) collective-permute-start(bf16[2,256,2048]{2,1,0:T(8,128)(2,1)} %pad_maximum_fusion.1.refs_1_), channel_id=1, source_target_pairs={{2,0},{1,3},{6,4},{5,7},{10,8},{9,11},{14,12},{13,15},{18,16},{17,... | collective-permute-start | bytes 6291464 | tf_op jit(solution)/shard_map/ppermute | solution.py:274
  30.9 17.9 %collective-permute-start.10 = (bf16[1024,256]{1,0:T(8,128)(2,1)S(1)}, bf16[1024,256]{1,0:T(8,128)(2,1)}, u32[]{:S(2)}, u32[]{:S(2)}) collective-permute-start(bf16[1024,256]{1,0:T(8,128)(2,1)S(1)} %collective-permute-done.9), channel_id=1, source_target_pairs={{0,16},{8,24},{16,0},{24,8},{1,17},{9,25},{17,1},{25,9},{2,18},{10... | collective-permute-start | bytes 1572872 | tf_op jit(solution)/shard_map/ppermute | solution.py:197
  45.1 25.5 %collective-permute-start.11 = (bf16[1024,256]{1,0:T(8,128)(2,1)S(1)}, bf16[1024,256]{1,0:T(8,128)(2,1)S(1)}, u32[]{:S(2)}, u32[]{:S(2)}) collective-permute-start(bf16[1024,256]{1,0:T(8,128)(2,1)S(1)} %collective-permute-done.9), channel_id=1, source_target_pairs={{0,8},{8,0},{16,24},{24,16},{1,9},{9,1},{17,25},{25,17},{2,10},{10... | collective-permute-start | bytes 1572872 | tf_op jit(solution)/shard_map/ppermute | solution.py:197
  46.6 21.6 %collective-permute-start.2 = (bf16[1024,256]{1,0:T(8,128)(2,1)S(1)}, bf16[1024,256]{1,0:T(8,128)(2,1)S(1)}, u32[]{:S(2)}, u32[]{:S(2)}) collective-permute-start(bf16[1024,256]{1,0:T(8,128)(2,1)S(1)} %collective-permute-done.1), channel_id=1, source_target_pairs={{0,8},{8,0},{16,24},{24,16},{1,9},{9,1},{17,25},{25,17},{2,10},{10... | collective-permute-start | bytes 1572872 | tf_op jit(solution)/shard_map/ppermute | solution.py:197
  48.8 23.1 %collective-permute-start.3 = (bf16[1024,256]{1,0:T(8,128)(2,1)S(1)}, bf16[1024,256]{1,0:T(8,128)(2,1)S(1)}, u32[]{:S(2)}, u32[]{:S(2)}) collective-permute-start(bf16[1024,256]{1,0:T(8,128)(2,1)S(1)} %collective-permute-done.1), channel_id=1, source_target_pairs={{0,16},{8,24},{16,0},{24,8},{1,17},{9,25},{17,1},{25,9},{2,18},{10... | collective-permute-start | bytes 1572872 | tf_op jit(solution)/shard_map/ppermute | solution.py:197
  68.2 10.7 %collective-permute-start.12 = (bf16[1024,256]{1,0:T(8,128)(2,1)}, bf16[1024,256]{1,0:T(8,128)(2,1)S(1)}, u32[]{:S(2)}, u32[]{:S(2)}) collective-permute-start(bf16[1024,256]{1,0:T(8,128)(2,1)} %collective-permute-done.10), channel_id=1, source_target_pairs={{0,8},{8,0},{16,24},{24,16},{1,9},{9,1},{17,25},{25,17},{2,10},{10... | collective-permute-start | bytes 1572872 | tf_op jit(solution)/shard_map/ppermute | solution.py:197
  70.5 9.6 %collective-permute-start.4 = (bf16[1024,256]{1,0:T(8,128)(2,1)S(1)}, bf16[1024,256]{1,0:T(8,128)(2,1)S(1)}, u32[]{:S(2)}, u32[]{:S(2)}) collective-permute-start(bf16[1024,256]{1,0:T(8,128)(2,1)S(1)} %collective-permute-done.2), channel_id=1, source_target_pairs={{0,16},{8,24},{16,0},{24,8},{1,17},{9,25},{17,1},{25,9},{2,18},{10... | collective-permute-start | bytes 1572872 | tf_op jit(solution)/shard_map/ppermute | solution.py:197
  71.9 9.3 %collective-permute-start.13 = (bf16[1024,256]{1,0:T(8,128)(2,1)S(1)}, bf16[1024,256]{1,0:T(8,128)(2,1)S(1)}, u32[]{:S(2)}, u32[]{:S(2)}) collective-permute-start(bf16[1024,256]{1,0:T(8,128)(2,1)S(1)} %collective-permute-done.9), channel_id=1, source_target_pairs={{0,4},{4,0},{1,5},{5,1},{2,6},{6,2},{3,7},{7,3},{8,12},{12,8},{9,1... | collective-permute-start | bytes 1572872 | tf_op jit(solution)/shard_map/ppermute | solution.py:197
  78.9 3.4 %collective-permute-start.5 = (bf16[1024,256]{1,0:T(8,128)(2,1)S(1)}, bf16[1024,256]{1,0:T(8,128)(2,1)S(1)}, u32[]{:S(2)}, u32[]{:S(2)}) collective-permute-start(bf16[1024,256]{1,0:T(8,128)(2,1)S(1)} %collective-permute-done.1), channel_id=1, source_target_pairs={{0,4},{4,0},{1,5},{5,1},{2,6},{6,2},{3,7},{7,3},{8,12},{12,8},{9,1... | collective-permute-start | bytes 1572872 | tf_op jit(solution)/shard_map/ppermute | solution.py:197
  80.2 3.2 %collective-permute-start.14 = (bf16[1024,256]{1,0:T(8,128)(2,1)}, bf16[1024,256]{1,0:T(8,128)(2,1)S(1)}, u32[]{:S(2)}, u32[]{:S(2)}) collective-permute-start(bf16[1024,256]{1,0:T(8,128)(2,1)} %collective-permute-done.10), channel_id=1, source_target_pairs={{0,4},{4,0},{1,5},{5,1},{2,6},{6,2},{3,7},{7,3},{8,12},{12,8},{9,1... | collective-permute-start | bytes 1572872 | tf_op jit(solution)/shard_map/ppermute | solution.py:197
  81.1 3.4 %collective-permute-start.15 = (bf16[1024,256]{1,0:T(8,128)(2,1)S(1)}, bf16[1024,256]{1,0:T(8,128)(2,1)S(1)}, u32[]{:S(2)}, u32[]{:S(2)}) collective-permute-start(bf16[1024,256]{1,0:T(8,128)(2,1)S(1)} %collective-permute-done.11), channel_id=1, source_target_pairs={{0,4},{4,0},{1,5},{5,1},{2,6},{6,2},{3,7},{7,3},{8,12},{12,8},{9,1... | collective-permute-start | bytes 1572872 | tf_op jit(solution)/shard_map/ppermute | solution.py:197
  82.3 3.2 %collective-permute-start.6 = (bf16[1024,256]{1,0:T(8,128)(2,1)S(1)}, bf16[1024,256]{1,0:T(8,128)(2,1)S(1)}, u32[]{:S(2)}, u32[]{:S(2)}) collective-permute-start(bf16[1024,256]{1,0:T(8,128)(2,1)S(1)} %collective-permute-done.2), channel_id=1, source_target_pairs={{0,4},{4,0},{1,5},{5,1},{2,6},{6,2},{3,7},{7,3},{8,12},{12,8},{9,1... | collective-permute-start | bytes 1572872 | tf_op jit(solution)/shard_map/ppermute | solution.py:197
  83.4 3.3 %collective-permute-start.7 = (bf16[1024,256]{1,0:T(8,128)(2,1)S(1)}, bf16[1024,256]{1,0:T(8,128)(2,1)S(1)}, u32[]{:S(2)}, u32[]{:S(2)}) collective-permute-start(bf16[1024,256]{1,0:T(8,128)(2,1)S(1)} %collective-permute-done.3), channel_id=1, source_target_pairs={{0,4},{4,0},{1,5},{5,1},{2,6},{6,2},{3,7},{7,3},{8,12},{12,8},{9,1... | collective-permute-start | bytes 1572872 | tf_op jit(solution)/shard_map/ppermute | solution.py:197
  84.5 3.0 %collective-permute-start.16 = (bf16[1024,256]{1,0:T(8,128)(2,1)S(1)}, bf16[1024,256]{1,0:T(8,128)(2,1)S(1)}, u32[]{:S(2)}, u32[]{:S(2)}) collective-permute-start(bf16[1024,256]{1,0:T(8,128)(2,1)S(1)} %collective-permute-done.12), channel_id=1, source_target_pairs={{0,4},{4,0},{1,5},{5,1},{2,6},{6,2},{3,7},{7,3},{8,12},{12,8},{9,1... | collective-permute-start | bytes 1572872 | tf_op jit(solution)/shard_map/ppermute | solution.py:197
  85.5 2.9 %collective-permute-start.8 = (bf16[1024,256]{1,0:T(8,128)(2,1)S(1)}, bf16[1024,256]{1,0:T(8,128)(2,1)S(1)}, u32[]{:S(2)}, u32[]{:S(2)}) collective-permute-start(bf16[1024,256]{1,0:T(8,128)(2,1)S(1)} %collective-permute-done.4), channel_id=1, source_target_pairs={{0,4},{4,0},{1,5},{5,1},{2,6},{6,2},{3,7},{7,3},{8,12},{12,8},{9,1... | collective-permute-start | bytes 1572872 | tf_op jit(solution)/shard_map/ppermute | solution.py:197
  119.6 38.5 %collective-permute-start.18 = (bf16[2,192,2048]{2,1,0:T(8,128)(2,1)}, bf16[2,192,2048]{2,1,0:T(8,128)(2,1)}, u32[]{:S(2)}, u32[]{:S(2)}) collective-permute-start(bf16[2,192,2048]{2,1,0:T(8,128)(2,1)} %get-tuple-element.46), channel_id=1, source_target_pairs={{0,2},{3,1},{4,6},{7,5},{8,10},{11,9},{12,14},{15,13},{16,18},{19,... | collective-permute-start | bytes 4718600 | tf_op jit(solution)/shard_map/ppermute | solution.py:296
  120.9 37.7 %copy-start.4 = (bf16[2,256,2048]{2,1,0:T(8,128)(2,1)S(1)}, bf16[2,256,2048]{2,1,0:T(8,128)(2,1)}, u32[]{:S(2)}) copy-start(bf16[2,256,2048]{2,1,0:T(8,128)(2,1)} %get-tuple-element.44) | copy-start | bytes 6291460
  158.1 7.5 %collective-permute-start.20 = (bf16[2,4,16,2,32,256]{5,4,3,2,1,0:T(8,128)(2,1)}, bf16[2,4,16,2,32,256]{5,4,3,2,1,0:T(8,128)(2,1)}, u32[]{:S(2)}, u32[]{:S(2)}) collective-permute-start(bf16[2,4,16,2,32,256]{5,4,3,2,1,0:T(8,128)(2,1)} %get-tuple-element.62), channel_id=1, source_target_pairs={{0,4},{4,0},{1,5},{5,1},{2,6},{6,2},{3,7},{7,3},{8,12},{12,8},{9,1... | collective-permute-start | bytes 12582920 | tf_op jit(solution)/shard_map/ppermute | solution.py:197
  158.1 15.5 %collective-permute-start.19 = (bf16[2,4,16,2,32,256]{5,4,3,2,1,0:T(8,128)(2,1)}, bf16[2,4,16,2,32,256]{5,4,3,2,1,0:T(8,128)(2,1)}, u32[]{:S(2)}, u32[]{:S(2)}) collective-permute-start(bf16[2,4,16,2,32,256]{5,4,3,2,1,0:T(8,128)(2,1)} %get-tuple-element.60), channel_id=1, source_target_pairs={{0,4},{4,0},{1,5},{5,1},{2,6},{6,2},{3,7},{7,3},{8,12},{12,8},{9,1... | collective-permute-start | bytes 12582920 | tf_op jit(solution)/shard_map/ppermute | solution.py:197
  158.6 7.0 %copy-start.2 = (bf16[2,4,16,2,32,256]{5,4,3,2,1,0:T(8,128)(2,1)S(1)}, bf16[2,4,16,2,32,256]{5,4,3,2,1,0:T(8,128)(2,1)}, u32[]{:S(2)}) copy-start(bf16[2,4,16,2,32,256]{5,4,3,2,1,0:T(8,128)(2,1)} %get-tuple-element.61) | copy-start | bytes 12582916
  158.7 12.8 %copy-start.1 = (bf16[2,4,16,2,32,256]{5,4,3,2,1,0:T(8,128)(2,1)S(1)}, bf16[2,4,16,2,32,256]{5,4,3,2,1,0:T(8,128)(2,1)}, u32[]{:S(2)}) copy-start(bf16[2,4,16,2,32,256]{5,4,3,2,1,0:T(8,128)(2,1)} %get-tuple-element.59) | copy-start | bytes 12582916
  158.7 73.4 %collective-permute-start.27 = (bf16[2,320,2048]{2,1,0:T(8,128)(2,1)}, bf16[2,320,2048]{2,1,0:T(8,128)(2,1)S(1)}, u32[]{:S(2)}, u32[]{:S(2)}) collective-permute-start(bf16[2,320,2048]{2,1,0:T(8,128)(2,1)} %get-tuple-element.71), channel_id=1, source_target_pairs={{0,2},{3,1},{4,6},{7,5},{8,10},{11,9},{12,14},{15,13},{16,18},{19,... | collective-permute-start | bytes 7864328 | tf_op jit(solution)/shard_map/ppermute | solution.py:298
  168.1 25.3 %collective-permute-start.22 = (bf16[2,16,2,32,256]{4,3,2,1,0:T(8,128)(2,1)S(1)}, bf16[2,16,2,32,256]{4,3,2,1,0:T(8,128)(2,1)S(1)}, u32[]{:S(2)}, u32[]{:S(2)}) collective-permute-start(bf16[2,16,2,32,256]{4,3,2,1,0:T(8,128)(2,1)S(1)} %get-tuple-element.84), channel_id=1, source_target_pairs={{0,16},{8,24},{16,0},{24,8},{1,17},{9,25},{17,1},{25,9},{2,18},{10... | collective-permute-start | bytes 3145736 | tf_op jit(solution)/shard_map/ppermute | solution.py:197
  169.7 24.9 %collective-permute-start.21 = (bf16[2,16,2,32,256]{4,3,2,1,0:T(8,128)(2,1)S(1)}, bf16[2,16,2,32,256]{4,3,2,1,0:T(8,128)(2,1)S(1)}, u32[]{:S(2)}, u32[]{:S(2)}) collective-permute-start(bf16[2,16,2,32,256]{4,3,2,1,0:T(8,128)(2,1)S(1)} %get-tuple-element.85), channel_id=1, source_target_pairs={{0,8},{8,0},{16,24},{24,16},{1,9},{9,1},{17,25},{25,17},{2,10},{10... | collective-permute-start | bytes 3145736 | tf_op jit(solution)/shard_map/ppermute | solution.py:197
  194.9 14.9 %collective-permute-start.24 = (bf16[1,16,2,32,256]{4,3,2,1,0:T(8,128)(2,1)S(1)}, bf16[1,16,2,32,256]{4,3,2,1,0:T(8,128)(2,1)S(1)}, u32[]{:S(2)}, u32[]{:S(2)}) collective-permute-start(bf16[1,16,2,32,256]{4,3,2,1,0:T(8,128)(2,1)S(1)} %add_convert_fusion.7), channel_id=1, source_target_pairs={{0,8},{8,0},{16,24},{24,16},{1,9},{9,1},{17,25},{25,17},{2,10},{10... | collective-permute-start | bytes 1572872 | tf_op jit(solution)/shard_map/ppermute | solution.py:197
  196.5 35.7 %collective-permute-start.25 = (bf16[2,16,2,32,256]{4,3,2,1,0:T(8,128)(2,1)S(1)}, bf16[2,16,2,32,256]{4,3,2,1,0:T(8,128)(2,1)S(1)}, u32[]{:S(2)}, u32[]{:S(2)}) collective-permute-start(bf16[2,16,2,32,256]{4,3,2,1,0:T(8,128)(2,1)S(1)} %get-tuple-element.69), channel_id=1, source_target_pairs={{0,8},{8,0},{16,24},{24,16},{1,9},{9,1},{17,25},{25,17},{2,10},{10... | collective-permute-start | bytes 3145736 | tf_op jit(solution)/shard_map/ppermute | solution.py:197
  197.0 35.1 %collective-permute-start.26 = (bf16[2,16,2,32,256]{4,3,2,1,0:T(8,128)(2,1)S(1)}, bf16[2,16,2,32,256]{4,3,2,1,0:T(8,128)(2,1)S(1)}, u32[]{:S(2)}, u32[]{:S(2)}) collective-permute-start(bf16[2,16,2,32,256]{4,3,2,1,0:T(8,128)(2,1)S(1)} %get-tuple-element.70), channel_id=1, source_target_pairs={{0,16},{8,24},{16,0},{24,8},{1,17},{9,25},{17,1},{25,9},{2,18},{10... | collective-permute-start | bytes 3145736 | tf_op jit(solution)/shard_map/ppermute | solution.py:197
  197.8 33.9 %collective-permute-start.23 = (bf16[1,16,2,32,256]{4,3,2,1,0:T(8,128)(2,1)S(1)}, bf16[1,16,2,32,256]{4,3,2,1,0:T(8,128)(2,1)S(1)}, u32[]{:S(2)}, u32[]{:S(2)}) collective-permute-start(bf16[1,16,2,32,256]{4,3,2,1,0:T(8,128)(2,1)S(1)} %add_convert_fusion.9), channel_id=1, source_target_pairs={{0,16},{8,24},{16,0},{24,8},{1,17},{9,25},{17,1},{25,9},{2,18},{10... | collective-permute-start | bytes 1572872 | tf_op jit(solution)/shard_map/ppermute | solution.py:197
  201.1 32.0 %copy-start.3 = (bf16[2,256,2048]{2,1,0:T(8,128)(2,1)S(1)}, bf16[2,256,2048]{2,1,0:T(8,128)(2,1)}, u32[]{:S(2)}) copy-start(bf16[2,256,2048]{2,1,0:T(8,128)(2,1)} %get-tuple-element.57) | copy-start | bytes 6291460
  232.4 11.4 %collective-permute-start.28 = (bf16[1,16,2,32,256]{4,3,2,1,0:T(8,128)(2,1)S(1)}, bf16[1,16,2,32,256]{4,3,2,1,0:T(8,128)(2,1)S(1)}, u32[]{:S(2)}, u32[]{:S(2)}) collective-permute-start(bf16[1,16,2,32,256]{4,3,2,1,0:T(8,128)(2,1)S(1)} %add_convert_fusion.5), channel_id=1, source_target_pairs={{0,16},{8,24},{16,0},{24,8},{1,17},{9,25},{17,1},{25,9},{2,18},{10... | collective-permute-start | bytes 1572872 | tf_op jit(solution)/shard_map/ppermute | solution.py:197
  233.7 20.4 %collective-permute-start.30 = (bf16[1,16,2,32,256]{4,3,2,1,0:T(8,128)(2,1)S(1)}, bf16[1,16,2,32,256]{4,3,2,1,0:T(8,128)(2,1)S(1)}, u32[]{:S(2)}, u32[]{:S(2)}) collective-permute-start(bf16[1,16,2,32,256]{4,3,2,1,0:T(8,128)(2,1)S(1)} %add_convert_fusion.4), channel_id=1, source_target_pairs={{0,8},{8,0},{16,24},{24,16},{1,9},{9,1},{17,25},{25,17},{2,10},{10... | collective-permute-start | bytes 1572872 | tf_op jit(solution)/shard_map/ppermute | solution.py:197
  235.2 17.7 %collective-permute-start.29 = (bf16[16,2,32,256]{3,2,1,0:T(8,128)(2,1)S(1)}, bf16[16,2,32,256]{3,2,1,0:T(8,128)(2,1)S(1)}, u32[]{:S(2)}, u32[]{:S(2)}) collective-permute-start(bf16[16,2,32,256]{3,2,1,0:T(8,128)(2,1)S(1)} %fusion.5), channel_id=1, source_target_pairs={{0,2},{3,1},{4,6},{7,5},{8,10},{11,9},{12,14},{15,13},{16,18},{19,... | collective-permute-start | bytes 1572872 | tf_op jit(solution)/shard_map/ppermute | solution.py:311
  236.5 24.0 %collective-permute-start.31 = (bf16[16,2,32,256]{3,2,1,0:T(8,128)(2,1)S(1)}, bf16[16,2,32,256]{3,2,1,0:T(8,128)(2,1)S(1)}, u32[]{:S(2)}, u32[]{:S(2)}) collective-permute-start(bf16[16,2,32,256]{3,2,1,0:T(8,128)(2,1)S(1)} %fusion.6), channel_id=1, source_target_pairs={{0,2},{3,1},{4,6},{7,5},{8,10},{11,9},{12,14},{15,13},{16,18},{19,... | collective-permute-start | bytes 1572872 | tf_op jit(solution)/shard_map/ppermute | solution.py:311

commit v4 on v3

--- a/solution.py
+++ b/solution.py
@@ -32,9 +32,9 @@
     chunks = 2 if last else 1
     nears, fars = take(chunks), take(chunks)
     near, far = nears[-1], fars[-1]
-    up, down = take(2)
-    if last:
-        hidden_kept, d_pre_kept, _ = take(3)
+    weights = take(4)
+    if last:
+        hidden_kept, d_pre_kept = take(2)
     (near_out,) = take(1)
     far_out = take(1 if last else 2)
     if last:
@@ -46,7 +46,7 @@
         up_sum, down_sum = take(2)
     step = pl.program_id(0)
     steps = pl.num_programs(0)
-    each, _, size, _ = up.shape
+    each, _, size, _ = weights[0].shape
 
     @pl.when(step == 0)
     def _():
@@ -54,7 +54,6 @@
         back_acc[...] = jnp.zeros_like(back_acc)
 
     theirs = step < steps // 2
-    meets = theirs.astype(jnp.int32)
 
     def columns(block):
         return pl.ds(pl.multiple_of(block * size, size), size)
@@ -65,30 +64,34 @@
     def tall(first, second):
         return jnp.concatenate([first, second], axis=0)
 
-    work = []
-    for e in range(each):
-        ins = [columns(ids[k, step * each + e]) for k in (0, 1)]
-        outs = [columns(ids[k, step * each + e]) for k in (2, 3)]
-        x_cat, g_cat = both(0, ins), both(1, outs)
-        up_cat = jnp.concatenate([up[e, meets], up[e, 1 - meets]], axis=0)
-        down_cat = jnp.concatenate([down[e, meets], down[e, 1 - meets]], axis=1)
-        pre = dot(x_cat, up_cat, (1, 0))
-        d_hidden = dot(g_cat, down_cat, (1, 1))
-        work.append((ins, outs, x_cat, g_cat, up_cat, down_cat, pre, d_hidden))
-    done = []
-    for e, (ins, outs, x_cat, g_cat, up_cat, down_cat, pre, d_hidden) in enumerate(work):
-        hidden, d_pre = activate(pre, d_hidden)
-        done.append((dot(hidden, down_cat, (1, 0)), dot(d_pre, up_cat, (1, 1))))
-        if last:
-            up_sum[e] = dot(tall(both(0, ins, 0), x_cat), tall(d_pre_kept[e], d_pre), (0, 0))
-            down_sum[e] = dot(tall(hidden_kept[e], hidden), tall(both(1, outs, 0), g_cat), (0, 0))
-        else:
-            hidden_kept[e] = hidden
-            d_pre_kept[e] = d_pre
-    for (ins, outs, *_), (out, back) in zip(work, done):
-        for s in range(2):
-            out_acc[s, :, outs[s]] += out[:, s * size : (s + 1) * size]
-            back_acc[s, :, ins[s]] += back[:, s * size : (s + 1) * size]
+    def work_on(up, down, meets):
+        work = []
+        for e in range(each):
+            ins = [columns(ids[k, step * each + e]) for k in (0, 1)]
+            outs = [columns(ids[k, step * each + e]) for k in (2, 3)]
+            x_cat, g_cat = both(0, ins), both(1, outs)
+            up_cat = jnp.concatenate([up[e, meets], up[e, 1 - meets]], axis=0)
+            down_cat = jnp.concatenate([down[e, meets], down[e, 1 - meets]], axis=1)
+            pre = dot(x_cat, up_cat, (1, 0))
+            d_hidden = dot(g_cat, down_cat, (1, 1))
+            work.append((ins, outs, x_cat, g_cat, up_cat, down_cat, pre, d_hidden))
+        done = []
+        for e, (ins, outs, x_cat, g_cat, up_cat, down_cat, pre, d_hidden) in enumerate(work):
+            hidden, d_pre = activate(pre, d_hidden)
+            done.append((dot(hidden, down_cat, (1, 0)), dot(d_pre, up_cat, (1, 1))))
+            if last:
+                up_sum[e] = dot(tall(both(0, ins, 0), x_cat), tall(d_pre_kept[e], d_pre), (0, 0))
+                down_sum[e] = dot(tall(hidden_kept[e], hidden), tall(both(1, outs, 0), g_cat), (0, 0))
+            else:
+                hidden_kept[e] = hidden
+                d_pre_kept[e] = d_pre
+        for (ins, outs, *_), (out, back) in zip(work, done):
+            for s in range(2):
+                out_acc[s, :, outs[s]] += out[:, s * size : (s + 1) * size]
+                back_acc[s, :, ins[s]] += back[:, s * size : (s + 1) * size]
+
+    pl.when(theirs)(lambda: work_on(*weights[:2], 1))
+    pl.when(jnp.logical_not(theirs))(lambda: work_on(*weights[2:], 0))
     if last:
         me = ids[4, 0]
         shard = sums[0].shape[4]
@@ -121,9 +124,9 @@
                 row += part.shape[1]
 
 
-def layer(slots, ids, nears, fars, weights, split=None, earlier=()):
-    steps, _, size, _ = weights[0].shape
-    hid = steps // 2
+def layer(slots, ids, nears, fars, weights, split=None, kept=()):
+    hid, _, size, _ = weights[0].shape
+    steps = 2 * hid
     _, count, width = nears[-1].shape
     shards = len(slots[0])
     last = split is None
@@ -133,21 +136,24 @@
     def whole(shape):
         return pl.BlockSpec(shape, lambda i, ids: (0,) * len(shape))
 
+    def weight(part):
+        return pl.BlockSpec(
+            (each, 2, size, size),
+            lambda i, ids: (jnp.clip(i - part * turns, 0, turns - 1), 0, 0, 0),
+        )
+
     def blocks(shape):
         return pl.BlockSpec((each, *shape[1:]), lambda i, ids: (i,) + (0,) * (len(shape) - 1))
 
     in_specs = [whole(part.shape) for part in (*nears, *fars)]
-    in_specs += [blocks(weight.shape) for weight in weights]
+    in_specs += [weight(part) for part in (0, 0, 1, 1)]
     result = jax.ShapeDtypeStruct((2, count, width), BF16)
     out_shape = [result]
     out_specs = [whole(result.shape)]
     scratch = [pltpu.VMEM((2, count, width), F32)] * 2
-    aliases = {}
-    if last:
-        in_specs += [blocks(part.shape) for part in earlier[:2]]
-        in_specs += [pl.BlockSpec(memory_space=pl.ANY)]
-        aliases = {len(in_specs): 1}
-        out_shape.append(jax.ShapeDtypeStruct(earlier[2].shape, BF16))
+    if last:
+        in_specs += [blocks(part.shape) for part in kept]
+        out_shape.append(result)
         out_specs.append(whole(result.shape))
         shard = size // shards
         out_shape += [jax.ShapeDtypeStruct((2, shards // 2, hid, 2, shard, size), BF16)] * 4
@@ -166,11 +172,9 @@
             pltpu.VMEM((each, size, 2 * size), F32),
         ]
     else:
-        rest, behind = count - split[0], split[1]
-        out_shape.append(jax.ShapeDtypeStruct((2, split[0], width), BF16))
-        out_shape.append(jax.ShapeDtypeStruct((2, behind + rest, width), BF16))
-        out_specs.append(whole((2, split[0], width)))
-        out_specs.append(pl.BlockSpec((2, rest, width), lambda i, ids: (0, behind // rest, 0)))
+        for part in (split, count - split):
+            out_shape.append(jax.ShapeDtypeStruct((2, part, width), BF16))
+            out_specs.append(whole((2, part, width)))
         out_shape += [jax.ShapeDtypeStruct((steps, count, size), BF16)] * 2
         out_specs += [blocks(out_shape[-1].shape)] * 2
     return pl.pallas_call(
@@ -183,12 +187,11 @@
             out_specs=out_specs,
             scratch_shapes=scratch,
         ),
-        input_output_aliases=aliases,
         compiler_params=pltpu.CompilerParams(
             dimension_semantics=("arbitrary",), vmem_limit_bytes=60 << 20
         ),
         cost_estimate=pl.CostEstimate(flops=0, bytes_accessed=0, transcendentals=0),
-    )(ids, *nears, *fars, *weights, *earlier)
+    )(ids, *nears, *fars, *weights, *kept)
 
 
 def hop(block, bit):
@@ -201,16 +204,15 @@
     return [unit << k for k in range(count.bit_length() - 1)]
 
 
-def gather(shard, order, me, weight):
+def gather(shard, order, me, shape):
     parts = {0: shard}
     for bit in order:
         for place in list(parts):
             parts[place | bit] = hop(parts[place], bit)
-    ours = weight.reshape(-1, *shard.shape)
-    table = jnp.concatenate([jnp.zeros_like(ours), ours])
+    table = jnp.zeros((len(parts), *shard.shape), shard.dtype)
     for place, part in parts.items():
         table = lax.dynamic_update_slice_in_dim(table, part[None], place ^ me, 0)
-    return table.reshape(-1, *weight.shape[1:])
+    return table.reshape(shape)
 
 
 def total(terms):
@@ -258,7 +260,7 @@
     works = (group % away % 2 == 0) != (group >= away)
     partner = (group + away) % groups
 
-    first, split = tok_rows // 2, 3 * tok_rows // 8
+    first, split = 11 * tok_rows // 16, 3 * tok_rows // 8
     lines = hid * 2 * size // shards
 
     def fetch(weight):
@@ -271,10 +273,11 @@
         for low, high in ((0, first), (first, tok_rows))
     ]
     far = [lax.ppermute(near[0], "tensor", into)]
-    far.append(lax.ppermute(near[1], "tensor", into))
-    up = gather(up_shard, dp_bits + seq_bits, me, up_weight)
-    down = gather(down_shard, dp_bits[::-1] + seq_bits, me, down_weight)
-    weights = (up, down)
+    later, up_shard = lax.optimization_barrier((near[1], up_shard))
+    far.append(lax.ppermute(later, "tensor", into))
+    up = gather(up_shard, dp_bits + seq_bits, me, up_weight.shape)
+    down = gather(down_shard, dp_bits[::-1] + seq_bits, me, up_weight.shape)
+    weights = (up, down, up_weight, down_weight)
 
     def block_ids(perm):
         flat = perm.reshape(2, -1)
@@ -288,14 +291,13 @@
 
     orders = [dp_bits + seq_bits[1:], dp_bits[::-1] + seq_bits[1:]]
     slots = [slots_of(order, shards) for order in orders]
-    near_one, early, rest, *kept = layer(
-        slots, ids, near[:1], far[:1], weights, (split, tok_rows - first)
-    )
-    early, far[1] = lax.optimization_barrier((early, far[1]))
-    near_two, rest, *sums = layer(slots, ids, near, far, weights, earlier=(*kept, rest))
+    near_one, early, middle, *kept = layer(slots, ids, near[:1], far[:1], weights, split)
+    early, middle, far[1] = lax.optimization_barrier((early, middle, far[1]))
+    near_two, late, *sums = layer(slots, ids, near, far, weights, kept=kept)
     early = lax.ppermute(early, "tensor", back)
-    early, rest, near_two, sums = lax.optimization_barrier((early, rest, near_two, sums))
-    rest = lax.ppermute(rest, "tensor", back)
+    early, near_two, late, sums = lax.optimization_barrier((early, near_two, late, sums))
+    middle = lax.ppermute(middle, "tensor", back)
+    late = lax.ppermute(late, "tensor", back)
 
     def terms_of(keep, send):
         come = hop(send, seq_bits[0])
@@ -304,18 +306,18 @@
     theirs, mine = terms_of(*sums[:2]), terms_of(*sums[2:])
     theirs = [halved(*halve(theirs[k], orders[k][0])) for k in range(2)]
     mine = [halve(mine[k], orders[k][0]) for k in range(2)]
-    uppers, theirs = lax.optimization_barrier(([upper for _, upper, _ in mine], theirs))
+    uppers, theirs, middle = lax.optimization_barrier(
+        ([upper for _, upper, _ in mine], theirs, middle)
+    )
     mine = [halved(terms, upper, bit) for (terms, _, bit), upper in zip(mine, uppers)]
     theirs = [reduce_scatter(theirs[k], orders[k][1:]).astype(BF16) for k in range(2)]
-    theirs, mine, rest = lax.optimization_barrier((theirs, mine, rest))
     theirs = [lax.ppermute(part, "tensor", back) for part in theirs]
+    theirs[1], mine, late = lax.optimization_barrier((theirs[1], mine, late))
     mine = [reduce_scatter(mine[k], orders[k][1:]) for k in range(2)]
-    early, rest, mine[0] = lax.optimization_barrier((early, rest, mine[0]))
 
     def deliver(k):
-        after = tok_rows - first
         ours = jnp.concatenate([near_one[k], near_two[k]])
-        return jnp.where(works, ours, jnp.concatenate([early[k], rest[k, after:], rest[k, :after]]))
+        return jnp.where(works, ours, jnp.concatenate([early[k], middle[k], late[k]]))
 
     scale = float(tok_rows * shards) ** (-0.5)
     grads = [jnp.where(works, m, t.astype(F32)) * scale for m, t in zip(mine, theirs)]

time: 263 us -> 250 us (0.951)
  waiting for transfers between devices: 114 us -> 91.2 us
  starting transfers between devices: 34.1 us -> 39.8 us
  Pallas kernels: 57.5 us -> 61.3 us
    ppermute x24, waiting for transfers between devices: 83.6 us -> 48 us  [hop(): lax.ppermute(block, axis, [(i, i ^ bit) for i in range(lax.axis_size(axis...]
    ppermute x2 -> x3, waiting for transfers between devices: 8.88 us -> 24.2 us  [the longest x1 17.9 us: on_device(): middle = lax.ppermute(middle, 'tensor', back)]
    ppermute x1, waiting for transfers between devices: 0.01 us -> 14.2 us  [on_device(): far = [lax.ppermute(near[0], 'tensor', into)]]
    concatenate x2 -> x0, local copies, waits for them, and re-layouts: 12 us -> none  [gather(): table = jnp.concatenate([jnp.zeros_like(ours), ours])]
    ppermute x2, waiting for transfers between devices: 9.56 us -> 0.01 us  [on_device(): theirs = [lax.ppermute(part, 'tensor', back) for part in theirs]]
    ppermute x2, waiting for transfers between devices: 10.6 us -> 1.61 us  [fetch(): return lax.ppermute(shard, 'tensor', into)]
    another operation x0 -> x2, local copies, waits for them, and re-layouts: none -> 4.51 us
    pallas_call x2, Pallas kernels: 57.5 us -> 61.3 us  [layer(): pl.pallas_call(functools.partial(layer_kernel, last, slots), out_shape=ou...]
  transfers between devices with their start and end apart: 32 -> 33, of which waited for: 14 -> 15; matrix products, arithmetic and copies ran while one was open for 20% -> 21% of each run, Pallas kernels for 22% -> 25%
where the time goes in v4:
time: 250 us; the launch traced here: 249 us
  waiting for transfers between devices  91.2 us (36%)
  Pallas kernels  61.3 us (25%)
  starting transfers between devices  39.8 us (16%)
  local copies, waits for them, and re-layouts  38.2 us (15%)
  other arithmetic  17.5 us (7%)
    pallas_call x2, Pallas kernels, layer(): pl.pallas_call(functools.partial(layer_kernel, last, slots), out_shape=ou...  61.3 us
    ppermute x24, waiting for transfers between devices, hop(): lax.ppermute(block, axis, [(i, i ^ bit) for i in range(lax.axis_size(axis...  48 us
    ppermute x24, starting transfers between devices, hop(): lax.ppermute(block, axis, [(i, i ^ bit) for i in range(lax.axis_size(axis...  19.8 us
    ppermute x1, waiting for transfers between devices, on_device(): middle = lax.ppermute(middle, 'tensor', back)  17.9 us
    dynamic_update_slice x16, local copies, waits for them, and re-layouts, gather(): table = lax.dynamic_update_slice_in_dim(table, part[None], place ^ me, 0)  15.6 us
    ppermute x1, waiting for transfers between devices, on_device(): far = [lax.ppermute(near[0], 'tensor', into)]  14.2 us
    ppermute x2, starting transfers between devices, fetch(): return lax.ppermute(shard, 'tensor', into)  7.37 us
    ppermute x1, waiting for transfers between devices, on_device(): late = lax.ppermute(late, 'tensor', back)  6.28 us
  transfers between devices with their start and end apart: 33, of which 15 were waited for; matrix products, arithmetic and copies ran while one was open for 21% of the time, Pallas kernels for 25%

profile of v4, /device:TPU:8, one launch (start us, length us, event | category | flops | bytes accessed | tf_op | source)
XLA Modules:
  0.0 249.0 jit_solution(17717939000185992103)
XLA Ops:
  0.6 1.9 constant_dynamic-slice_fusion.1
  2.5 5.3 %collective-permute-start.1 = (bf16[1024,256]{1,0:T(8,128)(2,1)}, bf16[1024,256]{1,0:T(8,128)(2,1)}, u32[]{:S(2)}, u32[]{:S(2)}) collective-permute-start(bf16[1024,256]{1,0:T(8,128)(2,1)} %constant_dynamic-slice_fusion.1), channel_id=1, source_target_pairs={{2,0},{1,3},{6,4},{5,7},{10,8},{9,11},{14,12},{13,15},{18,16},{17,... | collective-permute-start | bytes 1572872 | tf_op jit(solution)/shard_map/ppermute | solution.py:268
  7.8 1.9 constant_dynamic-slice_fusion
  9.7 2.1 collective-permute-start.9
  11.8 2.0 slice_bitcast_fusion.2
  14.0 2.9 %collective-permute-start = (bf16[2,352,2048]{2,1,0:T(8,128)(2,1)S(1)}, bf16[2,352,2048]{2,1,0:T(8,128)(2,1)}, u32[]{:S(2)}, u32[]{:S(2)}) collective-permute-start(bf16[2,352,2048]{2,1,0:T(8,128)(2,1)S(1)} %pad_maximum_fusion.refs_0_), channel_id=1, source_target_pairs={{2,0},{1,3},{6,4},{5,7},{10,8},{9,11},{14,12},{13,15},{18,16},{17,... | collective-permute-start | bytes 8650760 | tf_op jit(solution)/shard_map/ppermute | solution.py:275
  16.9 2.2 slice_bitcast_fusion.20
  22.6 2.3 pad_maximum_fusion.1.refs_1_
  24.9 1.5 collective-permute-start.2
  27.7 1.5 collective-permute-start.3
  29.3 1.6 collective-permute-done.9
  30.9 1.5 collective-permute-start.10
  32.4 2.2 broadcast.9.clone
  34.6 1.9 bitcast_dynamic-update-slice_fusion.15
  36.5 2.3 broadcast.9.clone.1
  38.8 1.9 bitcast_dynamic-update-slice_fusion.7
  40.7 1.5 collective-permute-start.11
  43.0 10.6 %collective-permute-done.10 = bf16[1024,256]{1,0:T(8,128)(2,1)S(1)} collective-permute-done((bf16[1024,256]{1,0:T(8,128)(2,1)}, bf16[1024,256]{1,0:T(8,128)(2,1)S(1)}, u32[]{:S(2)}, u32[]{:S(2)}) %collective-permute-start.10) | collective-permute-done | bytes 524320 | tf_op jit(solution)/shard_map/ppermute | solution.py:200
  53.5 1.5 collective-permute-start.4
  57.3 2.3 collective-permute-start.17
  60.5 6.6 %collective-permute-done.4 = bf16[1024,256]{1,0:T(8,128)(2,1)S(1)} collective-permute-done((bf16[1024,256]{1,0:T(8,128)(2,1)S(1)}, bf16[1024,256]{1,0:T(8,128)(2,1)S(1)}, u32[]{:S(2)}, u32[]{:S(2)}) %collective-permute-start.4) | collective-permute-done | bytes 524320 | tf_op jit(solution)/shard_map/ppermute | solution.py:200
  78.4 14.2 %collective-permute-done.refs_1_.refs_2_ = bf16[2,352,2048]{2,1,0:T(8,128)(2,1)} collective-permute-done((bf16[2,352,2048]{2,1,0:T(8,128)(2,1)S(1)}, bf16[2,352,2048]{2,1,0:T(8,128)(2,1)}, u32[]{:S(2)}, u32[]{:S(2)}) %collective-permute-start) | collective-permute-done | bytes 2883616 | tf_op jit(solution)/shard_map/ppermute | solution.py:275
  92.6 28.5 %shard_map.93 = (bf16[2,352,2048]{2,1,0:T(8,128)(2,1)}, bf16[2,192,2048]{2,1,0:T(8,128)(2,1)}, bf16[2,160,2048]{2,1,0:T(8,128)(2,1)}, bf16[32,352,256]{2,1,0:T(8,128)(2,1)}, bf16[32,352,256]{2,1,0:T(8,128)(2,1)}) custom-call(s32[5,32]{1,0:T(8,128)} %add_add_fusion.ids, bf16[2,352,2048]{2,1,0:T(8,128)(2,1)} %copy-done, ...), custom_call_target="tpu_custom_call" | custom-call | tf_op jit(solution)/shard_map/pallas_call | solution.py:180
  121.1 1.5 collective-permute-start.18
  122.6 32.8 %shard_map.94 = (bf16[2,160,2048]{2,1,0:T(8,128)(2,1)}, bf16[2,160,2048]{2,1,0:T(8,128)(2,1)}, bf16[2,4,16,2,32,256]{5,4,3,2,1,0:T(8,128)(2,1)}, bf16[2,4,16,2,3...) custom-call(s32[5,32]{1,0:T(8,128)} %add_add_fusion.ids, ...), custom_call_target="tpu_custom_call" | custom-call | tf_op jit(solution)/shard_map/pallas_call | solution.py:180
  155.3 3.2 %collective-permute-done.18 = bf16[2,192,2048]{2,1,0:T(8,128)(2,1)} collective-permute-done((bf16[2,192,2048]{2,1,0:T(8,128)(2,1)}, bf16[2,192,2048]{2,1,0:T(8,128)(2,1)}, u32[]{:S(2)}, u32[]{:S(2)}) %collective-permute-start.18) | collective-permute-done | bytes 1572896 | tf_op jit(solution)/shard_map/ppermute | solution.py:297
  159.1 1.5 collective-permute-start.23
  160.9 1.6 collective-permute-start.28
  163.4 1.6 slice_bitcast_fusion.12
  166.0 2.5 %fusion.3 = (bf16[2,16,2,32,256]{4,3,2,1,0:T(8,128)(2,1)S(1)}, bf16[2,16,2,32,256]{4,3,2,1,0:T(8,128)(2,1)S(1)}) fusion(bf16[2,4,16,2,32,256]{5,4,3,2,1,0:T(8,128)(2,1)} %collective-permute-done.20, bf16[2,4,16,2,32,256]{5,4,3,2,1,0:T(8,128)(2,1)S(1)} %copy-done.2), kind=kLoop, calls=%fused_computation.15 | loop fusion | flops 4194304 | bytes 6291456 | tf_op jit(solution)/shard_map/convert_element_type | solution.py:224
  168.6 1.6 collective-permute-start.22
  170.1 1.5 collective-permute-start.21
  171.8 1.7 slice_bitcast_fusion.6
  173.5 2.5 %fusion.1 = (bf16[2,16,2,32,256]{4,3,2,1,0:T(8,128)(2,1)S(1)}, bf16[2,16,2,32,256]{4,3,2,1,0:T(8,128)(2,1)S(1)}) fusion(bf16[2,4,16,2,32,256]{5,4,3,2,1,0:T(8,128)(2,1)} %collective-permute-done.19, bf16[2,4,16,2,32,256]{5,4,3,2,1,0:T(8,128)(2,1)S(1)} %copy-done.1), kind=kLoop, calls=%fused_computation.13 | loop fusion | flops 4194304 | bytes 6291456 | tf_op jit(solution)/shard_map/convert_element_type | solution.py:224
  176.1 17.9 %collective-permute-done.23 = bf16[2,160,2048]{2,1,0:T(8,128)(2,1)S(1)} collective-permute-done((bf16[2,160,2048]{2,1,0:T(8,128)(2,1)}, bf16[2,160,2048]{2,1,0:T(8,128)(2,1)S(1)}, u32[]{:S(2)}, u32[]{:S(2)}) %collective-permute-start.23) | collective-permute-done | bytes 1310752 | tf_op jit(solution)/shard_map/ppermute | solution.py:299
  195.4 1.6 collective-permute-start.24
  196.9 1.7 slice_bitcast_fusion.4
  200.1 1.5 collective-permute-start.27
  201.6 8.7 %collective-permute-done.24 = bf16[1,16,2,32,256]{4,3,2,1,0:T(8,128)(2,1)S(1)} collective-permute-done((bf16[1,16,2,32,256]{4,3,2,1,0:T(8,128)(2,1)S(1)}, bf16[1,16,2,32,256]{4,3,2,1,0:T(8,128)(2,1)S(1)}, u32[]{:S(2)}, u32[]{:S(2)}) %collective-permute-start.24) | collective-permute-done | bytes 524320 | tf_op jit(solution)/shard_map/ppermute | solution.py:200
  212.1 1.8 collective-permute-done.30
  214.2 1.5 collective-permute-start.31
  215.8 6.3 %collective-permute-done.28 = bf16[2,160,2048]{2,1,0:T(8,128)(2,1)S(1)} collective-permute-done((bf16[2,160,2048]{2,1,0:T(8,128)(2,1)S(1)}, bf16[2,160,2048]{2,1,0:T(8,128)(2,1)S(1)}, u32[]{:S(2)}, u32[]{:S(2)}) %collective-permute-start.28) | collective-permute-done | bytes 1310752 | tf_op jit(solution)/shard_map/ppermute | solution.py:300
  222.0 8.7 %collective-permute-done.26 = bf16[2,16,2,32,256]{4,3,2,1,0:T(8,128)(2,1)S(1)} collective-permute-done((bf16[2,16,2,32,256]{4,3,2,1,0:T(8,128)(2,1)S(1)}, bf16[2,16,2,32,256]{4,3,2,1,0:T(8,128)(2,1)S(1)}, u32[]{:S(2)}, u32[]{:S(2)}) %collective-permute-start.26) | collective-permute-done | bytes 1048608 | tf_op jit(solution)/shard_map/ppermute | solution.py:200
  230.7 3.3 %collective-permute-done.27 = bf16[2,16,2,32,256]{4,3,2,1,0:T(8,128)(2,1)S(1)} collective-permute-done((bf16[2,16,2,32,256]{4,3,2,1,0:T(8,128)(2,1)S(1)}, bf16[2,16,2,32,256]{4,3,2,1,0:T(8,128)(2,1)S(1)}, u32[]{:S(2)}, u32[]{:S(2)}) %collective-permute-start.27) | collective-permute-done | bytes 1048608 | tf_op jit(solution)/shard_map/ppermute | solution.py:200
  235.6 1.6 collective-permute-start.29
  237.2 1.9 maximum_select_fusion
  239.1 1.9 maximum_select_fusion.1
  241.1 5.1 %collective-permute-done.32 = bf16[1,16,2,32,256]{4,3,2,1,0:T(8,128)(2,1)S(1)} collective-permute-done((bf16[1,16,2,32,256]{4,3,2,1,0:T(8,128)(2,1)S(1)}, bf16[1,16,2,32,256]{4,3,2,1,0:T(8,128)(2,1)S(1)}, u32[]{:S(2)}, u32[]{:S(2)}) %collective-permute-start.32) | collective-permute-done | bytes 524320 | tf_op jit(solution)/shard_map/ppermute | solution.py:200
  (86 shorter events, 32.5 us)
Async XLA Ops:
  2.5 22.4 %collective-permute-start.1 = (bf16[1024,256]{1,0:T(8,128)(2,1)}, bf16[1024,256]{1,0:T(8,128)(2,1)}, u32[]{:S(2)}, u32[]{:S(2)}) collective-permute-start(bf16[1024,256]{1,0:T(8,128)(2,1)} %constant_dynamic-slice_fusion.1), channel_id=1, source_target_pairs={{2,0},{1,3},{6,4},{5,7},{10,8},{9,11},{14,12},{13,15},{18,16},{17,... | collective-permute-start | bytes 1572872 | tf_op jit(solution)/shard_map/ppermute | solution.py:268
  9.7 21.2 %collective-permute-start.9 = (bf16[1024,256]{1,0:T(8,128)(2,1)}, bf16[1024,256]{1,0:T(8,128)(2,1)}, u32[]{:S(2)}, u32[]{:S(2)}) collective-permute-start(bf16[1024,256]{1,0:T(8,128)(2,1)} %constant_dynamic-slice_fusion), channel_id=1, source_target_pairs={{2,0},{1,3},{6,4},{5,7},{10,8},{9,11},{14,12},{13,15},{18,16},{17,... | collective-permute-start | bytes 1572872 | tf_op jit(solution)/shard_map/ppermute | solution.py:268
  13.8 5.4 %copy-start.5 = (s32[2,8,8]{2,1,0:T(8,128)S(1)}, s32[2,8,8]{2,1,0:T(8,128)}, u32[]{:S(2)}) copy-start(s32[2,8,8]{2,1,0:T(8,128)} %param.8) | copy-start | bytes 1540
  14.0 20.6 %copy-start = (bf16[2,352,2048]{2,1,0:T(8,128)(2,1)}, bf16[2,352,2048]{2,1,0:T(8,128)(2,1)S(1)}, u32[]{:S(2)}) copy-start(bf16[2,352,2048]{2,1,0:T(8,128)(2,1)S(1)} %pad_maximum_fusion.refs_0_) | copy-start | bytes 8650756
  14.0 78.5 %collective-permute-start = (bf16[2,352,2048]{2,1,0:T(8,128)(2,1)S(1)}, bf16[2,352,2048]{2,1,0:T(8,128)(2,1)}, u32[]{:S(2)}, u32[]{:S(2)}) collective-permute-start(bf16[2,352,2048]{2,1,0:T(8,128)(2,1)S(1)} %pad_maximum_fusion.refs_0_), channel_id=1, source_target_pairs={{2,0},{1,3},{6,4},{5,7},{10,8},{9,11},{14,12},{13,15},{18,16},{17,... | collective-permute-start | bytes 8650760 | tf_op jit(solution)/shard_map/ppermute | solution.py:275
  24.9 15.8 %collective-permute-start.2 = (bf16[1024,256]{1,0:T(8,128)(2,1)}, bf16[1024,256]{1,0:T(8,128)(2,1)S(1)}, u32[]{:S(2)}, u32[]{:S(2)}) collective-permute-start(bf16[1024,256]{1,0:T(8,128)(2,1)} %collective-permute-done.1), channel_id=1, source_target_pairs={{0,8},{8,0},{16,24},{24,16},{1,9},{9,1},{17,25},{25,17},{2,10},{10... | collective-permute-start | bytes 1572872 | tf_op jit(solution)/shard_map/ppermute | solution.py:200
  27.7 42.3 %collective-permute-start.5 = (bf16[1024,256]{1,0:T(8,128)(2,1)}, bf16[1024,256]{1,0:T(8,128)(2,1)S(1)}, u32[]{:S(2)}, u32[]{:S(2)}) collective-permute-start(bf16[1024,256]{1,0:T(8,128)(2,1)} %collective-permute-done.1), channel_id=1, source_target_pairs={{0,4},{4,0},{1,5},{5,1},{2,6},{6,2},{3,7},{7,3},{8,12},{12,8},{9,1... | collective-permute-start | bytes 1572872 | tf_op jit(solution)/shard_map/ppermute | solution.py:200
  27.7 28.1 %collective-permute-start.3 = (bf16[1024,256]{1,0:T(8,128)(2,1)}, bf16[1024,256]{1,0:T(8,128)(2,1)S(1)}, u32[]{:S(2)}, u32[]{:S(2)}) collective-permute-start(bf16[1024,256]{1,0:T(8,128)(2,1)} %collective-permute-done.1), channel_id=1, source_target_pairs={{0,16},{8,24},{16,0},{24,8},{1,17},{9,25},{17,1},{25,9},{2,18},{10... | collective-permute-start | bytes 1572872 | tf_op jit(solution)/shard_map/ppermute | solution.py:200
  30.9 22.7 %collective-permute-start.10 = (bf16[1024,256]{1,0:T(8,128)(2,1)}, bf16[1024,256]{1,0:T(8,128)(2,1)S(1)}, u32[]{:S(2)}, u32[]{:S(2)}) collective-permute-start(bf16[1024,256]{1,0:T(8,128)(2,1)} %collective-permute-done.9), channel_id=1, source_target_pairs={{0,16},{8,24},{16,0},{24,8},{1,17},{9,25},{17,1},{25,9},{2,18},{10... | collective-permute-start | bytes 1572872 | tf_op jit(solution)/shard_map/ppermute | solution.py:200
  40.7 16.6 %collective-permute-start.11 = (bf16[1024,256]{1,0:T(8,128)(2,1)}, bf16[1024,256]{1,0:T(8,128)(2,1)S(1)}, u32[]{:S(2)}, u32[]{:S(2)}) collective-permute-start(bf16[1024,256]{1,0:T(8,128)(2,1)} %collective-permute-done.9), channel_id=1, source_target_pairs={{0,8},{8,0},{16,24},{24,16},{1,9},{9,1},{17,25},{25,17},{2,10},{10... | collective-permute-start | bytes 1572872 | tf_op jit(solution)/shard_map/ppermute | solution.py:200
  53.5 13.6 %collective-permute-start.4 = (bf16[1024,256]{1,0:T(8,128)(2,1)S(1)}, bf16[1024,256]{1,0:T(8,128)(2,1)S(1)}, u32[]{:S(2)}, u32[]{:S(2)}) collective-permute-start(bf16[1024,256]{1,0:T(8,128)(2,1)S(1)} %collective-permute-done.2), channel_id=1, source_target_pairs={{0,16},{8,24},{16,0},{24,8},{1,17},{9,25},{17,1},{25,9},{2,18},{10... | collective-permute-start | bytes 1572872 | tf_op jit(solution)/shard_map/ppermute | solution.py:200
  55.9 13.3 %collective-permute-start.12 = (bf16[1024,256]{1,0:T(8,128)(2,1)S(1)}, bf16[1024,256]{1,0:T(8,128)(2,1)S(1)}, u32[]{:S(2)}, u32[]{:S(2)}) collective-permute-start(bf16[1024,256]{1,0:T(8,128)(2,1)S(1)} %collective-permute-done.10), channel_id=1, source_target_pairs={{0,8},{8,0},{16,24},{24,16},{1,9},{9,1},{17,25},{25,17},{2,10},{10... | collective-permute-start | bytes 1572872 | tf_op jit(solution)/shard_map/ppermute | solution.py:200
  57.3 63.8 %collective-permute-start.17 = (bf16[2,160,2048]{2,1,0:T(8,128)(2,1)}, bf16[2,160,2048]{2,1,0:T(8,128)(2,1)}, u32[]{:S(2)}, u32[]{:S(2)}) collective-permute-start(bf16[2,160,2048]{2,1,0:T(8,128)(2,1)} %pad_maximum_fusion.1.refs_1_), channel_id=1, source_target_pairs={{2,0},{1,3},{6,4},{5,7},{10,8},{9,11},{14,12},{13,15},{18,16},{17,... | collective-permute-start | bytes 3932168 | tf_op jit(solution)/shard_map/ppermute | solution.py:277
  67.1 4.3 %collective-permute-start.13 = (bf16[1024,256]{1,0:T(8,128)(2,1)}, bf16[1024,256]{1,0:T(8,128)(2,1)S(1)}, u32[]{:S(2)}, u32[]{:S(2)}) collective-permute-start(bf16[1024,256]{1,0:T(8,128)(2,1)} %collective-permute-done.9), channel_id=1, source_target_pairs={{0,4},{4,0},{1,5},{5,1},{2,6},{6,2},{3,7},{7,3},{8,12},{12,8},{9,1... | collective-permute-start | bytes 1572872 | tf_op jit(solution)/shard_map/ppermute | solution.py:200
  69.2 3.1 %collective-permute-start.6 = (bf16[1024,256]{1,0:T(8,128)(2,1)S(1)}, bf16[1024,256]{1,0:T(8,128)(2,1)S(1)}, u32[]{:S(2)}, u32[]{:S(2)}) collective-permute-start(bf16[1024,256]{1,0:T(8,128)(2,1)S(1)} %collective-permute-done.2), channel_id=1, source_target_pairs={{0,4},{4,0},{1,5},{5,1},{2,6},{6,2},{3,7},{7,3},{8,12},{12,8},{9,1... | collective-permute-start | bytes 1572872 | tf_op jit(solution)/shard_map/ppermute | solution.py:200
  70.0 3.6 %collective-permute-start.7 = (bf16[1024,256]{1,0:T(8,128)(2,1)S(1)}, bf16[1024,256]{1,0:T(8,128)(2,1)S(1)}, u32[]{:S(2)}, u32[]{:S(2)}) collective-permute-start(bf16[1024,256]{1,0:T(8,128)(2,1)S(1)} %collective-permute-done.3), channel_id=1, source_target_pairs={{0,4},{4,0},{1,5},{5,1},{2,6},{6,2},{3,7},{7,3},{8,12},{12,8},{9,1... | collective-permute-start | bytes 1572872 | tf_op jit(solution)/shard_map/ppermute | solution.py:200
  71.4 3.0 %collective-permute-start.14 = (bf16[1024,256]{1,0:T(8,128)(2,1)S(1)}, bf16[1024,256]{1,0:T(8,128)(2,1)S(1)}, u32[]{:S(2)}, u32[]{:S(2)}) collective-permute-start(bf16[1024,256]{1,0:T(8,128)(2,1)S(1)} %collective-permute-done.10), channel_id=1, source_target_pairs={{0,4},{4,0},{1,5},{5,1},{2,6},{6,2},{3,7},{7,3},{8,12},{12,8},{9,1... | collective-permute-start | bytes 1572872 | tf_op jit(solution)/shard_map/ppermute | solution.py:200
  72.2 3.6 %collective-permute-start.15 = (bf16[1024,256]{1,0:T(8,128)(2,1)S(1)}, bf16[1024,256]{1,0:T(8,128)(2,1)S(1)}, u32[]{:S(2)}, u32[]{:S(2)}) collective-permute-start(bf16[1024,256]{1,0:T(8,128)(2,1)S(1)} %collective-permute-done.11), channel_id=1, source_target_pairs={{0,4},{4,0},{1,5},{5,1},{2,6},{6,2},{3,7},{7,3},{8,12},{12,8},{9,1... | collective-permute-start | bytes 1572872 | tf_op jit(solution)/shard_map/ppermute | solution.py:200
  73.6 3.0 %collective-permute-start.8 = (bf16[1024,256]{1,0:T(8,128)(2,1)S(1)}, bf16[1024,256]{1,0:T(8,128)(2,1)S(1)}, u32[]{:S(2)}, u32[]{:S(2)}) collective-permute-start(bf16[1024,256]{1,0:T(8,128)(2,1)S(1)} %collective-permute-done.4), channel_id=1, source_target_pairs={{0,4},{4,0},{1,5},{5,1},{2,6},{6,2},{3,7},{7,3},{8,12},{12,8},{9,1... | collective-permute-start | bytes 1572872 | tf_op jit(solution)/shard_map/ppermute | solution.py:200
  74.5 3.0 %collective-permute-start.16 = (bf16[1024,256]{1,0:T(8,128)(2,1)S(1)}, bf16[1024,256]{1,0:T(8,128)(2,1)S(1)}, u32[]{:S(2)}, u32[]{:S(2)}) collective-permute-start(bf16[1024,256]{1,0:T(8,128)(2,1)S(1)} %collective-permute-done.12), channel_id=1, source_target_pairs={{0,4},{4,0},{1,5},{5,1},{2,6},{6,2},{3,7},{7,3},{8,12},{12,8},{9,1... | collective-permute-start | bytes 1572872 | tf_op jit(solution)/shard_map/ppermute | solution.py:200
  121.1 37.5 %collective-permute-start.18 = (bf16[2,192,2048]{2,1,0:T(8,128)(2,1)}, bf16[2,192,2048]{2,1,0:T(8,128)(2,1)}, u32[]{:S(2)}, u32[]{:S(2)}) collective-permute-start(bf16[2,192,2048]{2,1,0:T(8,128)(2,1)} %get-tuple-element.49), channel_id=1, source_target_pairs={{0,2},{3,1},{4,6},{7,5},{8,10},{11,9},{12,14},{15,13},{16,18},{19,... | collective-permute-start | bytes 4718600 | tf_op jit(solution)/shard_map/ppermute | solution.py:297
  122.6 38.1 %copy-start.3 = (bf16[2,352,2048]{2,1,0:T(8,128)(2,1)S(1)}, bf16[2,352,2048]{2,1,0:T(8,128)(2,1)}, u32[]{:S(2)}) copy-start(bf16[2,352,2048]{2,1,0:T(8,128)(2,1)} %get-tuple-element.45) | copy-start | bytes 8650756
  158.5 7.5 %collective-permute-start.20 = (bf16[2,4,16,2,32,256]{5,4,3,2,1,0:T(8,128)(2,1)}, bf16[2,4,16,2,32,256]{5,4,3,2,1,0:T(8,128)(2,1)}, u32[]{:S(2)}, u32[]{:S(2)}) collective-permute-start(bf16[2,4,16,2,32,256]{5,4,3,2,1,0:T(8,128)(2,1)} %get-tuple-element.64), channel_id=1, source_target_pairs={{0,4},{4,0},{1,5},{5,1},{2,6},{6,2},{3,7},{7,3},{8,12},{12,8},{9,1... | collective-permute-start | bytes 12582920 | tf_op jit(solution)/shard_map/ppermute | solution.py:200
  158.5 15.0 %collective-permute-start.19 = (bf16[2,4,16,2,32,256]{5,4,3,2,1,0:T(8,128)(2,1)}, bf16[2,4,16,2,32,256]{5,4,3,2,1,0:T(8,128)(2,1)}, u32[]{:S(2)}, u32[]{:S(2)}) collective-permute-start(bf16[2,4,16,2,32,256]{5,4,3,2,1,0:T(8,128)(2,1)} %get-tuple-element.62), channel_id=1, source_target_pairs={{0,4},{4,0},{1,5},{5,1},{2,6},{6,2},{3,7},{7,3},{8,12},{12,8},{9,1... | collective-permute-start | bytes 12582920 | tf_op jit(solution)/shard_map/ppermute | solution.py:200
  159.1 1.8 copy-start.6
  159.1 3.4 %copy-start.1 = (bf16[2,4,16,2,32,256]{5,4,3,2,1,0:T(8,128)(2,1)S(1)}, bf16[2,4,16,2,32,256]{5,4,3,2,1,0:T(8,128)(2,1)}, u32[]{:S(2)}) copy-start(bf16[2,4,16,2,32,256]{5,4,3,2,1,0:T(8,128)(2,1)} %get-tuple-element.61) | copy-start | bytes 12582916
  159.1 34.9 %collective-permute-start.23 = (bf16[2,160,2048]{2,1,0:T(8,128)(2,1)}, bf16[2,160,2048]{2,1,0:T(8,128)(2,1)S(1)}, u32[]{:S(2)}, u32[]{:S(2)}) collective-permute-start(bf16[2,160,2048]{2,1,0:T(8,128)(2,1)} %get-tuple-element.65), channel_id=1, source_target_pairs={{0,2},{3,1},{4,6},{7,5},{8,10},{11,9},{12,14},{15,13},{16,18},{19,... | collective-permute-start | bytes 3932168 | tf_op jit(solution)/shard_map/ppermute | solution.py:299
  160.6 2.5 %copy-start.2 = (bf16[2,4,16,2,32,256]{5,4,3,2,1,0:T(8,128)(2,1)S(1)}, bf16[2,4,16,2,32,256]{5,4,3,2,1,0:T(8,128)(2,1)}, u32[]{:S(2)}) copy-start(bf16[2,4,16,2,32,256]{5,4,3,2,1,0:T(8,128)(2,1)} %get-tuple-element.63) | copy-start | bytes 12582916
  160.9 61.2 %collective-permute-start.28 = (bf16[2,160,2048]{2,1,0:T(8,128)(2,1)S(1)}, bf16[2,160,2048]{2,1,0:T(8,128)(2,1)S(1)}, u32[]{:S(2)}, u32[]{:S(2)}) collective-permute-start(bf16[2,160,2048]{2,1,0:T(8,128)(2,1)S(1)} %copy-done.6), channel_id=1, source_target_pairs={{0,2},{3,1},{4,6},{7,5},{8,10},{11,9},{12,14},{15,13},{16,18},{19,... | collective-permute-start | bytes 3932168 | tf_op jit(solution)/shard_map/ppermute | solution.py:300
  163.4 8.2 %copy-start.4 = (bf16[2,160,2048]{2,1,0:T(8,128)(2,1)S(1)}, bf16[2,160,2048]{2,1,0:T(8,128)(2,1)}, u32[]{:S(2)}) copy-start(bf16[2,160,2048]{2,1,0:T(8,128)(2,1)} %get-tuple-element.59) | copy-start | bytes 3932164
  168.6 25.4 %collective-permute-start.22 = (bf16[2,16,2,32,256]{4,3,2,1,0:T(8,128)(2,1)S(1)}, bf16[2,16,2,32,256]{4,3,2,1,0:T(8,128)(2,1)S(1)}, u32[]{:S(2)}, u32[]{:S(2)}) collective-permute-start(bf16[2,16,2,32,256]{4,3,2,1,0:T(8,128)(2,1)S(1)} %get-tuple-element.84), channel_id=1, source_target_pairs={{0,16},{8,24},{16,0},{24,8},{1,17},{9,25},{17,1},{25,9},{2,18},{10... | collective-permute-start | bytes 3145736 | tf_op jit(solution)/shard_map/ppermute | solution.py:200
  170.1 24.9 %collective-permute-start.21 = (bf16[2,16,2,32,256]{4,3,2,1,0:T(8,128)(2,1)S(1)}, bf16[2,16,2,32,256]{4,3,2,1,0:T(8,128)(2,1)S(1)}, u32[]{:S(2)}, u32[]{:S(2)}) collective-permute-start(bf16[2,16,2,32,256]{4,3,2,1,0:T(8,128)(2,1)S(1)} %get-tuple-element.85), channel_id=1, source_target_pairs={{0,8},{8,0},{16,24},{24,16},{1,9},{9,1},{17,25},{25,17},{2,10},{10... | collective-permute-start | bytes 3145736 | tf_op jit(solution)/shard_map/ppermute | solution.py:200
  195.4 14.9 %collective-permute-start.24 = (bf16[1,16,2,32,256]{4,3,2,1,0:T(8,128)(2,1)S(1)}, bf16[1,16,2,32,256]{4,3,2,1,0:T(8,128)(2,1)S(1)}, u32[]{:S(2)}, u32[]{:S(2)}) collective-permute-start(bf16[1,16,2,32,256]{4,3,2,1,0:T(8,128)(2,1)S(1)} %add_convert_fusion.9), channel_id=1, source_target_pairs={{0,8},{8,0},{16,24},{24,16},{1,9},{9,1},{17,25},{25,17},{2,10},{10... | collective-permute-start | bytes 1572872 | tf_op jit(solution)/shard_map/ppermute | solution.py:200
  198.9 14.9 %collective-permute-start.30 = (bf16[1,16,2,32,256]{4,3,2,1,0:T(8,128)(2,1)S(1)}, bf16[1,16,2,32,256]{4,3,2,1,0:T(8,128)(2,1)S(1)}, u32[]{:S(2)}, u32[]{:S(2)}) collective-permute-start(bf16[1,16,2,32,256]{4,3,2,1,0:T(8,128)(2,1)S(1)} %add_convert_fusion.6), channel_id=1, source_target_pairs={{0,16},{8,24},{16,0},{24,8},{1,17},{9,25},{17,1},{25,9},{2,18},{10... | collective-permute-start | bytes 1572872 | tf_op jit(solution)/shard_map/ppermute | solution.py:200
  199.5 31.2 %collective-permute-start.26 = (bf16[2,16,2,32,256]{4,3,2,1,0:T(8,128)(2,1)S(1)}, bf16[2,16,2,32,256]{4,3,2,1,0:T(8,128)(2,1)S(1)}, u32[]{:S(2)}, u32[]{:S(2)}) collective-permute-start(bf16[2,16,2,32,256]{4,3,2,1,0:T(8,128)(2,1)S(1)} %get-tuple-element.70), channel_id=1, source_target_pairs={{0,8},{8,0},{16,24},{24,16},{1,9},{9,1},{17,25},{25,17},{2,10},{10... | collective-permute-start | bytes 3145736 | tf_op jit(solution)/shard_map/ppermute | solution.py:200
  200.1 34.0 %collective-permute-start.27 = (bf16[2,16,2,32,256]{4,3,2,1,0:T(8,128)(2,1)S(1)}, bf16[2,16,2,32,256]{4,3,2,1,0:T(8,128)(2,1)S(1)}, u32[]{:S(2)}, u32[]{:S(2)}) collective-permute-start(bf16[2,16,2,32,256]{4,3,2,1,0:T(8,128)(2,1)S(1)} %get-tuple-element.71), channel_id=1, source_target_pairs={{0,16},{8,24},{16,0},{24,8},{1,17},{9,25},{17,1},{25,9},{2,18},{10... | collective-permute-start | bytes 3145736 | tf_op jit(solution)/shard_map/ppermute | solution.py:200
  210.7 23.3 %collective-permute-start.25 = (bf16[16,2,32,256]{3,2,1,0:T(8,128)(2,1)S(1)}, bf16[16,2,32,256]{3,2,1,0:T(8,128)(2,1)S(1)}, u32[]{:S(2)}, u32[]{:S(2)}) collective-permute-start(bf16[16,2,32,256]{3,2,1,0:T(8,128)(2,1)S(1)} %fusion.6), channel_id=1, source_target_pairs={{0,2},{3,1},{4,6},{7,5},{8,10},{11,9},{12,14},{15,13},{16,18},{19,... | collective-permute-start | bytes 1572872 | tf_op jit(solution)/shard_map/ppermute | solution.py:314
  214.2 33.3 %collective-permute-start.31 = (bf16[16,2,32,256]{3,2,1,0:T(8,128)(2,1)S(1)}, bf16[16,2,32,256]{3,2,1,0:T(8,128)(2,1)S(1)}, u32[]{:S(2)}, u32[]{:S(2)}) collective-permute-start(bf16[16,2,32,256]{3,2,1,0:T(8,128)(2,1)S(1)} %fusion.7), channel_id=1, source_target_pairs={{0,2},{3,1},{4,6},{7,5},{8,10},{11,9},{12,14},{15,13},{16,18},{19,... | collective-permute-start | bytes 1572872 | tf_op jit(solution)/shard_map/ppermute | solution.py:314
  234.5 11.7 %collective-permute-start.32 = (bf16[1,16,2,32,256]{4,3,2,1,0:T(8,128)(2,1)S(1)}, bf16[1,16,2,32,256]{4,3,2,1,0:T(8,128)(2,1)S(1)}, u32[]{:S(2)}, u32[]{:S(2)}) collective-permute-start(bf16[1,16,2,32,256]{4,3,2,1,0:T(8,128)(2,1)S(1)} %add_convert_fusion.4), channel_id=1, source_target_pairs={{0,8},{8,0},{16,24},{24,16},{1,9},{9,1},{17,25},{25,17},{2,10},{10... | collective-permute-start | bytes 1572872 | tf_op jit(solution)/shard_map/ppermute | solution.py:200
  235.6 12.0 %collective-permute-start.29 = (bf16[1,16,2,32,256]{4,3,2,1,0:T(8,128)(2,1)S(1)}, bf16[1,16,2,32,256]{4,3,2,1,0:T(8,128)(2,1)S(1)}, u32[]{:S(2)}, u32[]{:S(2)}) collective-permute-start(bf16[1,16,2,32,256]{4,3,2,1,0:T(8,128)(2,1)S(1)} %add_convert_fusion.7), channel_id=1, source_target_pairs={{0,16},{8,24},{16,0},{24,8},{1,17},{9,25},{17,1},{25,9},{2,18},{10... | collective-permute-start | bytes 1572872 | tf_op jit(solution)/shard_map/ppermute | solution.py:200

commit v5 on v4

--- a/solution.py
+++ b/solution.py
@@ -90,8 +90,9 @@
                 out_acc[s, :, outs[s]] += out[:, s * size : (s + 1) * size]
                 back_acc[s, :, ins[s]] += back[:, s * size : (s + 1) * size]
 
-    pl.when(theirs)(lambda: work_on(*weights[:2], 1))
-    pl.when(jnp.logical_not(theirs))(lambda: work_on(*weights[2:], 0))
+    works = ids[5, 0] != 0
+    pl.when(works & theirs)(lambda: work_on(*weights[:2], 1))
+    pl.when(works & jnp.logical_not(theirs))(lambda: work_on(*weights[2:], 0))
     if last:
         me = ids[4, 0]
         shard = sums[0].shape[4]
@@ -111,8 +112,8 @@
                             e, pl.ds(start, shard), at : at + size
                         ].astype(BF16)
 
-        pl.when(theirs)(lambda: store(*sums[:2], True))
-        pl.when(jnp.logical_not(theirs))(lambda: store(*sums[2:], False))
+        pl.when(works & theirs)(lambda: store(*sums[:2], True))
+        pl.when(works & jnp.logical_not(theirs))(lambda: store(*sums[2:], False))
 
     @pl.when(step == steps - 1)
     def _():
@@ -260,7 +261,7 @@
     works = (group % away % 2 == 0) != (group >= away)
     partner = (group + away) % groups
 
-    first, split = 11 * tok_rows // 16, 3 * tok_rows // 8
+    first, split = 21 * tok_rows // 32, 12 * tok_rows // 32
     lines = hid * 2 * size // shards
 
     def fetch(weight):
@@ -285,9 +286,8 @@
         mine = lax.dynamic_slice_in_dim(flat, group * hid, hid, 1)
         return jnp.concatenate([theirs[::-1], mine], axis=1)
 
-    ids = jnp.concatenate(
-        [block_ids(up_perm), block_ids(down_perm), jnp.full((1, 2 * hid), me, jnp.int32)]
-    )
+    flags = [jnp.full((1, 2 * hid), flag, jnp.int32) for flag in (me, works)]
+    ids = jnp.concatenate([block_ids(up_perm), block_ids(down_perm), *flags])
 
     orders = [dp_bits + seq_bits[1:], dp_bits[::-1] + seq_bits[1:]]
     slots = [slots_of(order, shards) for order in orders]

time: 250 us -> 248 us (level)
  waiting for transfers between devices: 91.2 us -> 120 us
  Pallas kernels: 61.3 us -> 37.8 us
  local copies, waits for them, and re-layouts: 38.2 us -> 32.3 us
  other arithmetic: 17.5 us -> 14.1 us
  starting transfers between devices: 39.8 us -> 42.9 us
    pallas_call x2, Pallas kernels: 61.3 us -> 37.8 us  [layer(): pl.pallas_call(functools.partial(layer_kernel, last, slots), out_shape=ou...]
    ppermute x1, waiting for transfers between devices: 3.2 us -> 16.6 us  [on_device(): early = lax.ppermute(early, 'tensor', back)]
    ppermute x1, waiting for transfers between devices: 0.01 us -> 12.4 us  [on_device(): far.append(lax.ppermute(later, 'tensor', into))]
    ppermute x24, waiting for transfers between devices: 48 us -> 42.2 us  [hop(): lax.ppermute(block, axis, [(i, i ^ bit) for i in range(lax.axis_size(axis...]
    ppermute x2, waiting for transfers between devices: 1.61 us -> 5.17 us  [fetch(): return lax.ppermute(shard, 'tensor', into)]
    slice x4, local copies, waits for them, and re-layouts: 4.04 us -> 1.01 us  [halve(): return ([term[:half] for term in terms], upper, bit)]
    convert_element_type x6, other arithmetic: 6.21 us -> 3.39 us  [halve(): upper = total([term[half:] for term in terms]).astype(BF16)]
    ppermute x1, starting transfers between devices: 2.34 us -> 5.09 us  [on_device(): far.append(lax.ppermute(later, 'tensor', into))]
  transfers between devices with their start and end apart: 33 -> 33, of which waited for: 15 -> 20; matrix products, arithmetic and copies ran while one was open for 21% -> 17% of each run, Pallas kernels for 25% -> 15%
where the time goes in v5:
time: 248 us
  waiting for transfers between devices  120 us (48%)
  starting transfers between devices  42.9 us (17%)
  Pallas kernels  37.8 us (15%)
  local copies, waits for them, and re-layouts  32.3 us (13%)
  other arithmetic  14.1 us (6%)
    ppermute x24, waiting for transfers between devices, hop(): lax.ppermute(block, axis, [(i, i ^ bit) for i in range(lax.axis_size(axis...  42.2 us
    pallas_call x2, Pallas kernels, layer(): pl.pallas_call(functools.partial(layer_kernel, last, slots), out_shape=ou...  37.8 us
    ppermute x24, starting transfers between devices, hop(): lax.ppermute(block, axis, [(i, i ^ bit) for i in range(lax.axis_size(axis...  20.5 us
    ppermute x1, waiting for transfers between devices, on_device(): middle = lax.ppermute(middle, 'tensor', back)  17.6 us
    ppermute x1, waiting for transfers between devices, on_device(): early = lax.ppermute(early, 'tensor', back)  16.6 us
    dynamic_update_slice x16, local copies, waits for them, and re-layouts, gather(): table = lax.dynamic_update_slice_in_dim(table, part[None], place ^ me, 0)  15.5 us
    ppermute x1, waiting for transfers between devices, on_device(): far = [lax.ppermute(near[0], 'tensor', into)]  15.1 us
    ppermute x1, waiting for transfers between devices, on_device(): far.append(lax.ppermute(later, 'tensor', into))  12.4 us
  transfers between devices with their start and end apart: 33, of which 20 were waited for; matrix products, arithmetic and copies ran while one was open for 17% of the time, Pallas kernels for 15%

profile of v5, /device:TPU:8, one launch (start us, length us, event | category | flops | bytes accessed | tf_op | source)
XLA Modules:
  0.0 247.8 jit_solution(214096745889433534)
XLA Ops:
  0.6 1.9 constant_dynamic-slice_fusion.1
  2.5 5.3 %collective-permute-start.1 = (bf16[1024,256]{1,0:T(8,128)(2,1)}, bf16[1024,256]{1,0:T(8,128)(2,1)}, u32[]{:S(2)}, u32[]{:S(2)}) collective-permute-start(bf16[1024,256]{1,0:T(8,128)(2,1)} %constant_dynamic-slice_fusion.1), channel_id=1, source_target_pairs={{2,0},{1,3},{6,4},{5,7},{10,8},{9,11},{14,12},{13,15},{18,16},{17,... | collective-permute-start | bytes 1572872 | tf_op jit(solution)/shard_map/ppermute | solution.py:269
  7.8 1.9 constant_dynamic-slice_fusion
  9.7 2.1 collective-permute-start.9
  11.8 1.9 slice_bitcast_fusion.2
  14.0 2.9 %collective-permute-start = (bf16[2,336,2048]{2,1,0:T(8,128)(2,1)S(1)}, bf16[2,336,2048]{2,1,0:T(8,128)(2,1)}, u32[]{:S(2)}, u32[]{:S(2)}) collective-permute-start(bf16[2,336,2048]{2,1,0:T(8,128)(2,1)S(1)} %pad_maximum_fusion.refs_0_), channel_id=1, source_target_pairs={{2,0},{1,3},{6,4},{5,7},{10,8},{9,11},{14,12},{13,15},{18,16},{17,... | collective-permute-start | bytes 8257544 | tf_op jit(solution)/shard_map/ppermute | solution.py:276
  16.9 2.3 slice_bitcast_fusion.18
  19.7 2.3 pad_maximum_fusion.1.refs_1_
  22.0 1.5 collective-permute-start.2
  24.2 1.5 collective-permute-start.3
  25.7 5.2 %collective-permute-done.9 = bf16[1024,256]{1,0:T(8,128)(2,1)} collective-permute-done((bf16[1024,256]{1,0:T(8,128)(2,1)}, bf16[1024,256]{1,0:T(8,128)(2,1)}, u32[]{:S(2)}, u32[]{:S(2)}) %collective-permute-start.9) | collective-permute-done | bytes 524320 | tf_op jit(solution)/shard_map/ppermute | solution.py:269
  30.9 1.5 collective-permute-start.10
  32.4 2.3 broadcast.9.clone
  34.7 1.9 bitcast_dynamic-update-slice_fusion.15
  36.5 2.2 broadcast.9.clone.1
  38.8 1.9 bitcast_dynamic-update-slice_fusion.7
  40.6 1.5 collective-permute-start.11
  43.1 6.9 %collective-permute-done.10 = bf16[1024,256]{1,0:T(8,128)(2,1)S(1)} collective-permute-done((bf16[1024,256]{1,0:T(8,128)(2,1)}, bf16[1024,256]{1,0:T(8,128)(2,1)S(1)}, u32[]{:S(2)}, u32[]{:S(2)}) %collective-permute-start.10) | collective-permute-done | bytes 524320 | tf_op jit(solution)/shard_map/ppermute | solution.py:201
  50.0 1.5 collective-permute-start.4
  53.7 5.1 %collective-permute-start.17 = (bf16[2,176,2048]{2,1,0:T(8,128)(2,1)}, bf16[2,176,2048]{2,1,0:T(8,128)(2,1)}, u32[]{:S(2)}, u32[]{:S(2)}) collective-permute-start(bf16[2,176,2048]{2,1,0:T(8,128)(2,1)} %pad_maximum_fusion.1.refs_1_), channel_id=1, source_target_pairs={{2,0},{1,3},{6,4},{5,7},{10,8},{9,11},{14,12},{13,15},{18,16},{17,... | collective-permute-start | bytes 4325384 | tf_op jit(solution)/shard_map/ppermute | solution.py:278
  59.6 3.9 %collective-permute-done.4 = bf16[1024,256]{1,0:T(8,128)(2,1)S(1)} collective-permute-done((bf16[1024,256]{1,0:T(8,128)(2,1)S(1)}, bf16[1024,256]{1,0:T(8,128)(2,1)S(1)}, u32[]{:S(2)}, u32[]{:S(2)}) %collective-permute-start.4) | collective-permute-done | bytes 524320 | tf_op jit(solution)/shard_map/ppermute | solution.py:201
  74.7 15.1 %collective-permute-done.refs_1_.refs_2_ = bf16[2,336,2048]{2,1,0:T(8,128)(2,1)} collective-permute-done((bf16[2,336,2048]{2,1,0:T(8,128)(2,1)S(1)}, bf16[2,336,2048]{2,1,0:T(8,128)(2,1)}, u32[]{:S(2)}, u32[]{:S(2)}) %collective-permute-start) | collective-permute-done | bytes 2752544 | tf_op jit(solution)/shard_map/ppermute | solution.py:276
  89.7 17.5 %shard_map.93 = (bf16[2,336,2048]{2,1,0:T(8,128)(2,1)}, bf16[2,192,2048]{2,1,0:T(8,128)(2,1)}, bf16[2,144,2048]{2,1,0:T(8,128)(2,1)}, bf16[32,336,256]{2,1,0:T(8,128)(2,1)}, bf16[32,336,256]{2,1,0:T(8,128)(2,1)}) custom-call(s32[6,32]{1,0:T(8,128)} %add_add_fusion.ids, bf16[2,336,2048]{2,1,0:T(8,128)(2,1)} %copy-done, ...), custom_call_target="tpu_custom_call" | custom-call | tf_op jit(solution)/shard_map/pallas_call | solution.py:181
  107.2 12.4 %collective-permute-done.17.refs_3_ = bf16[2,176,2048]{2,1,0:T(8,128)(2,1)} collective-permute-done((bf16[2,176,2048]{2,1,0:T(8,128)(2,1)}, bf16[2,176,2048]{2,1,0:T(8,128)(2,1)}, u32[]{:S(2)}, u32[]{:S(2)}) %collective-permute-start.17) | collective-permute-done | bytes 1441824 | tf_op jit(solution)/shard_map/ppermute | solution.py:278
  119.6 1.5 collective-permute-start.18
  121.1 20.3 %shard_map.94 = (bf16[2,176,2048]{2,1,0:T(8,128)(2,1)}, bf16[2,176,2048]{2,1,0:T(8,128)(2,1)}, bf16[2,4,16,2,32,256]{5,4,3,2,1,0:T(8,128)(2,1)}, bf16[2,4,16,2,3...) custom-call(s32[6,32]{1,0:T(8,128)} %add_add_fusion.ids, ...), custom_call_target="tpu_custom_call" | custom-call | tf_op jit(solution)/shard_map/pallas_call | solution.py:181
  141.4 16.6 %collective-permute-done.18 = bf16[2,192,2048]{2,1,0:T(8,128)(2,1)S(1)} collective-permute-done((bf16[2,192,2048]{2,1,0:T(8,128)(2,1)}, bf16[2,192,2048]{2,1,0:T(8,128)(2,1)S(1)}, u32[]{:S(2)}, u32[]{:S(2)}) %collective-permute-start.18) | collective-permute-done | bytes 1572896 | tf_op jit(solution)/shard_map/ppermute | solution.py:297
  159.8 2.2 slice_bitcast_fusion
  162.1 1.4 collective-permute-start.28
  166.5 1.6 collective-permute-start.22
  168.0 1.5 collective-permute-start.21
  172.5 17.6 %collective-permute-done.23 = bf16[2,144,2048]{2,1,0:T(8,128)(2,1)S(1)} collective-permute-done((bf16[2,144,2048]{2,1,0:T(8,128)(2,1)S(1)}, bf16[2,144,2048]{2,1,0:T(8,128)(2,1)S(1)}, u32[]{:S(2)}, u32[]{:S(2)}) %collective-permute-start.23) | collective-permute-done | bytes 1179680 | tf_op jit(solution)/shard_map/ppermute | solution.py:299
  190.1 1.6 collective-permute-done.22
  193.3 1.6 collective-permute-start.24
  196.4 1.5 collective-permute-start.27
  197.9 10.3 %collective-permute-done.24 = bf16[1,16,2,32,256]{4,3,2,1,0:T(8,128)(2,1)S(1)} collective-permute-done((bf16[1,16,2,32,256]{4,3,2,1,0:T(8,128)(2,1)S(1)}, bf16[1,16,2,32,256]{4,3,2,1,0:T(8,128)(2,1)S(1)}, u32[]{:S(2)}, u32[]{:S(2)}) %collective-permute-start.24) | collective-permute-done | bytes 524320 | tf_op jit(solution)/shard_map/ppermute | solution.py:201
  210.6 1.5 collective-permute-start.31
  212.1 8.9 %collective-permute-done.28 = bf16[2,176,2048]{2,1,0:T(8,128)(2,1)S(1)} collective-permute-done((bf16[2,176,2048]{2,1,0:T(8,128)(2,1)}, bf16[2,176,2048]{2,1,0:T(8,128)(2,1)S(1)}, u32[]{:S(2)}, u32[]{:S(2)}) %collective-permute-start.28) | collective-permute-done | bytes 1441824 | tf_op jit(solution)/shard_map/ppermute | solution.py:300
  221.0 7.6 %collective-permute-done.26 = bf16[2,16,2,32,256]{4,3,2,1,0:T(8,128)(2,1)S(1)} collective-permute-done((bf16[2,16,2,32,256]{4,3,2,1,0:T(8,128)(2,1)S(1)}, bf16[2,16,2,32,256]{4,3,2,1,0:T(8,128)(2,1)S(1)}, u32[]{:S(2)}, u32[]{:S(2)}) %collective-permute-start.26) | collective-permute-done | bytes 1048608 | tf_op jit(solution)/shard_map/ppermute | solution.py:201
  228.6 1.8 collective-permute-done.27
  230.4 1.8 collective-permute-done.25
  232.7 1.6 collective-permute-start.32
  234.6 1.6 collective-permute-start.29
  236.1 1.9 maximum_select_fusion
  238.1 1.9 maximum_select_fusion.1
  240.0 4.8 %collective-permute-done.32 = bf16[1,16,2,32,256]{4,3,2,1,0:T(8,128)(2,1)S(1)} collective-permute-done((bf16[1,16,2,32,256]{4,3,2,1,0:T(8,128)(2,1)S(1)}, bf16[1,16,2,32,256]{4,3,2,1,0:T(8,128)(2,1)S(1)}, u32[]{:S(2)}, u32[]{:S(2)}) %collective-permute-start.32) | collective-permute-done | bytes 524320 | tf_op jit(solution)/shard_map/ppermute | solution.py:201
  244.8 1.4 fusion.4
  246.4 1.4 fusion.5
  (91 shorter events, 30.5 us)
Async XLA Ops:
  2.5 19.5 %collective-permute-start.1 = (bf16[1024,256]{1,0:T(8,128)(2,1)}, bf16[1024,256]{1,0:T(8,128)(2,1)}, u32[]{:S(2)}, u32[]{:S(2)}) collective-permute-start(bf16[1024,256]{1,0:T(8,128)(2,1)} %constant_dynamic-slice_fusion.1), channel_id=1, source_target_pairs={{2,0},{1,3},{6,4},{5,7},{10,8},{9,11},{14,12},{13,15},{18,16},{17,... | collective-permute-start | bytes 1572872 | tf_op jit(solution)/shard_map/ppermute | solution.py:269
  9.7 21.2 %collective-permute-start.9 = (bf16[1024,256]{1,0:T(8,128)(2,1)}, bf16[1024,256]{1,0:T(8,128)(2,1)}, u32[]{:S(2)}, u32[]{:S(2)}) collective-permute-start(bf16[1024,256]{1,0:T(8,128)(2,1)} %constant_dynamic-slice_fusion), channel_id=1, source_target_pairs={{2,0},{1,3},{6,4},{5,7},{10,8},{9,11},{14,12},{13,15},{18,16},{17,... | collective-permute-start | bytes 1572872 | tf_op jit(solution)/shard_map/ppermute | solution.py:269
  13.7 5.5 %copy-start.6 = (s32[2,8,8]{2,1,0:T(8,128)S(1)}, s32[2,8,8]{2,1,0:T(8,128)}, u32[]{:S(2)}) copy-start(s32[2,8,8]{2,1,0:T(8,128)} %param.8) | copy-start | bytes 1540
  13.7 5.6 %copy-start.7 = (s32[2,8,8]{2,1,0:T(8,128)S(1)}, s32[2,8,8]{2,1,0:T(8,128)}, u32[]{:S(2)}) copy-start(s32[2,8,8]{2,1,0:T(8,128)} %param.9) | copy-start | bytes 1540
  14.0 20.7 %copy-start = (bf16[2,336,2048]{2,1,0:T(8,128)(2,1)}, bf16[2,336,2048]{2,1,0:T(8,128)(2,1)S(1)}, u32[]{:S(2)}) copy-start(bf16[2,336,2048]{2,1,0:T(8,128)(2,1)S(1)} %pad_maximum_fusion.refs_0_) | copy-start | bytes 8257540
  14.0 75.7 %collective-permute-start = (bf16[2,336,2048]{2,1,0:T(8,128)(2,1)S(1)}, bf16[2,336,2048]{2,1,0:T(8,128)(2,1)}, u32[]{:S(2)}, u32[]{:S(2)}) collective-permute-start(bf16[2,336,2048]{2,1,0:T(8,128)(2,1)S(1)} %pad_maximum_fusion.refs_0_), channel_id=1, source_target_pairs={{2,0},{1,3},{6,4},{5,7},{10,8},{9,11},{14,12},{13,15},{18,16},{17,... | collective-permute-start | bytes 8257544 | tf_op jit(solution)/shard_map/ppermute | solution.py:276
  22.0 18.6 %collective-permute-start.2 = (bf16[1024,256]{1,0:T(8,128)(2,1)}, bf16[1024,256]{1,0:T(8,128)(2,1)S(1)}, u32[]{:S(2)}, u32[]{:S(2)}) collective-permute-start(bf16[1024,256]{1,0:T(8,128)(2,1)} %collective-permute-done.1), channel_id=1, source_target_pairs={{0,8},{8,0},{16,24},{24,16},{1,9},{9,1},{17,25},{25,17},{2,10},{10... | collective-permute-start | bytes 1572872 | tf_op jit(solution)/shard_map/ppermute | solution.py:201
  24.2 42.3 %collective-permute-start.5 = (bf16[1024,256]{1,0:T(8,128)(2,1)}, bf16[1024,256]{1,0:T(8,128)(2,1)S(1)}, u32[]{:S(2)}, u32[]{:S(2)}) collective-permute-start(bf16[1024,256]{1,0:T(8,128)(2,1)} %collective-permute-done.1), channel_id=1, source_target_pairs={{0,4},{4,0},{1,5},{5,1},{2,6},{6,2},{3,7},{7,3},{8,12},{12,8},{9,1... | collective-permute-start | bytes 1572872 | tf_op jit(solution)/shard_map/ppermute | solution.py:201
  24.2 28.1 %collective-permute-start.3 = (bf16[1024,256]{1,0:T(8,128)(2,1)}, bf16[1024,256]{1,0:T(8,128)(2,1)S(1)}, u32[]{:S(2)}, u32[]{:S(2)}) collective-permute-start(bf16[1024,256]{1,0:T(8,128)(2,1)} %collective-permute-done.1), channel_id=1, source_target_pairs={{0,16},{8,24},{16,0},{24,8},{1,17},{9,25},{17,1},{25,9},{2,18},{10... | collective-permute-start | bytes 1572872 | tf_op jit(solution)/shard_map/ppermute | solution.py:201
  30.9 19.1 %collective-permute-start.10 = (bf16[1024,256]{1,0:T(8,128)(2,1)}, bf16[1024,256]{1,0:T(8,128)(2,1)S(1)}, u32[]{:S(2)}, u32[]{:S(2)}) collective-permute-start(bf16[1024,256]{1,0:T(8,128)(2,1)} %collective-permute-done.9), channel_id=1, source_target_pairs={{0,16},{8,24},{16,0},{24,8},{1,17},{9,25},{17,1},{25,9},{2,18},{10... | collective-permute-start | bytes 1572872 | tf_op jit(solution)/shard_map/ppermute | solution.py:201
  40.6 13.0 %collective-permute-start.11 = (bf16[1024,256]{1,0:T(8,128)(2,1)}, bf16[1024,256]{1,0:T(8,128)(2,1)S(1)}, u32[]{:S(2)}, u32[]{:S(2)}) collective-permute-start(bf16[1024,256]{1,0:T(8,128)(2,1)} %collective-permute-done.9), channel_id=1, source_target_pairs={{0,8},{8,0},{16,24},{24,16},{1,9},{9,1},{17,25},{25,17},{2,10},{10... | collective-permute-start | bytes 1572872 | tf_op jit(solution)/shard_map/ppermute | solution.py:201
  50.0 13.6 %collective-permute-start.4 = (bf16[1024,256]{1,0:T(8,128)(2,1)S(1)}, bf16[1024,256]{1,0:T(8,128)(2,1)S(1)}, u32[]{:S(2)}, u32[]{:S(2)}) collective-permute-start(bf16[1024,256]{1,0:T(8,128)(2,1)S(1)} %collective-permute-done.2), channel_id=1, source_target_pairs={{0,16},{8,24},{16,0},{24,8},{1,17},{9,25},{17,1},{25,9},{2,18},{10... | collective-permute-start | bytes 1572872 | tf_op jit(solution)/shard_map/ppermute | solution.py:201
  52.3 13.3 %collective-permute-start.12 = (bf16[1024,256]{1,0:T(8,128)(2,1)S(1)}, bf16[1024,256]{1,0:T(8,128)(2,1)S(1)}, u32[]{:S(2)}, u32[]{:S(2)}) collective-permute-start(bf16[1024,256]{1,0:T(8,128)(2,1)S(1)} %collective-permute-done.10), channel_id=1, source_target_pairs={{0,8},{8,0},{16,24},{24,16},{1,9},{9,1},{17,25},{25,17},{2,10},{10... | collective-permute-start | bytes 1572872 | tf_op jit(solution)/shard_map/ppermute | solution.py:201
  53.7 65.9 %collective-permute-start.17 = (bf16[2,176,2048]{2,1,0:T(8,128)(2,1)}, bf16[2,176,2048]{2,1,0:T(8,128)(2,1)}, u32[]{:S(2)}, u32[]{:S(2)}) collective-permute-start(bf16[2,176,2048]{2,1,0:T(8,128)(2,1)} %pad_maximum_fusion.1.refs_1_), channel_id=1, source_target_pairs={{2,0},{1,3},{6,4},{5,7},{10,8},{9,11},{14,12},{13,15},{18,16},{17,... | collective-permute-start | bytes 4325384 | tf_op jit(solution)/shard_map/ppermute | solution.py:278
  63.5 4.3 %collective-permute-start.13 = (bf16[1024,256]{1,0:T(8,128)(2,1)}, bf16[1024,256]{1,0:T(8,128)(2,1)S(1)}, u32[]{:S(2)}, u32[]{:S(2)}) collective-permute-start(bf16[1024,256]{1,0:T(8,128)(2,1)} %collective-permute-done.9), channel_id=1, source_target_pairs={{0,4},{4,0},{1,5},{5,1},{2,6},{6,2},{3,7},{7,3},{8,12},{12,8},{9,1... | collective-permute-start | bytes 1572872 | tf_op jit(solution)/shard_map/ppermute | solution.py:201
  65.6 3.1 %collective-permute-start.6 = (bf16[1024,256]{1,0:T(8,128)(2,1)S(1)}, bf16[1024,256]{1,0:T(8,128)(2,1)S(1)}, u32[]{:S(2)}, u32[]{:S(2)}) collective-permute-start(bf16[1024,256]{1,0:T(8,128)(2,1)S(1)} %collective-permute-done.2), channel_id=1, source_target_pairs={{0,4},{4,0},{1,5},{5,1},{2,6},{6,2},{3,7},{7,3},{8,12},{12,8},{9,1... | collective-permute-start | bytes 1572872 | tf_op jit(solution)/shard_map/ppermute | solution.py:201
  66.4 3.5 %collective-permute-start.7 = (bf16[1024,256]{1,0:T(8,128)(2,1)S(1)}, bf16[1024,256]{1,0:T(8,128)(2,1)S(1)}, u32[]{:S(2)}, u32[]{:S(2)}) collective-permute-start(bf16[1024,256]{1,0:T(8,128)(2,1)S(1)} %collective-permute-done.3), channel_id=1, source_target_pairs={{0,4},{4,0},{1,5},{5,1},{2,6},{6,2},{3,7},{7,3},{8,12},{12,8},{9,1... | collective-permute-start | bytes 1572872 | tf_op jit(solution)/shard_map/ppermute | solution.py:201
  67.8 3.1 %collective-permute-start.14 = (bf16[1024,256]{1,0:T(8,128)(2,1)S(1)}, bf16[1024,256]{1,0:T(8,128)(2,1)S(1)}, u32[]{:S(2)}, u32[]{:S(2)}) collective-permute-start(bf16[1024,256]{1,0:T(8,128)(2,1)S(1)} %collective-permute-done.10), channel_id=1, source_target_pairs={{0,4},{4,0},{1,5},{5,1},{2,6},{6,2},{3,7},{7,3},{8,12},{12,8},{9,1... | collective-permute-start | bytes 1572872 | tf_op jit(solution)/shard_map/ppermute | solution.py:201
  68.6 3.5 %collective-permute-start.15 = (bf16[1024,256]{1,0:T(8,128)(2,1)S(1)}, bf16[1024,256]{1,0:T(8,128)(2,1)S(1)}, u32[]{:S(2)}, u32[]{:S(2)}) collective-permute-start(bf16[1024,256]{1,0:T(8,128)(2,1)S(1)} %collective-permute-done.11), channel_id=1, source_target_pairs={{0,4},{4,0},{1,5},{5,1},{2,6},{6,2},{3,7},{7,3},{8,12},{12,8},{9,1... | collective-permute-start | bytes 1572872 | tf_op jit(solution)/shard_map/ppermute | solution.py:201
  70.0 3.0 %collective-permute-start.8 = (bf16[1024,256]{1,0:T(8,128)(2,1)S(1)}, bf16[1024,256]{1,0:T(8,128)(2,1)S(1)}, u32[]{:S(2)}, u32[]{:S(2)}) collective-permute-start(bf16[1024,256]{1,0:T(8,128)(2,1)S(1)} %collective-permute-done.4), channel_id=1, source_target_pairs={{0,4},{4,0},{1,5},{5,1},{2,6},{6,2},{3,7},{7,3},{8,12},{12,8},{9,1... | collective-permute-start | bytes 1572872 | tf_op jit(solution)/shard_map/ppermute | solution.py:201
  70.9 3.0 %collective-permute-start.16 = (bf16[1024,256]{1,0:T(8,128)(2,1)S(1)}, bf16[1024,256]{1,0:T(8,128)(2,1)S(1)}, u32[]{:S(2)}, u32[]{:S(2)}) collective-permute-start(bf16[1024,256]{1,0:T(8,128)(2,1)S(1)} %collective-permute-done.12), channel_id=1, source_target_pairs={{0,4},{4,0},{1,5},{5,1},{2,6},{6,2},{3,7},{7,3},{8,12},{12,8},{9,1... | collective-permute-start | bytes 1572872 | tf_op jit(solution)/shard_map/ppermute | solution.py:201
  119.6 38.4 %collective-permute-start.18 = (bf16[2,192,2048]{2,1,0:T(8,128)(2,1)}, bf16[2,192,2048]{2,1,0:T(8,128)(2,1)S(1)}, u32[]{:S(2)}, u32[]{:S(2)}) collective-permute-start(bf16[2,192,2048]{2,1,0:T(8,128)(2,1)} %get-tuple-element.49), channel_id=1, source_target_pairs={{0,2},{3,1},{4,6},{7,5},{8,10},{11,9},{12,14},{15,13},{16,18},{19,... | collective-permute-start | bytes 4718600 | tf_op jit(solution)/shard_map/ppermute | solution.py:297
  121.1 37.4 %copy-start.8 = (bf16[2,144,2048]{2,1,0:T(8,128)(2,1)S(1)}, bf16[2,144,2048]{2,1,0:T(8,128)(2,1)}, u32[]{:S(2)}) copy-start(bf16[2,144,2048]{2,1,0:T(8,128)(2,1)} %get-tuple-element.65) | copy-start | bytes 3538948
  141.4 22.1 %copy-start.1 = (bf16[2,4,16,2,32,256]{5,4,3,2,1,0:T(8,128)(2,1)S(1)}, bf16[2,4,16,2,32,256]{5,4,3,2,1,0:T(8,128)(2,1)}, u32[]{:S(2)}) copy-start(bf16[2,4,16,2,32,256]{5,4,3,2,1,0:T(8,128)(2,1)} %get-tuple-element.61) | copy-start | bytes 12582916
  158.0 1.8 copy-start.3
  158.0 7.4 %collective-permute-start.20 = (bf16[2,4,16,2,32,256]{5,4,3,2,1,0:T(8,128)(2,1)}, bf16[2,4,16,2,32,256]{5,4,3,2,1,0:T(8,128)(2,1)S(1)}, u32[]{:S(2)}, u32[]{:S(2)}) collective-permute-start(bf16[2,4,16,2,32,256]{5,4,3,2,1,0:T(8,128)(2,1)} %get-tuple-element.64), channel_id=1, source_target_pairs={{0,4},{4,0},{1,5},{5,1},{2,6},{6,2},{3,7},{7,3},{8,12},{12,8},{9,1... | collective-permute-start | bytes 12582920 | tf_op jit(solution)/shard_map/ppermute | solution.py:201
  158.0 13.4 %collective-permute-start.19 = (bf16[2,4,16,2,32,256]{5,4,3,2,1,0:T(8,128)(2,1)}, bf16[2,4,16,2,32,256]{5,4,3,2,1,0:T(8,128)(2,1)S(1)}, u32[]{:S(2)}, u32[]{:S(2)}) collective-permute-start(bf16[2,4,16,2,32,256]{5,4,3,2,1,0:T(8,128)(2,1)} %get-tuple-element.62), channel_id=1, source_target_pairs={{0,4},{4,0},{1,5},{5,1},{2,6},{6,2},{3,7},{7,3},{8,12},{12,8},{9,1... | collective-permute-start | bytes 12582920 | tf_op jit(solution)/shard_map/ppermute | solution.py:201
  158.5 31.6 %collective-permute-start.23 = (bf16[2,144,2048]{2,1,0:T(8,128)(2,1)S(1)}, bf16[2,144,2048]{2,1,0:T(8,128)(2,1)S(1)}, u32[]{:S(2)}, u32[]{:S(2)}) collective-permute-start(bf16[2,144,2048]{2,1,0:T(8,128)(2,1)S(1)} %copy-done.8), channel_id=1, source_target_pairs={{0,2},{3,1},{4,6},{7,5},{8,10},{11,9},{12,14},{15,13},{16,18},{19,... | collective-permute-start | bytes 3538952 | tf_op jit(solution)/shard_map/ppermute | solution.py:299
  159.8 3.9 %copy-start.2 = (bf16[2,4,16,2,32,256]{5,4,3,2,1,0:T(8,128)(2,1)S(1)}, bf16[2,4,16,2,32,256]{5,4,3,2,1,0:T(8,128)(2,1)}, u32[]{:S(2)}) copy-start(bf16[2,4,16,2,32,256]{5,4,3,2,1,0:T(8,128)(2,1)} %get-tuple-element.63) | copy-start | bytes 12582916
  162.0 2.0 copy-start.4
  162.1 59.0 %collective-permute-start.28 = (bf16[2,176,2048]{2,1,0:T(8,128)(2,1)}, bf16[2,176,2048]{2,1,0:T(8,128)(2,1)S(1)}, u32[]{:S(2)}, u32[]{:S(2)}) collective-permute-start(bf16[2,176,2048]{2,1,0:T(8,128)(2,1)} %get-tuple-element.72), channel_id=1, source_target_pairs={{0,2},{3,1},{4,6},{7,5},{8,10},{11,9},{12,14},{15,13},{16,18},{19,... | collective-permute-start | bytes 4325384 | tf_op jit(solution)/shard_map/ppermute | solution.py:300
  164.1 5.5 %copy-start.5 = (bf16[2,176,2048]{2,1,0:T(8,128)(2,1)S(1)}, bf16[2,176,2048]{2,1,0:T(8,128)(2,1)}, u32[]{:S(2)}) copy-start(bf16[2,176,2048]{2,1,0:T(8,128)(2,1)} %get-tuple-element.59) | copy-start | bytes 4325380
  166.5 25.3 %collective-permute-start.22 = (bf16[2,16,2,32,256]{4,3,2,1,0:T(8,128)(2,1)S(1)}, bf16[2,16,2,32,256]{4,3,2,1,0:T(8,128)(2,1)S(1)}, u32[]{:S(2)}, u32[]{:S(2)}) collective-permute-start(bf16[2,16,2,32,256]{4,3,2,1,0:T(8,128)(2,1)S(1)} %get-tuple-element.84), channel_id=1, source_target_pairs={{0,16},{8,24},{16,0},{24,8},{1,17},{9,25},{17,1},{25,9},{2,18},{10... | collective-permute-start | bytes 3145736 | tf_op jit(solution)/shard_map/ppermute | solution.py:201
  168.0 24.9 %collective-permute-start.21 = (bf16[2,16,2,32,256]{4,3,2,1,0:T(8,128)(2,1)S(1)}, bf16[2,16,2,32,256]{4,3,2,1,0:T(8,128)(2,1)S(1)}, u32[]{:S(2)}, u32[]{:S(2)}) collective-permute-start(bf16[2,16,2,32,256]{4,3,2,1,0:T(8,128)(2,1)S(1)} %get-tuple-element.85), channel_id=1, source_target_pairs={{0,8},{8,0},{16,24},{24,16},{1,9},{9,1},{17,25},{25,17},{2,10},{10... | collective-permute-start | bytes 3145736 | tf_op jit(solution)/shard_map/ppermute | solution.py:201
  193.3 14.9 %collective-permute-start.24 = (bf16[1,16,2,32,256]{4,3,2,1,0:T(8,128)(2,1)S(1)}, bf16[1,16,2,32,256]{4,3,2,1,0:T(8,128)(2,1)S(1)}, u32[]{:S(2)}, u32[]{:S(2)}) collective-permute-start(bf16[1,16,2,32,256]{4,3,2,1,0:T(8,128)(2,1)S(1)} %add_convert_fusion.9), channel_id=1, source_target_pairs={{0,8},{8,0},{16,24},{24,16},{1,9},{9,1},{17,25},{25,17},{2,10},{10... | collective-permute-start | bytes 1572872 | tf_op jit(solution)/shard_map/ppermute | solution.py:201
  195.3 14.9 %collective-permute-start.30 = (bf16[1,16,2,32,256]{4,3,2,1,0:T(8,128)(2,1)S(1)}, bf16[1,16,2,32,256]{4,3,2,1,0:T(8,128)(2,1)S(1)}, u32[]{:S(2)}, u32[]{:S(2)}) collective-permute-start(bf16[1,16,2,32,256]{4,3,2,1,0:T(8,128)(2,1)S(1)} %add_convert_fusion.6), channel_id=1, source_target_pairs={{0,16},{8,24},{16,0},{24,8},{1,17},{9,25},{17,1},{25,9},{2,18},{10... | collective-permute-start | bytes 1572872 | tf_op jit(solution)/shard_map/ppermute | solution.py:201
  195.9 32.7 %collective-permute-start.26 = (bf16[2,16,2,32,256]{4,3,2,1,0:T(8,128)(2,1)S(1)}, bf16[2,16,2,32,256]{4,3,2,1,0:T(8,128)(2,1)S(1)}, u32[]{:S(2)}, u32[]{:S(2)}) collective-permute-start(bf16[2,16,2,32,256]{4,3,2,1,0:T(8,128)(2,1)S(1)} %get-tuple-element.70), channel_id=1, source_target_pairs={{0,8},{8,0},{16,24},{24,16},{1,9},{9,1},{17,25},{25,17},{2,10},{10... | collective-permute-start | bytes 3145736 | tf_op jit(solution)/shard_map/ppermute | solution.py:201
  196.4 34.0 %collective-permute-start.27 = (bf16[2,16,2,32,256]{4,3,2,1,0:T(8,128)(2,1)S(1)}, bf16[2,16,2,32,256]{4,3,2,1,0:T(8,128)(2,1)S(1)}, u32[]{:S(2)}, u32[]{:S(2)}) collective-permute-start(bf16[2,16,2,32,256]{4,3,2,1,0:T(8,128)(2,1)S(1)} %get-tuple-element.71), channel_id=1, source_target_pairs={{0,16},{8,24},{16,0},{24,8},{1,17},{9,25},{17,1},{25,9},{2,18},{10... | collective-permute-start | bytes 3145736 | tf_op jit(solution)/shard_map/ppermute | solution.py:201
  208.6 23.7 %collective-permute-start.25 = (bf16[16,2,32,256]{3,2,1,0:T(8,128)(2,1)S(1)}, bf16[16,2,32,256]{3,2,1,0:T(8,128)(2,1)S(1)}, u32[]{:S(2)}, u32[]{:S(2)}) collective-permute-start(bf16[16,2,32,256]{3,2,1,0:T(8,128)(2,1)S(1)} %fusion.6), channel_id=1, source_target_pairs={{0,2},{3,1},{4,6},{7,5},{8,10},{11,9},{12,14},{15,13},{16,18},{19,... | collective-permute-start | bytes 1572872 | tf_op jit(solution)/shard_map/ppermute | solution.py:314
  210.6 35.6 %collective-permute-start.31 = (bf16[16,2,32,256]{3,2,1,0:T(8,128)(2,1)S(1)}, bf16[16,2,32,256]{3,2,1,0:T(8,128)(2,1)S(1)}, u32[]{:S(2)}, u32[]{:S(2)}) collective-permute-start(bf16[16,2,32,256]{3,2,1,0:T(8,128)(2,1)S(1)} %fusion.7), channel_id=1, source_target_pairs={{0,2},{3,1},{4,6},{7,5},{8,10},{11,9},{12,14},{15,13},{16,18},{19,... | collective-permute-start | bytes 1572872 | tf_op jit(solution)/shard_map/ppermute | solution.py:314
  232.7 12.1 %collective-permute-start.32 = (bf16[1,16,2,32,256]{4,3,2,1,0:T(8,128)(2,1)S(1)}, bf16[1,16,2,32,256]{4,3,2,1,0:T(8,128)(2,1)S(1)}, u32[]{:S(2)}, u32[]{:S(2)}) collective-permute-start(bf16[1,16,2,32,256]{4,3,2,1,0:T(8,128)(2,1)S(1)} %add_convert_fusion.4), channel_id=1, source_target_pairs={{0,8},{8,0},{16,24},{24,16},{1,9},{9,1},{17,25},{25,17},{2,10},{10... | collective-permute-start | bytes 1572872 | tf_op jit(solution)/shard_map/ppermute | solution.py:201
  234.6 11.8 %collective-permute-start.29 = (bf16[1,16,2,32,256]{4,3,2,1,0:T(8,128)(2,1)S(1)}, bf16[1,16,2,32,256]{4,3,2,1,0:T(8,128)(2,1)S(1)}, u32[]{:S(2)}, u32[]{:S(2)}) collective-permute-start(bf16[1,16,2,32,256]{4,3,2,1,0:T(8,128)(2,1)S(1)} %add_convert_fusion.7), channel_id=1, source_target_pairs={{0,16},{8,24},{16,0},{24,8},{1,17},{9,25},{17,1},{25,9},{2,18},{10... | collective-permute-start | bytes 1572872 | tf_op jit(solution)/shard_map/ppermute | solution.py:201

commit v6 on v5

--- a/solution.py
+++ b/solution.py
@@ -48,7 +48,9 @@
     steps = pl.num_programs(0)
     each, _, size, _ = weights[0].shape
 
-    @pl.when(step == 0)
+    works = ids[5, 0] != 0
+
+    @pl.when(works & (step == 0))
     def _():
         out_acc[...] = jnp.zeros_like(out_acc)
         back_acc[...] = jnp.zeros_like(back_acc)
@@ -90,7 +92,6 @@
                 out_acc[s, :, outs[s]] += out[:, s * size : (s + 1) * size]
                 back_acc[s, :, ins[s]] += back[:, s * size : (s + 1) * size]
 
-    works = ids[5, 0] != 0
     pl.when(works & theirs)(lambda: work_on(*weights[:2], 1))
     pl.when(works & jnp.logical_not(theirs))(lambda: work_on(*weights[2:], 0))
     if last:
@@ -115,7 +116,7 @@
         pl.when(works & theirs)(lambda: store(*sums[:2], True))
         pl.when(works & jnp.logical_not(theirs))(lambda: store(*sums[2:], False))
 
-    @pl.when(step == steps - 1)
+    @pl.when(works & (step == steps - 1))
     def _():
         for k, acc in enumerate((out_acc, back_acc)):
             near_out[k] = acc[0].astype(BF16)
@@ -140,7 +141,7 @@
     def weight(part):
         return pl.BlockSpec(
             (each, 2, size, size),
-            lambda i, ids: (jnp.clip(i - part * turns, 0, turns - 1), 0, 0, 0),
+            lambda i, ids: (jnp.clip(i - part * turns, 0, turns - 1) * ids[5, 0], 0, 0, 0),
         )
 
     def blocks(shape):
@@ -261,7 +262,7 @@
     works = (group % away % 2 == 0) != (group >= away)
     partner = (group + away) % groups
 
-    first, split = 21 * tok_rows // 32, 12 * tok_rows // 32
+    first, split = 21 * tok_rows // 32, 11 * tok_rows // 32
     lines = hid * 2 * size // shards
 
     def fetch(weight):

time: 248 us -> 249 us (level)
  waiting for transfers between devices: 120 us -> 130 us
  Pallas kernels: 37.8 us -> 27.8 us
    pallas_call x2, Pallas kernels: 37.8 us -> 27.8 us  [layer(): pl.pallas_call(functools.partial(layer_kernel, last, slots), out_shape=ou...]
    ppermute x1, waiting for transfers between devices: 12.4 us -> 18.7 us  [on_device(): far.append(lax.ppermute(later, 'tensor', into))]
    ppermute x24, waiting for transfers between devices: 42.2 us -> 36.4 us  [hop(): lax.ppermute(block, axis, [(i, i ^ bit) for i in range(lax.axis_size(axis...]
    ppermute x1, waiting for transfers between devices: 17.6 us -> 20.6 us  [on_device(): middle = lax.ppermute(middle, 'tensor', back)]
    ppermute x2, waiting for transfers between devices: 1.85 us -> 4.79 us  [on_device(): theirs = [lax.ppermute(part, 'tensor', back) for part in theirs]]
    ppermute x1, waiting for transfers between devices: 8.86 us -> 11.7 us  [on_device(): late = lax.ppermute(late, 'tensor', back)]
  transfers between devices with their start and end apart: 33 -> 33, of which waited for: 20 -> 18; matrix products, arithmetic and copies ran while one was open for 17% -> 17% of each run, Pallas kernels for 15% -> 11%
where the time goes in v6:
time: 249 us; the launch traced here: 248 us
  waiting for transfers between devices  130 us (52%)
  starting transfers between devices  42.9 us (17%)
  local copies, waits for them, and re-layouts  32.3 us (13%)
  Pallas kernels  27.8 us (11%)
  other arithmetic  14.1 us (6%)
    ppermute x24, waiting for transfers between devices, hop(): lax.ppermute(block, axis, [(i, i ^ bit) for i in range(lax.axis_size(axis...  36.4 us
    pallas_call x2, Pallas kernels, layer(): pl.pallas_call(functools.partial(layer_kernel, last, slots), out_shape=ou...  27.8 us
    ppermute x1, waiting for transfers between devices, on_device(): middle = lax.ppermute(middle, 'tensor', back)  20.6 us
    ppermute x24, starting transfers between devices, hop(): lax.ppermute(block, axis, [(i, i ^ bit) for i in range(lax.axis_size(axis...  20.6 us
    ppermute x1, waiting for transfers between devices, on_device(): far.append(lax.ppermute(later, 'tensor', into))  18.7 us
    ppermute x1, waiting for transfers between devices, on_device(): early = lax.ppermute(early, 'tensor', back)  17.3 us
    dynamic_update_slice x16, local copies, waits for them, and re-layouts, gather(): table = lax.dynamic_update_slice_in_dim(table, part[None], place ^ me, 0)  15.5 us
    ppermute x1, waiting for transfers between devices, on_device(): far = [lax.ppermute(near[0], 'tensor', into)]  15.1 us
  transfers between devices with their start and end apart: 33, of which 18 were waited for; matrix products, arithmetic and copies ran while one was open for 17% of the time, Pallas kernels for 11%

profile of v6, /device:TPU:8, one launch (start us, length us, event | category | flops | bytes accessed | tf_op | source)
XLA Modules:
  0.0 247.9 jit_solution(9282476717258722606)
XLA Ops:
  0.6 1.9 constant_dynamic-slice_fusion.1
  2.5 5.3 %collective-permute-start.1 = (bf16[1024,256]{1,0:T(8,128)(2,1)}, bf16[1024,256]{1,0:T(8,128)(2,1)}, u32[]{:S(2)}, u32[]{:S(2)}) collective-permute-start(bf16[1024,256]{1,0:T(8,128)(2,1)} %constant_dynamic-slice_fusion.1), channel_id=1, source_target_pairs={{2,0},{1,3},{6,4},{5,7},{10,8},{9,11},{14,12},{13,15},{18,16},{17,... | collective-permute-start | bytes 1572872 | tf_op jit(solution)/shard_map/ppermute | solution.py:270
  7.8 1.9 constant_dynamic-slice_fusion
  9.7 2.1 collective-permute-start.9
  11.8 1.9 slice_bitcast_fusion.2
  14.0 2.9 %collective-permute-start = (bf16[2,336,2048]{2,1,0:T(8,128)(2,1)S(1)}, bf16[2,336,2048]{2,1,0:T(8,128)(2,1)}, u32[]{:S(2)}, u32[]{:S(2)}) collective-permute-start(bf16[2,336,2048]{2,1,0:T(8,128)(2,1)S(1)} %pad_maximum_fusion.refs_0_), channel_id=1, source_target_pairs={{2,0},{1,3},{6,4},{5,7},{10,8},{9,11},{14,12},{13,15},{18,16},{17,... | collective-permute-start | bytes 8257544 | tf_op jit(solution)/shard_map/ppermute | solution.py:277
  16.9 2.3 slice_bitcast_fusion.18
  19.7 2.3 pad_maximum_fusion.1.refs_1_
  22.0 1.5 collective-permute-start.2
  24.2 1.5 collective-permute-start.3
  25.7 5.2 %collective-permute-done.9 = bf16[1024,256]{1,0:T(8,128)(2,1)} collective-permute-done((bf16[1024,256]{1,0:T(8,128)(2,1)}, bf16[1024,256]{1,0:T(8,128)(2,1)}, u32[]{:S(2)}, u32[]{:S(2)}) %collective-permute-start.9) | collective-permute-done | bytes 524320 | tf_op jit(solution)/shard_map/ppermute | solution.py:270
  30.9 1.5 collective-permute-start.10
  32.4 2.3 broadcast.9.clone
  34.7 1.9 bitcast_dynamic-update-slice_fusion.15
  36.5 2.2 broadcast.9.clone.1
  38.8 1.9 bitcast_dynamic-update-slice_fusion.7
  40.6 1.5 collective-permute-start.11
  43.1 6.9 %collective-permute-done.10 = bf16[1024,256]{1,0:T(8,128)(2,1)S(1)} collective-permute-done((bf16[1024,256]{1,0:T(8,128)(2,1)}, bf16[1024,256]{1,0:T(8,128)(2,1)S(1)}, u32[]{:S(2)}, u32[]{:S(2)}) %collective-permute-start.10) | collective-permute-done | bytes 524320 | tf_op jit(solution)/shard_map/ppermute | solution.py:202
  50.0 1.5 collective-permute-start.4
  53.7 5.1 %collective-permute-start.17 = (bf16[2,176,2048]{2,1,0:T(8,128)(2,1)}, bf16[2,176,2048]{2,1,0:T(8,128)(2,1)}, u32[]{:S(2)}, u32[]{:S(2)}) collective-permute-start(bf16[2,176,2048]{2,1,0:T(8,128)(2,1)} %pad_maximum_fusion.1.refs_1_), channel_id=1, source_target_pairs={{2,0},{1,3},{6,4},{5,7},{10,8},{9,11},{14,12},{13,15},{18,16},{17,... | collective-permute-start | bytes 4325384 | tf_op jit(solution)/shard_map/ppermute | solution.py:279
  59.6 3.9 %collective-permute-done.4 = bf16[1024,256]{1,0:T(8,128)(2,1)S(1)} collective-permute-done((bf16[1024,256]{1,0:T(8,128)(2,1)S(1)}, bf16[1024,256]{1,0:T(8,128)(2,1)S(1)}, u32[]{:S(2)}, u32[]{:S(2)}) %collective-permute-start.4) | collective-permute-done | bytes 524320 | tf_op jit(solution)/shard_map/ppermute | solution.py:202
  74.7 15.1 %collective-permute-done.refs_1_.refs_2_ = bf16[2,336,2048]{2,1,0:T(8,128)(2,1)} collective-permute-done((bf16[2,336,2048]{2,1,0:T(8,128)(2,1)S(1)}, bf16[2,336,2048]{2,1,0:T(8,128)(2,1)}, u32[]{:S(2)}, u32[]{:S(2)}) %collective-permute-start) | collective-permute-done | bytes 2752544 | tf_op jit(solution)/shard_map/ppermute | solution.py:277
  89.7 11.1 %shard_map.93 = (bf16[2,336,2048]{2,1,0:T(8,128)(2,1)}, bf16[2,176,2048]{2,1,0:T(8,128)(2,1)}, bf16[2,160,2048]{2,1,0:T(8,128)(2,1)}, bf16[32,336,256]{2,1,0:T(8,128)(2,1)}, bf16[32,336,256]{2,1,0:T(8,128)(2,1)}) custom-call(s32[6,32]{1,0:T(8,128)} %add_add_fusion.ids, bf16[2,336,2048]{2,1,0:T(8,128)(2,1)} %copy-done, ...), custom_call_target="tpu_custom_call" | custom-call | tf_op jit(solution)/shard_map/pallas_call | solution.py:182
  100.9 18.7 %collective-permute-done.17.refs_3_ = bf16[2,176,2048]{2,1,0:T(8,128)(2,1)} collective-permute-done((bf16[2,176,2048]{2,1,0:T(8,128)(2,1)}, bf16[2,176,2048]{2,1,0:T(8,128)(2,1)}, u32[]{:S(2)}, u32[]{:S(2)}) %collective-permute-start.17) | collective-permute-done | bytes 1441824 | tf_op jit(solution)/shard_map/ppermute | solution.py:279
  119.6 1.5 collective-permute-start.18
  121.1 16.7 %shard_map.94 = (bf16[2,176,2048]{2,1,0:T(8,128)(2,1)}, bf16[2,176,2048]{2,1,0:T(8,128)(2,1)}, bf16[2,4,16,2,32,256]{5,4,3,2,1,0:T(8,128)(2,1)}, bf16[2,4,16,2,3...) custom-call(s32[6,32]{1,0:T(8,128)} %add_add_fusion.ids, ...), custom_call_target="tpu_custom_call" | custom-call | tf_op jit(solution)/shard_map/pallas_call | solution.py:182
  137.8 17.3 %collective-permute-done.18 = bf16[2,176,2048]{2,1,0:T(8,128)(2,1)S(1)} collective-permute-done((bf16[2,176,2048]{2,1,0:T(8,128)(2,1)}, bf16[2,176,2048]{2,1,0:T(8,128)(2,1)S(1)}, u32[]{:S(2)}, u32[]{:S(2)}) %collective-permute-start.18) | collective-permute-done | bytes 1441824 | tf_op jit(solution)/shard_map/ppermute | solution.py:298
  157.0 2.2 slice_bitcast_fusion
  159.2 1.4 collective-permute-start.28
  163.7 1.6 collective-permute-start.22
  165.2 1.5 collective-permute-start.21
  167.2 1.3 collective-permute-done.19
  169.7 20.6 %collective-permute-done.23 = bf16[2,160,2048]{2,1,0:T(8,128)(2,1)S(1)} collective-permute-done((bf16[2,160,2048]{2,1,0:T(8,128)(2,1)S(1)}, bf16[2,160,2048]{2,1,0:T(8,128)(2,1)S(1)}, u32[]{:S(2)}, u32[]{:S(2)}) %collective-permute-start.23) | collective-permute-done | bytes 1310752 | tf_op jit(solution)/shard_map/ppermute | solution.py:300
  190.6 1.6 collective-permute-start.24
  192.6 1.6 collective-permute-start.30
  195.2 10.2 %collective-permute-done.24 = bf16[1,16,2,32,256]{4,3,2,1,0:T(8,128)(2,1)S(1)} collective-permute-done((bf16[1,16,2,32,256]{4,3,2,1,0:T(8,128)(2,1)S(1)}, bf16[1,16,2,32,256]{4,3,2,1,0:T(8,128)(2,1)S(1)}, u32[]{:S(2)}, u32[]{:S(2)}) %collective-permute-start.24) | collective-permute-done | bytes 524320 | tf_op jit(solution)/shard_map/ppermute | solution.py:202
  207.9 1.5 collective-permute-start.31
  209.4 11.7 %collective-permute-done.28 = bf16[2,176,2048]{2,1,0:T(8,128)(2,1)S(1)} collective-permute-done((bf16[2,176,2048]{2,1,0:T(8,128)(2,1)}, bf16[2,176,2048]{2,1,0:T(8,128)(2,1)S(1)}, u32[]{:S(2)}, u32[]{:S(2)}) %collective-permute-start.28) | collective-permute-done | bytes 1441824 | tf_op jit(solution)/shard_map/ppermute | solution.py:301
  221.1 4.7 %collective-permute-done.26 = bf16[2,16,2,32,256]{4,3,2,1,0:T(8,128)(2,1)S(1)} collective-permute-done((bf16[2,16,2,32,256]{4,3,2,1,0:T(8,128)(2,1)S(1)}, bf16[2,16,2,32,256]{4,3,2,1,0:T(8,128)(2,1)S(1)}, u32[]{:S(2)}, u32[]{:S(2)}) %collective-permute-start.26) | collective-permute-done | bytes 1048608 | tf_op jit(solution)/shard_map/ppermute | solution.py:202
  225.8 1.8 collective-permute-done.27
  227.6 4.8 %collective-permute-done.25 = bf16[16,2,32,256]{3,2,1,0:T(8,128)(2,1)S(1)} collective-permute-done((bf16[16,2,32,256]{3,2,1,0:T(8,128)(2,1)S(1)}, bf16[16,2,32,256]{3,2,1,0:T(8,128)(2,1)S(1)}, u32[]{:S(2)}, u32[]{:S(2)}) %collective-permute-start.25) | collective-permute-done | bytes 524320 | tf_op jit(solution)/shard_map/ppermute | solution.py:315
  232.8 1.6 collective-permute-start.32
  234.7 1.6 collective-permute-start.29
  236.3 1.9 maximum_select_fusion
  238.2 1.9 maximum_select_fusion.1
  240.1 4.8 %collective-permute-done.32 = bf16[1,16,2,32,256]{4,3,2,1,0:T(8,128)(2,1)S(1)} collective-permute-done((bf16[1,16,2,32,256]{4,3,2,1,0:T(8,128)(2,1)S(1)}, bf16[1,16,2,32,256]{4,3,2,1,0:T(8,128)(2,1)S(1)}, u32[]{:S(2)}, u32[]{:S(2)}) %collective-permute-start.32) | collective-permute-done | bytes 524320 | tf_op jit(solution)/shard_map/ppermute | solution.py:202
  244.9 1.4 fusion.4
  246.5 1.4 fusion.5
  (91 shorter events, 27.8 us)
Async XLA Ops:
  2.5 19.5 %collective-permute-start.1 = (bf16[1024,256]{1,0:T(8,128)(2,1)}, bf16[1024,256]{1,0:T(8,128)(2,1)}, u32[]{:S(2)}, u32[]{:S(2)}) collective-permute-start(bf16[1024,256]{1,0:T(8,128)(2,1)} %constant_dynamic-slice_fusion.1), channel_id=1, source_target_pairs={{2,0},{1,3},{6,4},{5,7},{10,8},{9,11},{14,12},{13,15},{18,16},{17,... | collective-permute-start | bytes 1572872 | tf_op jit(solution)/shard_map/ppermute | solution.py:270
  9.7 21.2 %collective-permute-start.9 = (bf16[1024,256]{1,0:T(8,128)(2,1)}, bf16[1024,256]{1,0:T(8,128)(2,1)}, u32[]{:S(2)}, u32[]{:S(2)}) collective-permute-start(bf16[1024,256]{1,0:T(8,128)(2,1)} %constant_dynamic-slice_fusion), channel_id=1, source_target_pairs={{2,0},{1,3},{6,4},{5,7},{10,8},{9,11},{14,12},{13,15},{18,16},{17,... | collective-permute-start | bytes 1572872 | tf_op jit(solution)/shard_map/ppermute | solution.py:270
  13.7 5.5 %copy-start.6 = (s32[2,8,8]{2,1,0:T(8,128)S(1)}, s32[2,8,8]{2,1,0:T(8,128)}, u32[]{:S(2)}) copy-start(s32[2,8,8]{2,1,0:T(8,128)} %param.8) | copy-start | bytes 1540
  13.7 5.6 %copy-start.7 = (s32[2,8,8]{2,1,0:T(8,128)S(1)}, s32[2,8,8]{2,1,0:T(8,128)}, u32[]{:S(2)}) copy-start(s32[2,8,8]{2,1,0:T(8,128)} %param.9) | copy-start | bytes 1540
  14.0 20.7 %copy-start = (bf16[2,336,2048]{2,1,0:T(8,128)(2,1)}, bf16[2,336,2048]{2,1,0:T(8,128)(2,1)S(1)}, u32[]{:S(2)}) copy-start(bf16[2,336,2048]{2,1,0:T(8,128)(2,1)S(1)} %pad_maximum_fusion.refs_0_) | copy-start | bytes 8257540
  14.0 75.7 %collective-permute-start = (bf16[2,336,2048]{2,1,0:T(8,128)(2,1)S(1)}, bf16[2,336,2048]{2,1,0:T(8,128)(2,1)}, u32[]{:S(2)}, u32[]{:S(2)}) collective-permute-start(bf16[2,336,2048]{2,1,0:T(8,128)(2,1)S(1)} %pad_maximum_fusion.refs_0_), channel_id=1, source_target_pairs={{2,0},{1,3},{6,4},{5,7},{10,8},{9,11},{14,12},{13,15},{18,16},{17,... | collective-permute-start | bytes 8257544 | tf_op jit(solution)/shard_map/ppermute | solution.py:277
  22.0 18.6 %collective-permute-start.2 = (bf16[1024,256]{1,0:T(8,128)(2,1)}, bf16[1024,256]{1,0:T(8,128)(2,1)S(1)}, u32[]{:S(2)}, u32[]{:S(2)}) collective-permute-start(bf16[1024,256]{1,0:T(8,128)(2,1)} %collective-permute-done.1), channel_id=1, source_target_pairs={{0,8},{8,0},{16,24},{24,16},{1,9},{9,1},{17,25},{25,17},{2,10},{10... | collective-permute-start | bytes 1572872 | tf_op jit(solution)/shard_map/ppermute | solution.py:202
  24.2 42.3 %collective-permute-start.5 = (bf16[1024,256]{1,0:T(8,128)(2,1)}, bf16[1024,256]{1,0:T(8,128)(2,1)S(1)}, u32[]{:S(2)}, u32[]{:S(2)}) collective-permute-start(bf16[1024,256]{1,0:T(8,128)(2,1)} %collective-permute-done.1), channel_id=1, source_target_pairs={{0,4},{4,0},{1,5},{5,1},{2,6},{6,2},{3,7},{7,3},{8,12},{12,8},{9,1... | collective-permute-start | bytes 1572872 | tf_op jit(solution)/shard_map/ppermute | solution.py:202
  24.2 28.1 %collective-permute-start.3 = (bf16[1024,256]{1,0:T(8,128)(2,1)}, bf16[1024,256]{1,0:T(8,128)(2,1)S(1)}, u32[]{:S(2)}, u32[]{:S(2)}) collective-permute-start(bf16[1024,256]{1,0:T(8,128)(2,1)} %collective-permute-done.1), channel_id=1, source_target_pairs={{0,16},{8,24},{16,0},{24,8},{1,17},{9,25},{17,1},{25,9},{2,18},{10... | collective-permute-start | bytes 1572872 | tf_op jit(solution)/shard_map/ppermute | solution.py:202
  30.9 19.1 %collective-permute-start.10 = (bf16[1024,256]{1,0:T(8,128)(2,1)}, bf16[1024,256]{1,0:T(8,128)(2,1)S(1)}, u32[]{:S(2)}, u32[]{:S(2)}) collective-permute-start(bf16[1024,256]{1,0:T(8,128)(2,1)} %collective-permute-done.9), channel_id=1, source_target_pairs={{0,16},{8,24},{16,0},{24,8},{1,17},{9,25},{17,1},{25,9},{2,18},{10... | collective-permute-start | bytes 1572872 | tf_op jit(solution)/shard_map/ppermute | solution.py:202
  40.6 13.0 %collective-permute-start.11 = (bf16[1024,256]{1,0:T(8,128)(2,1)}, bf16[1024,256]{1,0:T(8,128)(2,1)S(1)}, u32[]{:S(2)}, u32[]{:S(2)}) collective-permute-start(bf16[1024,256]{1,0:T(8,128)(2,1)} %collective-permute-done.9), channel_id=1, source_target_pairs={{0,8},{8,0},{16,24},{24,16},{1,9},{9,1},{17,25},{25,17},{2,10},{10... | collective-permute-start | bytes 1572872 | tf_op jit(solution)/shard_map/ppermute | solution.py:202
  50.0 13.6 %collective-permute-start.4 = (bf16[1024,256]{1,0:T(8,128)(2,1)S(1)}, bf16[1024,256]{1,0:T(8,128)(2,1)S(1)}, u32[]{:S(2)}, u32[]{:S(2)}) collective-permute-start(bf16[1024,256]{1,0:T(8,128)(2,1)S(1)} %collective-permute-done.2), channel_id=1, source_target_pairs={{0,16},{8,24},{16,0},{24,8},{1,17},{9,25},{17,1},{25,9},{2,18},{10... | collective-permute-start | bytes 1572872 | tf_op jit(solution)/shard_map/ppermute | solution.py:202
  52.3 13.3 %collective-permute-start.12 = (bf16[1024,256]{1,0:T(8,128)(2,1)S(1)}, bf16[1024,256]{1,0:T(8,128)(2,1)S(1)}, u32[]{:S(2)}, u32[]{:S(2)}) collective-permute-start(bf16[1024,256]{1,0:T(8,128)(2,1)S(1)} %collective-permute-done.10), channel_id=1, source_target_pairs={{0,8},{8,0},{16,24},{24,16},{1,9},{9,1},{17,25},{25,17},{2,10},{10... | collective-permute-start | bytes 1572872 | tf_op jit(solution)/shard_map/ppermute | solution.py:202
  53.7 65.9 %collective-permute-start.17 = (bf16[2,176,2048]{2,1,0:T(8,128)(2,1)}, bf16[2,176,2048]{2,1,0:T(8,128)(2,1)}, u32[]{:S(2)}, u32[]{:S(2)}) collective-permute-start(bf16[2,176,2048]{2,1,0:T(8,128)(2,1)} %pad_maximum_fusion.1.refs_1_), channel_id=1, source_target_pairs={{2,0},{1,3},{6,4},{5,7},{10,8},{9,11},{14,12},{13,15},{18,16},{17,... | collective-permute-start | bytes 4325384 | tf_op jit(solution)/shard_map/ppermute | solution.py:279
  63.5 4.3 %collective-permute-start.13 = (bf16[1024,256]{1,0:T(8,128)(2,1)}, bf16[1024,256]{1,0:T(8,128)(2,1)S(1)}, u32[]{:S(2)}, u32[]{:S(2)}) collective-permute-start(bf16[1024,256]{1,0:T(8,128)(2,1)} %collective-permute-done.9), channel_id=1, source_target_pairs={{0,4},{4,0},{1,5},{5,1},{2,6},{6,2},{3,7},{7,3},{8,12},{12,8},{9,1... | collective-permute-start | bytes 1572872 | tf_op jit(solution)/shard_map/ppermute | solution.py:202
  65.6 3.1 %collective-permute-start.6 = (bf16[1024,256]{1,0:T(8,128)(2,1)S(1)}, bf16[1024,256]{1,0:T(8,128)(2,1)S(1)}, u32[]{:S(2)}, u32[]{:S(2)}) collective-permute-start(bf16[1024,256]{1,0:T(8,128)(2,1)S(1)} %collective-permute-done.2), channel_id=1, source_target_pairs={{0,4},{4,0},{1,5},{5,1},{2,6},{6,2},{3,7},{7,3},{8,12},{12,8},{9,1... | collective-permute-start | bytes 1572872 | tf_op jit(solution)/shard_map/ppermute | solution.py:202
  66.4 3.5 %collective-permute-start.7 = (bf16[1024,256]{1,0:T(8,128)(2,1)S(1)}, bf16[1024,256]{1,0:T(8,128)(2,1)S(1)}, u32[]{:S(2)}, u32[]{:S(2)}) collective-permute-start(bf16[1024,256]{1,0:T(8,128)(2,1)S(1)} %collective-permute-done.3), channel_id=1, source_target_pairs={{0,4},{4,0},{1,5},{5,1},{2,6},{6,2},{3,7},{7,3},{8,12},{12,8},{9,1... | collective-permute-start | bytes 1572872 | tf_op jit(solution)/shard_map/ppermute | solution.py:202
  67.8 3.1 %collective-permute-start.14 = (bf16[1024,256]{1,0:T(8,128)(2,1)S(1)}, bf16[1024,256]{1,0:T(8,128)(2,1)S(1)}, u32[]{:S(2)}, u32[]{:S(2)}) collective-permute-start(bf16[1024,256]{1,0:T(8,128)(2,1)S(1)} %collective-permute-done.10), channel_id=1, source_target_pairs={{0,4},{4,0},{1,5},{5,1},{2,6},{6,2},{3,7},{7,3},{8,12},{12,8},{9,1... | collective-permute-start | bytes 1572872 | tf_op jit(solution)/shard_map/ppermute | solution.py:202
  68.6 3.5 %collective-permute-start.15 = (bf16[1024,256]{1,0:T(8,128)(2,1)S(1)}, bf16[1024,256]{1,0:T(8,128)(2,1)S(1)}, u32[]{:S(2)}, u32[]{:S(2)}) collective-permute-start(bf16[1024,256]{1,0:T(8,128)(2,1)S(1)} %collective-permute-done.11), channel_id=1, source_target_pairs={{0,4},{4,0},{1,5},{5,1},{2,6},{6,2},{3,7},{7,3},{8,12},{12,8},{9,1... | collective-permute-start | bytes 1572872 | tf_op jit(solution)/shard_map/ppermute | solution.py:202
  70.0 3.0 %collective-permute-start.8 = (bf16[1024,256]{1,0:T(8,128)(2,1)S(1)}, bf16[1024,256]{1,0:T(8,128)(2,1)S(1)}, u32[]{:S(2)}, u32[]{:S(2)}) collective-permute-start(bf16[1024,256]{1,0:T(8,128)(2,1)S(1)} %collective-permute-done.4), channel_id=1, source_target_pairs={{0,4},{4,0},{1,5},{5,1},{2,6},{6,2},{3,7},{7,3},{8,12},{12,8},{9,1... | collective-permute-start | bytes 1572872 | tf_op jit(solution)/shard_map/ppermute | solution.py:202
  70.9 3.0 %collective-permute-start.16 = (bf16[1024,256]{1,0:T(8,128)(2,1)S(1)}, bf16[1024,256]{1,0:T(8,128)(2,1)S(1)}, u32[]{:S(2)}, u32[]{:S(2)}) collective-permute-start(bf16[1024,256]{1,0:T(8,128)(2,1)S(1)} %collective-permute-done.12), channel_id=1, source_target_pairs={{0,4},{4,0},{1,5},{5,1},{2,6},{6,2},{3,7},{7,3},{8,12},{12,8},{9,1... | collective-permute-start | bytes 1572872 | tf_op jit(solution)/shard_map/ppermute | solution.py:202
  119.6 35.6 %collective-permute-start.18 = (bf16[2,176,2048]{2,1,0:T(8,128)(2,1)}, bf16[2,176,2048]{2,1,0:T(8,128)(2,1)S(1)}, u32[]{:S(2)}, u32[]{:S(2)}) collective-permute-start(bf16[2,176,2048]{2,1,0:T(8,128)(2,1)} %get-tuple-element.49), channel_id=1, source_target_pairs={{0,2},{3,1},{4,6},{7,5},{8,10},{11,9},{12,14},{15,13},{16,18},{19,... | collective-permute-start | bytes 4325384 | tf_op jit(solution)/shard_map/ppermute | solution.py:298
  121.1 34.6 %copy-start.8 = (bf16[2,160,2048]{2,1,0:T(8,128)(2,1)S(1)}, bf16[2,160,2048]{2,1,0:T(8,128)(2,1)}, u32[]{:S(2)}) copy-start(bf16[2,160,2048]{2,1,0:T(8,128)(2,1)} %get-tuple-element.65) | copy-start | bytes 3932164
  137.8 22.9 %copy-start.1 = (bf16[2,4,16,2,32,256]{5,4,3,2,1,0:T(8,128)(2,1)S(1)}, bf16[2,4,16,2,32,256]{5,4,3,2,1,0:T(8,128)(2,1)}, u32[]{:S(2)}) copy-start(bf16[2,4,16,2,32,256]{5,4,3,2,1,0:T(8,128)(2,1)} %get-tuple-element.61) | copy-start | bytes 12582916
  155.2 1.8 copy-start.3
  155.2 7.4 %collective-permute-start.20 = (bf16[2,4,16,2,32,256]{5,4,3,2,1,0:T(8,128)(2,1)}, bf16[2,4,16,2,32,256]{5,4,3,2,1,0:T(8,128)(2,1)S(1)}, u32[]{:S(2)}, u32[]{:S(2)}) collective-permute-start(bf16[2,4,16,2,32,256]{5,4,3,2,1,0:T(8,128)(2,1)} %get-tuple-element.64), channel_id=1, source_target_pairs={{0,4},{4,0},{1,5},{5,1},{2,6},{6,2},{3,7},{7,3},{8,12},{12,8},{9,1... | collective-permute-start | bytes 12582920 | tf_op jit(solution)/shard_map/ppermute | solution.py:202
  155.2 13.4 %collective-permute-start.19 = (bf16[2,4,16,2,32,256]{5,4,3,2,1,0:T(8,128)(2,1)}, bf16[2,4,16,2,32,256]{5,4,3,2,1,0:T(8,128)(2,1)S(1)}, u32[]{:S(2)}, u32[]{:S(2)}) collective-permute-start(bf16[2,4,16,2,32,256]{5,4,3,2,1,0:T(8,128)(2,1)} %get-tuple-element.62), channel_id=1, source_target_pairs={{0,4},{4,0},{1,5},{5,1},{2,6},{6,2},{3,7},{7,3},{8,12},{12,8},{9,1... | collective-permute-start | bytes 12582920 | tf_op jit(solution)/shard_map/ppermute | solution.py:202
  155.7 34.6 %collective-permute-start.23 = (bf16[2,160,2048]{2,1,0:T(8,128)(2,1)S(1)}, bf16[2,160,2048]{2,1,0:T(8,128)(2,1)S(1)}, u32[]{:S(2)}, u32[]{:S(2)}) collective-permute-start(bf16[2,160,2048]{2,1,0:T(8,128)(2,1)S(1)} %copy-done.8), channel_id=1, source_target_pairs={{0,2},{3,1},{4,6},{7,5},{8,10},{11,9},{12,14},{15,13},{16,18},{19,... | collective-permute-start | bytes 3932168 | tf_op jit(solution)/shard_map/ppermute | solution.py:300
  157.0 3.9 %copy-start.2 = (bf16[2,4,16,2,32,256]{5,4,3,2,1,0:T(8,128)(2,1)S(1)}, bf16[2,4,16,2,32,256]{5,4,3,2,1,0:T(8,128)(2,1)}, u32[]{:S(2)}) copy-start(bf16[2,4,16,2,32,256]{5,4,3,2,1,0:T(8,128)(2,1)} %get-tuple-element.63) | copy-start | bytes 12582916
  159.2 2.0 copy-start.5
  159.2 61.9 %collective-permute-start.28 = (bf16[2,176,2048]{2,1,0:T(8,128)(2,1)}, bf16[2,176,2048]{2,1,0:T(8,128)(2,1)S(1)}, u32[]{:S(2)}, u32[]{:S(2)}) collective-permute-start(bf16[2,176,2048]{2,1,0:T(8,128)(2,1)} %get-tuple-element.72), channel_id=1, source_target_pairs={{0,2},{3,1},{4,6},{7,5},{8,10},{11,9},{12,14},{15,13},{16,18},{19,... | collective-permute-start | bytes 4325384 | tf_op jit(solution)/shard_map/ppermute | solution.py:301
  161.3 5.5 %copy-start.4 = (bf16[2,176,2048]{2,1,0:T(8,128)(2,1)S(1)}, bf16[2,176,2048]{2,1,0:T(8,128)(2,1)}, u32[]{:S(2)}) copy-start(bf16[2,176,2048]{2,1,0:T(8,128)(2,1)} %copy-done.3) | copy-start | bytes 4325380
  163.7 26.6 %collective-permute-start.22 = (bf16[2,16,2,32,256]{4,3,2,1,0:T(8,128)(2,1)S(1)}, bf16[2,16,2,32,256]{4,3,2,1,0:T(8,128)(2,1)S(1)}, u32[]{:S(2)}, u32[]{:S(2)}) collective-permute-start(bf16[2,16,2,32,256]{4,3,2,1,0:T(8,128)(2,1)S(1)} %get-tuple-element.84), channel_id=1, source_target_pairs={{0,16},{8,24},{16,0},{24,8},{1,17},{9,25},{17,1},{25,9},{2,18},{10... | collective-permute-start | bytes 3145736 | tf_op jit(solution)/shard_map/ppermute | solution.py:202
  165.2 25.0 %collective-permute-start.21 = (bf16[2,16,2,32,256]{4,3,2,1,0:T(8,128)(2,1)S(1)}, bf16[2,16,2,32,256]{4,3,2,1,0:T(8,128)(2,1)S(1)}, u32[]{:S(2)}, u32[]{:S(2)}) collective-permute-start(bf16[2,16,2,32,256]{4,3,2,1,0:T(8,128)(2,1)S(1)} %get-tuple-element.85), channel_id=1, source_target_pairs={{0,8},{8,0},{16,24},{24,16},{1,9},{9,1},{17,25},{25,17},{2,10},{10... | collective-permute-start | bytes 3145736 | tf_op jit(solution)/shard_map/ppermute | solution.py:202
  190.6 14.9 %collective-permute-start.24 = (bf16[1,16,2,32,256]{4,3,2,1,0:T(8,128)(2,1)S(1)}, bf16[1,16,2,32,256]{4,3,2,1,0:T(8,128)(2,1)S(1)}, u32[]{:S(2)}, u32[]{:S(2)}) collective-permute-start(bf16[1,16,2,32,256]{4,3,2,1,0:T(8,128)(2,1)S(1)} %add_convert_fusion.9), channel_id=1, source_target_pairs={{0,8},{8,0},{16,24},{24,16},{1,9},{9,1},{17,25},{25,17},{2,10},{10... | collective-permute-start | bytes 1572872 | tf_op jit(solution)/shard_map/ppermute | solution.py:202
  192.6 14.9 %collective-permute-start.30 = (bf16[1,16,2,32,256]{4,3,2,1,0:T(8,128)(2,1)S(1)}, bf16[1,16,2,32,256]{4,3,2,1,0:T(8,128)(2,1)S(1)}, u32[]{:S(2)}, u32[]{:S(2)}) collective-permute-start(bf16[1,16,2,32,256]{4,3,2,1,0:T(8,128)(2,1)S(1)} %add_convert_fusion.6), channel_id=1, source_target_pairs={{0,16},{8,24},{16,0},{24,8},{1,17},{9,25},{17,1},{25,9},{2,18},{10... | collective-permute-start | bytes 1572872 | tf_op jit(solution)/shard_map/ppermute | solution.py:202
  194.2 31.6 %collective-permute-start.26 = (bf16[2,16,2,32,256]{4,3,2,1,0:T(8,128)(2,1)S(1)}, bf16[2,16,2,32,256]{4,3,2,1,0:T(8,128)(2,1)S(1)}, u32[]{:S(2)}, u32[]{:S(2)}) collective-permute-start(bf16[2,16,2,32,256]{4,3,2,1,0:T(8,128)(2,1)S(1)} %get-tuple-element.70), channel_id=1, source_target_pairs={{0,8},{8,0},{16,24},{24,16},{1,9},{9,1},{17,25},{25,17},{2,10},{10... | collective-permute-start | bytes 3145736 | tf_op jit(solution)/shard_map/ppermute | solution.py:202
  194.7 32.9 %collective-permute-start.27 = (bf16[2,16,2,32,256]{4,3,2,1,0:T(8,128)(2,1)S(1)}, bf16[2,16,2,32,256]{4,3,2,1,0:T(8,128)(2,1)S(1)}, u32[]{:S(2)}, u32[]{:S(2)}) collective-permute-start(bf16[2,16,2,32,256]{4,3,2,1,0:T(8,128)(2,1)S(1)} %get-tuple-element.71), channel_id=1, source_target_pairs={{0,16},{8,24},{16,0},{24,8},{1,17},{9,25},{17,1},{25,9},{2,18},{10... | collective-permute-start | bytes 3145736 | tf_op jit(solution)/shard_map/ppermute | solution.py:202
  205.9 26.5 %collective-permute-start.25 = (bf16[16,2,32,256]{3,2,1,0:T(8,128)(2,1)S(1)}, bf16[16,2,32,256]{3,2,1,0:T(8,128)(2,1)S(1)}, u32[]{:S(2)}, u32[]{:S(2)}) collective-permute-start(bf16[16,2,32,256]{3,2,1,0:T(8,128)(2,1)S(1)} %fusion.6), channel_id=1, source_target_pairs={{0,2},{3,1},{4,6},{7,5},{8,10},{11,9},{12,14},{15,13},{16,18},{19,... | collective-permute-start | bytes 1572872 | tf_op jit(solution)/shard_map/ppermute | solution.py:315
  207.9 38.5 %collective-permute-start.31 = (bf16[16,2,32,256]{3,2,1,0:T(8,128)(2,1)S(1)}, bf16[16,2,32,256]{3,2,1,0:T(8,128)(2,1)S(1)}, u32[]{:S(2)}, u32[]{:S(2)}) collective-permute-start(bf16[16,2,32,256]{3,2,1,0:T(8,128)(2,1)S(1)} %fusion.7), channel_id=1, source_target_pairs={{0,2},{3,1},{4,6},{7,5},{8,10},{11,9},{12,14},{15,13},{16,18},{19,... | collective-permute-start | bytes 1572872 | tf_op jit(solution)/shard_map/ppermute | solution.py:315
  232.8 12.1 %collective-permute-start.32 = (bf16[1,16,2,32,256]{4,3,2,1,0:T(8,128)(2,1)S(1)}, bf16[1,16,2,32,256]{4,3,2,1,0:T(8,128)(2,1)S(1)}, u32[]{:S(2)}, u32[]{:S(2)}) collective-permute-start(bf16[1,16,2,32,256]{4,3,2,1,0:T(8,128)(2,1)S(1)} %add_convert_fusion.4), channel_id=1, source_target_pairs={{0,8},{8,0},{16,24},{24,16},{1,9},{9,1},{17,25},{25,17},{2,10},{10... | collective-permute-start | bytes 1572872 | tf_op jit(solution)/shard_map/ppermute | solution.py:202
  234.7 11.8 %collective-permute-start.29 = (bf16[1,16,2,32,256]{4,3,2,1,0:T(8,128)(2,1)S(1)}, bf16[1,16,2,32,256]{4,3,2,1,0:T(8,128)(2,1)S(1)}, u32[]{:S(2)}, u32[]{:S(2)}) collective-permute-start(bf16[1,16,2,32,256]{4,3,2,1,0:T(8,128)(2,1)S(1)} %add_convert_fusion.7), channel_id=1, source_target_pairs={{0,16},{8,24},{16,0},{24,8},{1,17},{9,25},{17,1},{25,9},{2,18},{10... | collective-permute-start | bytes 1572872 | tf_op jit(solution)/shard_map/ppermute | solution.py:202
